TPU v7x, 512 devices: a whole 4x4x16 slice. The times are simulated.
512 devices in a mesh: lat: 32 (over z_lo, x), lon: 16 (over y, z_hi, core).
Axes of the slice: x: 4, y: 4, z: 16 (z_hi: 2, z_lo: 8; z = z_hi * 8 + z_lo), core: 2. Of those that a mesh axis runs over, the one named last changes fastest.
Arguments:
- ocean_state: float32 [8, 48, 256, 2048], P(None, None, 'lat', 'lon'), may hold values from -6 to 6
- viscosity: float32 [47, 256, 2048], P(None, 'lat', 'lon'), may hold values from 0.02 to 20
- diffusivity: float32 [47, 256, 2048], P(None, 'lat', 'lon'), may hold values from 0.01 to 10
- wet_levels: int32 [256, 2048], P('lat', 'lon'), may hold values from 0 to 48
- storage: float32 [256, 2048], P('lat', 'lon'), may hold values from 0.2 to 2
- surface_old: float32 [256, 2048], P('lat', 'lon'), may hold values from -9 to 9
Outputs:
- mixed_state: float32 [8, 48, 256, 2048], P(None, None, 'lat', 'lon')
- surface: float32 [256, 2048], P('lat', 'lon')
All inputs are finite; a program needn't handle non-finite values.
Results may differ from a plain program's by a relative error of at most 0.0003.
Values sent between devices are 32-bit elements; how exact they have to be, the bound alone decides.
No kernel may reach another device: no remote copies, remote signals or barrier semaphores. Data moves between devices by JAX's collectives and lax.ppermute only.
A program may use at most 128 MiB of HBM per device.

v0:
```python
import jax
import jax.numpy as jnp
from jax import lax
from jax.sharding import PartitionSpec as P

ITERS = 3


HORIZONTAL_RATE = 0.2
FLUX_SCALE = 0.02
FACE_SCALE = 0.25


def with_halo(block, sides, width, periodic):
    for axis, dim in sides:
        count = lax.axis_size(axis)
        forward = [(i, i + 1) for i in range(count - 1)]
        if periodic:
            forward.append((count - 1, 0))
        backward = [(target, source) for source, target in forward]
        low = lax.ppermute(
            lax.slice_in_dim(block, block.shape[dim] - width, None, axis=dim), axis, forward
        )
        high = lax.ppermute(lax.slice_in_dim(block, 0, width, axis=dim), axis, backward)
        block = jnp.concatenate([low, block, high], axis=dim)
    return block


def partner(value, axis, bit):
    mask = 2**bit
    pairs = [(source, source ^ mask) for source in range(lax.axis_size(axis))]
    return lax.ppermute(value, axis, pairs)


def shifted(value, axis, steps):
    count = lax.axis_size(axis)
    pairs = [(source, (source + steps) % count) for source in range(count)]
    return lax.ppermute(value, axis, pairs)


def passed_along(block, axis, distance):
    devices = range(lax.axis_size(axis))
    route = [(i - distance, i) for i in devices if i - distance in devices]
    return lax.ppermute(block, axis, route)


def thickness_of(levels):
    return 0.5 + jnp.arange(levels, dtype=jnp.float32) / levels


def top_rows(row_count):
    at_top = lax.axis_index("lat") == lax.axis_size("lat") - 1
    last_row = jnp.arange(row_count)[:, None] == row_count - 1
    return jnp.logical_and(last_row, at_top)


def surface_rims(values):
    zonal_rim = with_halo(values, (("lon", 1),), 1, True)
    meridional_rim = with_halo(values, (("lat", 0),), 1, False)
    folded = values[-1:, ::-1]
    for fold_bit in range(lax.axis_size("lon").bit_length() - 1):
        folded = partner(folded, "lon", fold_bit)
    north_side = jnp.where(top_rows(values.shape[0]), folded, meridional_rim[2:])
    return (zonal_rim[:, 2:], zonal_rim[:, :-2], north_side, meridional_rim[:-2])


def field_rims(values, field_signs):
    field_count, level_total, row_count, col_count = values.shape
    zonal_rim = with_halo(values, (("lon", 3),), 1, True)
    meridional_rim = with_halo(values, (("lat", 2),), 1, False)
    reversed_row = values[:, :, -1, ::-1].reshape(field_count * level_total, 1, col_count)
    spread = lax.all_to_all(reversed_row, "lon", split_axis=0, concat_axis=1, tiled=True)
    returned = lax.all_to_all(spread[:, ::-1, :], "lon", split_axis=1, concat_axis=0, tiled=True)
    folded = returned.reshape(field_count, level_total, 1, col_count) * field_signs
    north_side = jnp.where(top_rows(row_count), folded, meridional_rim[:, :, 2:])
    return (zonal_rim[..., 2:], zonal_rim[..., :-2], north_side, meridional_rim[:, :, :-2])


def face_counts(level_count, neighbour_set):
    return tuple((jnp.minimum(level_count, neighbour) for neighbour in neighbour_set))


def column_depth(level_count, thickness):
    level_axis = jnp.arange(thickness.shape[0], dtype=jnp.float32)[:, None, None]
    return jnp.sum(jnp.where(level_axis < level_count[None], thickness[:, None, None], 0.0), axis=0)


def depth_sum(component, level_count, thickness):
    level_axis = jnp.arange(thickness.shape[0], dtype=jnp.float32)[:, None, None]
    return jnp.sum(
        jnp.where(level_axis < level_count[None], thickness[:, None, None] * component, 0.0), axis=0
    )


def horizontal(fields, counts, neighbour_set):
    level_axis = jnp.arange(fields.shape[-3], dtype=jnp.float32)[:, None, None]
    change = jnp.zeros_like(fields)
    for face_count, neighbour in zip(counts, neighbour_set):
        change = change + jnp.where(level_axis < face_count[None], neighbour - fields, 0.0)
    return fields + HORIZONTAL_RATE * change


def couplings(coefficient, level_count, thickness):
    spacing = 2.0 / (thickness[:-1] + thickness[1:])
    interface = jnp.arange(thickness.shape[0] - 1, dtype=jnp.float32)[:, None, None]
    return jnp.where(interface + 1.0 < level_count[None], coefficient * spacing[:, None, None], 0.0)


def vertical(fields, couple, thickness):
    levels = fields.shape[1]
    zero_plane = jnp.zeros_like(couple[0])
    gain_list = []
    eliminated = []
    prev_gain = zero_plane
    prev_value = jnp.zeros_like(fields[:, 0])
    for depth_index in range(levels):
        coupling_above = couple[depth_index - 1] if depth_index > 0 else zero_plane
        coupling_below = couple[depth_index] if depth_index < levels - 1 else zero_plane
        inverse = 1.0 / (
            thickness[depth_index] + coupling_above + coupling_below - coupling_above * prev_gain
        )
        prev_gain = coupling_below * inverse
        prev_value = (
            thickness[depth_index] * fields[:, depth_index] + coupling_above * prev_value
        ) * inverse
        gain_list.append(prev_gain)
        eliminated.append(prev_value)
    result = [None] * levels
    lower_value = eliminated[-1]
    result[-1] = lower_value
    for depth_index in range(levels - 2, -1, -1):
        lower_value = eliminated[depth_index] + gain_list[depth_index] * lower_value
        result[depth_index] = lower_value
    return jnp.stack(result, axis=1)


def residual_product(residual, scaled):
    return lax.psum(jnp.sum(residual * scaled), ("lat", "lon"))


def local(ocean_state, viscosity, diffusivity, wet_levels, storage, surface_old):
    thickness = thickness_of(ocean_state.shape[1])
    row_count = wet_levels.shape[0]
    level_count = wet_levels.astype(jnp.float32)
    counts = face_counts(level_count, surface_rims(level_count))
    field_signs = jnp.array([-1.0, -1.0, 1.0, 1.0, 1.0, 1.0, 1.0, 1.0], dtype=jnp.float32)[
        :, None, None, None
    ]
    blended = horizontal(ocean_state, counts, field_rims(ocean_state, field_signs))
    momentum = vertical(blended[:2], couplings(viscosity, level_count, thickness), thickness)
    zonal_flux = depth_sum(momentum[0], counts[0], thickness)
    meridional_flux = jnp.where(
        top_rows(row_count), 0.0, depth_sum(momentum[1], counts[2], thickness)
    )
    west_flux = shifted(zonal_flux[:, -1:], "lon", 1)
    south_flux = passed_along(meridional_flux[-1:, :], "lat", 1)
    divergence = (
        zonal_flux
        - jnp.concatenate([west_flux, zonal_flux[:, :-1]], axis=1)
        + meridional_flux
        - jnp.concatenate([south_flux, meridional_flux[:-1]], axis=0)
    )
    scalars = vertical(blended[2:], couplings(diffusivity, level_count, thickness), thickness)
    ocean_mask = wet_levels > 0
    forcing = jnp.where(ocean_mask, storage * surface_old - FLUX_SCALE * divergence, 0.0)
    face_terms = tuple((FACE_SCALE * column_depth(face_count, thickness) for face_count in counts))
    diagonal = storage + face_terms[0] + face_terms[1] + face_terms[2] + face_terms[3]

    def operate(values):
        result = storage * values
        for face_term, neighbour in zip(face_terms, surface_rims(values)):
            result = result + face_term * (values - neighbour)
        return result

    surface = jnp.where(ocean_mask, surface_old, 0.0)
    residual = forcing - operate(surface)
    scaled = residual / diagonal
    direction = scaled
    product = residual_product(residual, scaled)
    for iteration in range(ITERS):
        image_field = operate(direction)
        step_size = product / lax.psum(jnp.sum(direction * image_field), ("lat", "lon"))
        surface = surface + step_size * direction
        residual = residual - step_size * image_field
        if iteration + 1 < ITERS:
            scaled = residual / diagonal
            next_product = residual_product(residual, scaled)
            direction = scaled + next_product / product * direction
            product = next_product
    return (jnp.concatenate([momentum, scalars], axis=0), surface)


def solution(mesh):
    placed = (
        P(None, None, "lat", "lon"),
        P(None, "lat", "lon"),
        P(None, "lat", "lon"),
        P("lat", "lon"),
        P("lat", "lon"),
        P("lat", "lon"),
    )
    return jax.shard_map(
        local,
        mesh=mesh,
        in_specs=placed,
        out_specs=(P(None, None, "lat", "lon"), P("lat", "lon")),
        check_vma=False,
    )
```

profile of v0, /device:TPU:1, one launch (start us, length us, event | category | flops | bytes accessed | tf_op | source)
XLA Modules:
  0.0 1179.7 jit_solution(5480302512754705781)
XLA Ops:
  3.1 19.2 %all-to-all-start = ((f32[384,1,128]{2,1,0:T(1,128)}), f32[384,1,128]{2,1,0:T(1,128)S(1)}, u32[]{:S(2)}, u32[]{:S(2)}) async-start(f32[384,1,128]{2,1,0:T(1,128)} %bitcast.3), calls=%async_computation | async-start | bytes 393216 | tf_op jit(solution)/shard_map/all_to_all | solution.py:72
  32.1 15.0 %collective-permute-start.4 = (f32[1,128]{1,0:T(1,128)S(1)}, f32[1,128]{1,0:T(1,128)S(1)}, u32[]{:S(2)}, u32[]{:S(2)}) collective-permute-start(f32[1,128]{1,0:T(1,128)S(1)} %rev.21), channel_id=1, source_target_pairs={{0,1},{1,0},{2,3},{3,2},{4,5},{5,4},{6,7},{7,6},{8,9},{9,8},{10,11... | collective-permute-start | bytes 1544 | tf_op jit(solution)/shard_map/ppermute | solution.py:32
  87.7 29.0 %subtract_divide_fusion.5 = (f32[8,128]{1,0:T(8,128)}, f32[8,128]{1,0:T(8,128)S(1)}, f32[8,128]{1,0:T(8,128)}, f32[8,128]{1,0:T(8,128)S(1)}, f32[8,128]{1,0:T(8,...) fusion(f32[]{:T(128)} %bitcast.157, ...), kind=kLoop, calls=%fused_computation.951 | loop fusion | flops 260096 | bytes 225452 | tf_op jit(solution)/shard_map/div | solution.py:119
  116.8 27.9 %subtract_divide_fusion.51 = (f32[8,128]{1,0:T(8,128)}, f32[8,128]{1,0:T(8,128)S(1)}, f32[8,128]{1,0:T(8,128)}, f32[8,128]{1,0:T(8,128)S(1)}, f32[8,128]{1,0:T(8...) fusion(f32[]{:T(128)} %bitcast.157, ...), kind=kLoop, calls=%fused_computation.1001 | loop fusion | flops 260096 | bytes 225452 | tf_op jit(solution)/shard_map/div | solution.py:119
  219.5 10.5 collective-permute-done.5
  243.1 12.0 %collective-permute-start.17 = (f32[1,128]{1,0:T(1,128)}, f32[1,128]{1,0:T(1,128)S(1)}, u32[]{:S(2)}, u32[]{:S(2)}) collective-permute-start(f32[1,128]{1,0:T(1,128)} %collective-permute-done.16), channel_id=1, source_target_pairs={{0,2},{1,3},{2,0},{3,1},{4,6},{5,7},{6,4},{7,5},{8,10},{9,11},{10,... | collective-permute-start | bytes 1544 | tf_op jit(solution)/shard_map/ppermute | solution.py:32
  270.1 13.4 %collective-permute-start.3 = (f32[8,48,8,1]{1,2,3,0:T(8,128)}, f32[8,48,8,1]{1,2,3,0:T(8,128)S(1)}, u32[]{:S(2)}, u32[]{:S(2)}) collective-permute-start(f32[8,48,8,1]{1,2,3,0:T(8,128)} %copy.203), channel_id=1, source_target_pairs={{0,1},{1,2},{2,3},{3,4},{4,5},{5,6},{6,7},{7,8},{8,9},{9,10},{10,1... | collective-permute-start | bytes 36872 | tf_op jit(solution)/shard_map/ppermute | solution.py:21
  301.4 8.6 collective-permute-start.15
  319.9 31.8 %constant_dynamic-update-slice_fusion.95 = (f32[6,48,8,128]{3,2,1,0:T(8,128)S(1)}, f32[6,1,8,128]{3,2,0,1:T(8,128)S(1)}, f32[6,1,8,128]{3,2,0,1:T(8,128)S(1)}, f...) fusion(f32[8,48,8,128]{3,2,0,1:T(8,128)S(1)} %fusion.4, ...), kind=kLoop, calls=%fused_computation.116 | loop fusion | flops 1744895 | bytes 2818240
  358.9 27.1 %add_multiply_fusion.42 = (f32[2,1,8,128]{3,2,0,1:T(8,128)S(1)}, f32[2,1,8,128]{3,2,0,1:T(8,128)S(1)}, f32[2,1,8,128]{3,2,0,1:T(8,128)S(1)}, f32[2,1,8,128]{3,2,...) fusion(f32[8,48,8,128]{3,2,0,1:T(8,128)S(1)} %fusion.4, ...), kind=kLoop, calls=%fused_computation.618 | loop fusion | flops 331776 | bytes 995492 | tf_op jit(solution)/shard_map/mul | solution.py:123
  386.3 29.5 %fusion.141 = (f32[2,8,128]{2,1,0:T(8,128)S(1)}, f32[2,8,128]{2,1,0:T(8,128)S(1)}) fusion(f32[8,48,8,128]{3,2,0,1:T(8,128)S(1)} %fusion.4, f32[8,128]{1,0:T(8,128)S(1)} %copy-done.149, f32[8,128]{1,0:T(8,128)} %get-tuple-element.313, f32[]{:T(128)} %bitcast.161, f32[8,128]{1,0:T(8,128)S(1)} %copy-done.148, f32[8,128]{1,0:T(8,128)S(1)} %copy-done.144, ...), kind=kLoop, calls=%fused_computation.453 | loop fusion | flops 364544 | bytes 749748 | tf_op jit(solution)/shard_map/mul | solution.py:123
  435.7 9.5 collective-permute-done.14
  452.6 15.1 %collective-permute-start.24 = (f32[1,128]{1,0:T(1,128)S(1)}, f32[1,128]{1,0:T(1,128)S(1)}, u32[]{:S(2)}, u32[]{:S(2)}) collective-permute-start(f32[1,128]{1,0:T(1,128)S(1)} %rev.25), channel_id=1, source_target_pairs={{0,1},{1,0},{2,3},{3,2},{4,5},{5,4},{6,7},{7,6},{8,9},{9,8},{10,11... | collective-permute-start | bytes 1544 | tf_op jit(solution)/shard_map/ppermute | solution.py:32
  471.1 10.4 collective-permute-done.25
  498.8 11.5 collective-permute-done.22
  511.6 113.7 %all-reduce = (f32[]{:T(128)}, f32[]{:T(128)}) all-reduce(f32[]{:T(128)} %get-tuple-element.7, f32[]{:T(128)} %get-tuple-element.6), channel_id=1, replica_groups=mesh['lat'=32,'lon'=16] {'lat','lon'}, use_global_device_ids=true, to_apply=%region_7.8 | all-reduce | flops 2 | bytes 16 | tf_op jit(solution)/shard_map/psum | solution.py:138
  627.3 99.7 %psum.44 = f32[]{:T(128)} all-reduce(f32[]{:T(128)} %get-tuple-element.16), channel_id=1, replica_groups=mesh['lat'=32,'lon'=16] {'lat','lon'}, use_global_device_ids=true, to_apply=%region_11.12 | all-reduce | flops 1 | bytes 8 | tf_op jit(solution)/shard_map/psum | solution.py:138
  747.9 31.6 %constant_dynamic-update-slice_fusion.52 = (f32[6,48,8,128]{3,2,1,0:T(8,128)S(1)}, f32[6,8,128]{2,1,0:T(8,128)S(1)}, f32[6,8,128]{2,1,0:T(8,128)S(1)}, f32[6,8,128]{2,1,0:T(8,128)S(1)}) fusion(f32[6,48,8,128]{3,2,1,0:T(8,128)S(1)} %constant_dynamic-update-slice_fusion.53, f32[8,128]{1,0:T(8,128)} %copy-done.30, f32[8,128]{1,0:T(8,128)} %get-tuple-element.280, ...), kind=kLoop, calls=%fused_computation.73 | loop fusion | flops 1216512 | bytes 1683648
  796.1 11.7 collective-permute-done.30
  808.6 106.8 %psum.45 = f32[]{:T(128)} all-reduce(f32[]{:T(128)} %get-tuple-element.14), channel_id=1, replica_groups=mesh['lat'=32,'lon'=16] {'lat','lon'}, use_global_device_ids=true, to_apply=%region_13.14 | all-reduce | flops 1 | bytes 8 | tf_op jit(solution)/shard_map/psum | solution.py:182
  917.3 101.5 %psum.46 = f32[]{:T(128)} all-reduce(f32[]{:T(128)} %multiply_reduce_fusion), channel_id=1, replica_groups=mesh['lat'=32,'lon'=16] {'lat','lon'}, use_global_device_ids=true, to_apply=%region_15.16 | all-reduce | flops 1 | bytes 8 | tf_op jit(solution)/shard_map/psum | solution.py:138
  1047.7 7.8 collective-permute-start.39
  1057.4 11.7 collective-permute-done.38
  1071.1 106.8 %psum.47 = f32[]{:T(128)} all-reduce(f32[]{:T(128)} %fusion.345), channel_id=1, replica_groups=mesh['lat'=32,'lon'=16] {'lat','lon'}, use_global_device_ids=true, to_apply=%region_17.18 | all-reduce | flops 1 | bytes 8 | tf_op jit(solution)/shard_map/psum | solution.py:182
  (682 shorter events, 306.9 us)
Async XLA Ops:
  3.1 228.9 %all-to-all-start = ((f32[384,1,128]{2,1,0:T(1,128)}), f32[384,1,128]{2,1,0:T(1,128)S(1)}, u32[]{:S(2)}, u32[]{:S(2)}) async-start(f32[384,1,128]{2,1,0:T(1,128)} %bitcast.3), calls=%async_computation | async-start | bytes 393216 | tf_op jit(solution)/shard_map/all_to_all | solution.py:72
  23.0 236.7 %collective-permute-start = (f32[8,1]{1,0:T(8,128)}, f32[8,1]{1,0:T(8,128)}, u32[]{:S(2)}, u32[]{:S(2)}) collective-permute-start(f32[8,1]{1,0:T(8,128)} %get-tuple-element.454), channel_id=1, source_target_pairs={{1,0},{2,1},{3,2},{4,3},{5,4},{6,5},{7,6},{8,7},{9,8},{10,9},{11,1... | collective-permute-start | bytes 104 | tf_op jit(solution)/shard_map/ppermute | solution.py:24
  25.6 240.7 %collective-permute-start.8 = (f32[1,128]{1,0:T(1,128)}, f32[1,128]{1,0:T(1,128)}, u32[]{:S(2)}, u32[]{:S(2)}) collective-permute-start(f32[1,128]{1,0:T(1,128)} %get-tuple-element.456), channel_id=1, source_target_pairs={{16,0},{32,16},{48,32},{64,48},{80,64},{96,80},{112,96},{128,112},... | collective-permute-start | bytes 1544 | tf_op jit(solution)/shard_map/ppermute | solution.py:24
  26.9 243.2 %collective-permute-start.10 = (f32[1,128]{1,0:T(1,128)}, f32[1,128]{1,0:T(1,128)}, u32[]{:S(2)}, u32[]{:S(2)}) collective-permute-start(f32[1,128]{1,0:T(1,128)} %get-tuple-element.457), channel_id=1, source_target_pairs={{0,16},{16,32},{32,48},{48,64},{64,80},{80,96},{96,112},{112,128},... | collective-permute-start | bytes 1544 | tf_op jit(solution)/shard_map/ppermute | solution.py:21
  32.1 184.9 %collective-permute-start.4 = (f32[1,128]{1,0:T(1,128)S(1)}, f32[1,128]{1,0:T(1,128)S(1)}, u32[]{:S(2)}, u32[]{:S(2)}) collective-permute-start(f32[1,128]{1,0:T(1,128)S(1)} %rev.21), channel_id=1, source_target_pairs={{0,1},{1,0},{2,3},{3,2},{4,5},{5,4},{6,7},{7,6},{8,9},{9,8},{10,11... | collective-permute-start | bytes 1544 | tf_op jit(solution)/shard_map/ppermute | solution.py:32
  48.8 194.3 %collective-permute-start.16 = (f32[1,128]{1,0:T(1,128)}, f32[1,128]{1,0:T(1,128)}, u32[]{:S(2)}, u32[]{:S(2)}) collective-permute-start(f32[1,128]{1,0:T(1,128)} %rev.24), channel_id=1, source_target_pairs={{0,1},{1,0},{2,3},{3,2},{4,5},{5,4},{6,7},{7,6},{8,9},{9,8},{10,11... | collective-permute-start | bytes 1544 | tf_op jit(solution)/shard_map/ppermute | solution.py:32
  230.1 25.1 %collective-permute-start.6 = (f32[1,128]{1,0:T(1,128)}, f32[1,128]{1,0:T(1,128)}, u32[]{:S(2)}, u32[]{:S(2)}) collective-permute-start(f32[1,128]{1,0:T(1,128)} %collective-permute-done.5), channel_id=1, source_target_pairs={{0,4},{1,5},{2,6},{3,7},{4,0},{5,1},{6,2},{7,3},{8,12},{9,13},{10,... | collective-permute-start | bytes 1544 | tf_op jit(solution)/shard_map/ppermute | solution.py:32
  232.7 81.4 %all-to-all-start.1 = ((f32[24,16,128]{2,0,1:T(8,128)}), f32[24,16,128]{2,0,1:T(8,128)S(1)}, u32[]{:S(2)}, u32[]{:S(2)}) async-start(f32[24,16,128]{2,0,1:T(8,128)} %rev.23), calls=%async_computation.1 | async-start | bytes 393216 | tf_op jit(solution)/shard_map/all_to_all | solution.py:73
  243.1 40.4 %collective-permute-start.17 = (f32[1,128]{1,0:T(1,128)}, f32[1,128]{1,0:T(1,128)S(1)}, u32[]{:S(2)}, u32[]{:S(2)}) collective-permute-start(f32[1,128]{1,0:T(1,128)} %collective-permute-done.16), channel_id=1, source_target_pairs={{0,2},{1,3},{2,0},{3,1},{4,6},{5,7},{6,4},{7,5},{8,10},{9,11},{10,... | collective-permute-start | bytes 1544 | tf_op jit(solution)/shard_map/ppermute | solution.py:32
  255.1 32.3 %collective-permute-start.7 = (f32[1,128]{1,0:T(1,128)}, f32[1,128]{1,0:T(1,128)S(1)}, u32[]{:S(2)}, u32[]{:S(2)}) collective-permute-start(f32[1,128]{1,0:T(1,128)} %collective-permute-done.6), channel_id=1, source_target_pairs={{0,8},{1,9},{2,10},{3,11},{4,12},{5,13},{6,14},{7,15},{8,0},{9,1},... | collective-permute-start | bytes 1544 | tf_op jit(solution)/shard_map/ppermute | solution.py:32
  263.7 46.3 %collective-permute-start.11 = (f32[8,48,1,128]{3,1,0,2:T(8,128)S(1)}, f32[8,48,1,128]{3,1,0,2:T(8,128)S(1)}, u32[]{:S(2)}, u32[]{:S(2)}) collective-permute-start(f32[8,48,1,128]{3,1,0,2:T(8,128)S(1)} %bitcast.1969), channel_id=1, source_target_pairs={{0,16},{16,32},{32,48},{48,64},{64,80},{80,96},{96,112},{112,128},... | collective-permute-start | bytes 589832 | tf_op jit(solution)/shard_map/ppermute | solution.py:21
  266.4 183.3 %collective-permute-start.21 = (f32[1,128]{1,0:T(1,128)}, f32[1,128]{1,0:T(1,128)}, u32[]{:S(2)}, u32[]{:S(2)}) collective-permute-start(f32[1,128]{1,0:T(1,128)} %copy-done.202), channel_id=1, source_target_pairs={{0,16},{16,32},{32,48},{48,64},{64,80},{80,96},{96,112},{112,128},... | collective-permute-start | bytes 1544 | tf_op jit(solution)/shard_map/ppermute | solution.py:21
  297.7 152.0 %collective-permute-start.20 = (f32[1,128]{1,0:T(1,128)}, f32[1,128]{1,0:T(1,128)}, u32[]{:S(2)}, u32[]{:S(2)}) collective-permute-start(f32[1,128]{1,0:T(1,128)} %get-tuple-element.448), channel_id=1, source_target_pairs={{16,0},{32,16},{48,32},{64,48},{80,64},{96,80},{112,96},{128,112},... | collective-permute-start | bytes 1544 | tf_op jit(solution)/shard_map/ppermute | solution.py:24
  301.4 130.2 %collective-permute-start.15 = (f32[8,1]{1,0:T(8,128)}, f32[8,1]{1,0:T(8,128)}, u32[]{:S(2)}, u32[]{:S(2)}) collective-permute-start(f32[8,1]{1,0:T(8,128)} %get-tuple-element.447), channel_id=1, source_target_pairs={{0,1},{1,2},{2,3},{3,4},{4,5},{5,6},{6,7},{7,8},{8,9},{9,10},{10,1... | collective-permute-start | bytes 104 | tf_op jit(solution)/shard_map/ppermute | solution.py:21
  310.0 139.7 %collective-permute-start.19 = (f32[1,128]{1,0:T(1,128)}, f32[1,128]{1,0:T(1,128)}, u32[]{:S(2)}, u32[]{:S(2)}) collective-permute-start(f32[1,128]{1,0:T(1,128)} %collective-permute-done.18), channel_id=1, source_target_pairs={{0,8},{1,9},{2,10},{3,11},{4,12},{5,13},{6,14},{7,15},{8,0},{9,1},... | collective-permute-start | bytes 1544 | tf_op jit(solution)/shard_map/ppermute | solution.py:32
  425.8 25.9 %collective-permute-start.13 = (f32[1,128]{1,0:T(1,128)S(1)}, f32[1,128]{1,0:T(1,128)S(1)}, u32[]{:S(2)}, u32[]{:S(2)}) collective-permute-start(f32[1,128]{1,0:T(1,128)S(1)} %slice.1514), channel_id=1, source_target_pairs={{0,16},{16,32},{32,48},{48,64},{64,80},{80,96},{96,112},{112,128},... | collective-permute-start | bytes 1544 | tf_op jit(solution)/shard_map/ppermute | solution.py:44
  483.4 26.8 %collective-permute-start.29 = (f32[1,128]{1,0:T(1,128)S(1)}, f32[1,128]{1,0:T(1,128)S(1)}, u32[]{:S(2)}, u32[]{:S(2)}) collective-permute-start(f32[1,128]{1,0:T(1,128)S(1)} %get-tuple-element.445), channel_id=1, source_target_pairs={{0,16},{16,32},{32,48},{48,64},{64,80},{80,96},{96,112},{112,128},... | collective-permute-start | bytes 1544 | tf_op jit(solution)/shard_map/ppermute | solution.py:21
  744.8 37.9 %collective-permute-start.34 = (f32[1,128]{1,0:T(1,128)S(1)}, f32[1,128]{1,0:T(1,128)S(1)}, u32[]{:S(2)}, u32[]{:S(2)}) collective-permute-start(f32[1,128]{1,0:T(1,128)S(1)} %collective-permute-done.33), channel_id=1, source_target_pairs={{0,4},{1,5},{2,6},{3,7},{4,0},{5,1},{6,2},{7,3},{8,12},{9,13},{10,... | collective-permute-start | bytes 1544 | tf_op jit(solution)/shard_map/ppermute | solution.py:32
  779.5 28.4 %collective-permute-start.37 = (f32[1,128]{1,0:T(1,128)S(1)}, f32[1,128]{1,0:T(1,128)S(1)}, u32[]{:S(2)}, u32[]{:S(2)}) collective-permute-start(f32[1,128]{1,0:T(1,128)S(1)} %get-tuple-element.441), channel_id=1, source_target_pairs={{0,16},{16,32},{32,48},{48,64},{64,80},{80,96},{96,112},{112,128},... | collective-permute-start | bytes 1544 | tf_op jit(solution)/shard_map/ppermute | solution.py:21
  781.4 26.4 %collective-permute-start.36 = (f32[1,128]{1,0:T(1,128)S(1)}, f32[1,128]{1,0:T(1,128)S(1)}, u32[]{:S(2)}, u32[]{:S(2)}) collective-permute-start(f32[1,128]{1,0:T(1,128)S(1)} %get-tuple-element.440), channel_id=1, source_target_pairs={{16,0},{32,16},{48,32},{64,48},{80,64},{96,80},{112,96},{128,112},... | collective-permute-start | bytes 1544 | tf_op jit(solution)/shard_map/ppermute | solution.py:24
  782.7 25.1 %collective-permute-start.35 = (f32[1,128]{1,0:T(1,128)S(1)}, f32[1,128]{1,0:T(1,128)S(1)}, u32[]{:S(2)}, u32[]{:S(2)}) collective-permute-start(f32[1,128]{1,0:T(1,128)S(1)} %collective-permute-done.34), channel_id=1, source_target_pairs={{0,8},{1,9},{2,10},{3,11},{4,12},{5,13},{6,14},{7,15},{8,0},{9,1},... | collective-permute-start | bytes 1544 | tf_op jit(solution)/shard_map/ppermute | solution.py:32
  1040.7 28.4 %collective-permute-start.45 = (f32[1,128]{1,0:T(1,128)S(1)}, f32[1,128]{1,0:T(1,128)S(1)}, u32[]{:S(2)}, u32[]{:S(2)}) collective-permute-start(f32[1,128]{1,0:T(1,128)S(1)} %get-tuple-element.437), channel_id=1, source_target_pairs={{0,16},{16,32},{32,48},{48,64},{64,80},{80,96},{96,112},{112,128},... | collective-permute-start | bytes 1544 | tf_op jit(solution)/shard_map/ppermute | solution.py:21
  1042.6 26.5 %collective-permute-start.44 = (f32[1,128]{1,0:T(1,128)S(1)}, f32[1,128]{1,0:T(1,128)S(1)}, u32[]{:S(2)}, u32[]{:S(2)}) collective-permute-start(f32[1,128]{1,0:T(1,128)S(1)} %get-tuple-element.436), channel_id=1, source_target_pairs={{16,0},{32,16},{48,32},{64,48},{80,64},{96,80},{112,96},{128,112},... | collective-permute-start | bytes 1544 | tf_op jit(solution)/shard_map/ppermute | solution.py:24
  1043.9 25.2 %collective-permute-start.43 = (f32[1,128]{1,0:T(1,128)S(1)}, f32[1,128]{1,0:T(1,128)S(1)}, u32[]{:S(2)}, u32[]{:S(2)}) collective-permute-start(f32[1,128]{1,0:T(1,128)S(1)} %collective-permute-done.42), channel_id=1, source_target_pairs={{0,8},{1,9},{2,10},{3,11},{4,12},{5,13},{6,14},{7,15},{8,0},{9,1},... | collective-permute-start | bytes 1544 | tf_op jit(solution)/shard_map/ppermute | solution.py:32
  (227 other events, 9474.3 us)
where the time goes:
time: 1190 us; the launch traced here: 1180 us
  blocking collectives  528 us (44%)
  other arithmetic  313 us (26%)
  starting transfers between devices  217 us (18%)
  waiting for transfers between devices  86.8 us (7%)
  local copies, waits for them, and re-layouts  23.8 us (2%)
    psum x3, blocking collectives, residual_product(): return lax.psum(jnp.sum(residual * scaled), ('lat', 'lon'))  315 us
    psum x2, blocking collectives, local(): lax.psum(jnp.sum(direction * image_field), ('lat', 'lon'))  214 us
    ppermute x20, starting transfers between devices, partner(): return lax.ppermute(value, axis, pairs)  96.2 us
    div x9, other arithmetic, vertical(): 1.0 / (thickness[depth_index] + coupling_above + coupling_below - couplin...  83.9 us
    unnamed x48, other arithmetic  79.2 us
    mul x32, other arithmetic, vertical(): lower_value = eliminated[depth_index] + gain_list[depth_index] * lower_value  68.1 us
    ppermute x12, starting transfers between devices, with_halo(): lax.ppermute(lax.slice_in_dim(block, block.shape[dim] - width, None, axis...  62.6 us
    mul x2, other arithmetic, vertical(): (thickness[depth_index] * fields[:, depth_index] + coupling_above * prev_...  56.6 us
  transfers between devices with their start and end apart: 48, of which 14 were waited for; matrix products, arithmetic and copies ran while one was open for 28% of the time, Pallas kernels for 0%

commit v1 on v0

v1 whole, which is shorter than its diff:
```python
import functools

import jax
import jax.numpy as jnp
import numpy as np
from jax import lax
from jax.experimental import pallas as pl
from jax.experimental.pallas import tpu as pltpu
from jax.sharding import PartitionSpec as P

ITERS = 3
K = 48
HORIZONTAL_RATE = 0.2
FLUX_SCALE = 0.02
FACE_SCALE = 0.25
F32 = jnp.float32

PAIR_UV = 0
PAIR_VISC = 48
PAIR_SURF = 72
ROW_X = 73
ROW_SCAL = 79
LAT_TILES = 115
PL_U, PL_V, PL_VISC, PL_WET, PL_STO, PL_SUR = 0, 48, 96, 143, 144, 145
PLANES = 146
LON_WIDE = 10
LON_TILES = LON_WIDE + 3


def sub_iota():
    return lax.broadcasted_iota(jnp.int32, (8, 128), 0)


def lane_iota():
    return lax.broadcasted_iota(jnp.int32, (8, 128), 1)


def lroll(x, shift):
    return pltpu.roll(x, shift, 1)


def sroll(x, shift):
    return pltpu.roll(x, shift, 0)


def flip_lanes(x):
    return jnp.take_along_axis(x, 127 - lane_iota(), axis=1)


def flip_rows(x):
    sub = sub_iota()
    x = sroll(x, 4)
    x = jnp.where((sub & 2) == 0, sroll(x, 6), sroll(x, 2))
    return jnp.where((sub & 1) == 0, sroll(x, 7), sroll(x, 1))


def thickness_at(level):
    return 0.5 + level / 48.0


def spacing_at(level):
    return 2.0 / (thickness_at(level) + thickness_at(level + 1.0))


def depth_of(count):
    return 0.5 * count + count * (count - 1.0) * (1.0 / 96.0)


def pack_lat(flags, state, visc, wet, storage, surf, pay_a, pay_b):
    odd = flags[0]
    sub = sub_iota()
    keep = (sub < 4).astype(jnp.int32) == odd

    def pair(tile, first, second):
        rolled = sroll(second, 4)
        pay_a[tile] = jnp.where(keep, first, rolled)
        pay_b[tile] = jnp.where(keep, rolled, first)

    wet_now = wet[...].astype(F32)

    @pl.loop(0, 48, unroll=8)
    def _(k):
        pair(k, state[pl.ds(k * 8, 8), :], state[pl.ds((k + 48) * 8, 8), :])

    @pl.loop(0, 23)
    def _(m):
        pair(PAIR_VISC + m, visc[2 * m], visc[2 * m + 1])

    pair(PAIR_VISC + 23, visc[46], wet_now)
    pair(PAIR_SURF, storage[...], surf[...])
    least = jnp.broadcast_to(jnp.minimum(wet_now[3:4], wet_now[4:5]), (8, 128))
    for m in range(6):
        start = (48 + 8 * m) * 8
        row3 = state[pl.ds(start + 3, 8, stride=8), :]
        row4 = state[pl.ds(start + 4, 8, stride=8), :]
        level = (sub + 8 * m).astype(F32)
        diff = jnp.where(level < least, row3 - row4, 0.0)
        pay_a[ROW_X + m] = diff
        pay_b[ROW_X + m] = diff
    for t in range(36):
        start = (96 + 8 * t) * 8
        row0 = state[pl.ds(start, 8, stride=8), :]
        row7 = state[pl.ds(start + 7, 8, stride=8), :]
        pay_a[ROW_SCAL + t] = jnp.where(odd == 1, row0, row7)
        pay_b[ROW_SCAL + t] = jnp.where(odd == 1, row7, row0)

    @pl.when(flags[1] == 1)
    def _():
        @pl.loop(0, 48, unroll=4)
        def _(t):
            pay_b[t] = -flip_rows(flip_lanes(pay_b[t]))

        @pl.loop(48, 73)
        def _(t):
            pay_b[t] = flip_rows(flip_lanes(pay_b[t]))

        @pl.loop(73, 79)
        def _(t):
            pay_b[t] = -flip_lanes(pay_b[t])

        @pl.loop(79, 115)
        def _(t):
            pay_b[t] = flip_lanes(pay_b[t])


def pack_lon(flags, state, visc, wet, storage, surf, rec_a, rec_b, rows, row_x, far, near):
    odd = flags[0]
    odd_lon = flags[2]
    sub = sub_iota()
    lane = lane_iota()
    keep = (sub < 4).astype(jnp.int32) != odd

    def unpair(tile):
        a, b = rec_a[tile], rec_b[tile]
        return jnp.where(keep, a, b), sroll(jnp.where(keep, b, a), 4)

    @pl.loop(0, 48, unroll=8)
    def _(k):
        first, second = unpair(k)
        rows[PL_U + k] = first
        rows[PL_V + k] = second

    @pl.loop(0, 24, unroll=4)
    def _(m):
        first, second = unpair(PAIR_VISC + m)
        rows[PL_VISC + 2 * m] = first
        rows[PL_VISC + 2 * m + 1] = second

    first, second = unpair(PAIR_SURF)
    rows[PL_STO] = first
    rows[PL_SUR] = second
    for m in range(6):
        row_x[m] = jnp.where(odd == 1, rec_b[ROW_X + m], rec_a[ROW_X + m])

    wet_now = wet[...].astype(F32)

    def plane(n):
        if n < 96:
            return state[n * 8 : n * 8 + 8, :]
        if n < 143:
            return visc[n - 96]
        if n == 143:
            return wet_now
        if n == 144:
            return storage[...]
        if n == 145:
            return surf[...]
        if n < 292:
            return rows[n - 146]
        return row_x[n - 292]

    def emit(tile, planes, width):
        east = jnp.zeros((8, 128), F32)
        west = jnp.zeros((8, 128), F32)
        slots = 128 // width
        slot_of = lane // width
        for j, load in enumerate(planes):
            x = load()
            x = lroll(x, j * width) if j else x
            west = jnp.where(slot_of == j, x, west)
            east = jnp.where(slot_of == (j - 1) % slots, x, east)
        far[tile] = jnp.where(odd_lon == 1, east, west)
        near[tile] = jnp.where(odd_lon == 1, west, east)

    for tile in range(LON_WIDE):
        emit(tile, [functools.partial(plane, n) for n in range(32 * tile, min(32 * tile + 32, 298))], 4)

    def scalar(n):
        return state[(96 + n) * 8 : (96 + n) * 8 + 8, :]

    for tile in range(3):
        emit(LON_WIDE + tile, [functools.partial(scalar, n) for n in range(128 * tile, min(128 * tile + 128, 288))], 1)


def momentum(
    flags, state, visc, wet, storage, surf, rows, row_x, far, near,
    mixed, zed, moments,
    field, couple, gain, done, planes2, xs,
):
    odd_lon = flags[2]
    top = flags[1] == 1
    lane = lane_iota()
    sub = sub_iota()
    slot_of = lane // 4
    valid = jnp.logical_or(lane < 4, lane >= 124)

    def strip(n):
        tile, j = n // 32, n % 32
        a, b = far[tile], near[tile]
        mine = (slot_of == j).astype(jnp.int32) == odd_lon
        return lroll(jnp.where(mine, a, b), (128 - 4 * j) % 128)

    @pl.loop(0, 96, unroll=8)
    def _(n):
        field[n, 0] = state[pl.ds(n * 8, 8), :]
        field[n, 1] = rows[n]
        field[n, 2] = strip(n)
        field[n, 3] = strip(n + 146)

    @pl.loop(0, 6)
    def _(m):
        xs[m] = strip(m + 292)

    def four(n, own, mask):
        out = [own, rows[n], strip(n), strip(n + 146)]
        if mask:
            out[2] = jnp.where(valid, out[2], 0.0)
            out[3] = jnp.where(valid, out[3], 0.0)
        return out

    def east(q):
        return [
            lroll(jnp.where(lane == 0, q[2], q[0]), 127),
            lroll(jnp.where(lane == 0, q[3], q[1]), 127),
            lroll(jnp.where(lane == 0, q[0], q[2]), 127),
            lroll(jnp.where(lane == 0, q[1], q[3]), 127),
        ]

    def west(q):
        return [
            lroll(jnp.where(lane == 127, q[2], q[0]), 1),
            lroll(jnp.where(lane == 127, q[3], q[1]), 1),
            lroll(jnp.where(lane == 127, q[0], q[2]), 1),
            lroll(jnp.where(lane == 127, q[1], q[3]), 1),
        ]

    def north(q):
        return [
            sroll(jnp.where(sub == 0, q[1], q[0]), 7),
            sroll(jnp.where(sub == 0, q[0], q[1]), 7),
            sroll(jnp.where(sub == 0, q[3], q[2]), 7),
            sroll(jnp.where(sub == 0, q[2], q[3]), 7),
        ]

    def south(q):
        return [
            sroll(jnp.where(sub == 7, q[1], q[0]), 1),
            sroll(jnp.where(sub == 7, q[0], q[1]), 1),
            sroll(jnp.where(sub == 7, q[3], q[2]), 1),
            sroll(jnp.where(sub == 7, q[2], q[3]), 1),
        ]

    def each(fn, *lists):
        return [fn(*items) for items in zip(*lists)]

    level_count = four(PL_WET, wet[...].astype(F32), True)
    counts = [each(jnp.minimum, level_count, shift(level_count)) for shift in (east, west, north, south)]
    for i, c in enumerate(counts):
        for j in range(4):
            planes2[4 * i + j] = c[j]
    for j in range(4):
        planes2[16 + j] = level_count[j]
    ghost = jnp.logical_and(top, sub < 4)
    planes2[20] = counts[0][0]
    planes2[21] = jnp.where(ghost, counts[1][1], counts[0][1])
    planes2[22] = counts[0][2]
    planes2[23] = jnp.where(ghost, counts[1][3], counts[0][3])
    planes2[24] = counts[2][0]
    planes2[25] = jnp.where(ghost, counts[3][1], counts[2][1])
    planes2[26] = counts[2][2]
    planes2[27] = jnp.where(ghost, counts[3][3], counts[2][3])

    def blend(base, k, kf):
        q = [field[base + k, j] for j in range(4)]
        faces = [east(q), west(q), north(q), south(q)]
        change = []
        for j in range(4):
            total = None
            for i in range(4):
                term = jnp.where(kf < planes2[4 * i + j], faces[i][j] - q[j], 0.0)
                if base == PL_V and i == 2 and j in (1, 3):
                    source = row_x if j == 1 else xs
                    extra = jnp.broadcast_to(source[k // 8, pl.ds(k % 8, 1), :], (8, 128))
                    term = jnp.where(jnp.logical_and(top, sub == 3), extra, term)
                total = term if total is None else total + term
            change.append(q[j] + HORIZONTAL_RATE * total)
        return change

    zero = jnp.zeros((8, 128), F32)

    @pl.loop(0, 47, unroll=8)
    def _(k):
        couple[k, 0] = visc[k]
        couple[k, 1] = rows[PL_VISC + k]
        couple[k, 2] = strip(PL_VISC + k)
        couple[k, 3] = strip(PL_VISC + k + 146)

    for j in range(4):
        couple[47, j] = zero

    def forward(k, carry):
        above, prev_gain, prev_u, prev_v = carry
        kf = k.astype(F32)
        thick = thickness_at(kf)
        space = spacing_at(kf)
        below = [jnp.where(kf + 1.0 < planes2[16 + j], couple[k, j] * space, 0.0) for j in range(4)]
        u = blend(PL_U, k, kf)
        v = blend(PL_V, k, kf)
        new_gain, new_u, new_v = [], [], []
        for j in range(4):
            inverse = 1.0 / (thick + above[j] + below[j] - above[j] * prev_gain[j])
            new_gain.append(below[j] * inverse)
            new_u.append((thick * u[j] + above[j] * prev_u[j]) * inverse)
            new_v.append((thick * v[j] + above[j] * prev_v[j]) * inverse)
            gain[k, j] = new_gain[j]
            done[k, j] = new_u[j]
            done[k + 48, j] = new_v[j]
        return below, new_gain, new_u, new_v

    zeros = [zero] * 4
    lax.fori_loop(0, 48, forward, (zeros, zeros, zeros, zeros), unroll=2)

    def backward(i, carry):
        k = 47 - i
        kf = k.astype(F32)
        thick = thickness_at(kf)
        low_u, low_v, flux_u, flux_v = carry
        new_u, new_v, out_u, out_v = [], [], [], []
        for j in range(4):
            g = gain[k, j]
            x_u = done[k, j] + g * low_u[j]
            x_v = done[k + 48, j] + g * low_v[j]
            new_u.append(x_u)
            new_v.append(x_v)
            out_u.append(flux_u[j] + jnp.where(kf < planes2[20 + j], thick * x_u, 0.0))
            out_v.append(flux_v[j] + jnp.where(kf < planes2[24 + j], thick * x_v, 0.0))
        mixed[pl.ds(k * 8, 8), :] = new_u[0]
        mixed[pl.ds((k + 48) * 8, 8), :] = new_v[0]
        return new_u, new_v, out_u, out_v

    _, _, flux_u, flux_v = lax.fori_loop(0, 48, backward, (zeros, zeros, zeros, zeros), unroll=4)

    last = jnp.logical_and(top, sub == 7)
    first_ghost = jnp.logical_and(top, sub == 0)
    flux_v = [
        jnp.where(last, 0.0, flux_v[0]),
        jnp.where(first_ghost, 0.0, flux_v[1]),
        jnp.where(last, 0.0, flux_v[2]),
        jnp.where(first_ghost, 0.0, flux_v[3]),
    ]
    plain = each(
        lambda a, b, c, d: a - b + c - d, flux_u, west(flux_u), flux_v, south(flux_v)
    )
    mirrored = each(
        lambda a, b, c, d: a - b + c - d, east(flux_u), flux_u, north(flux_v), flux_v
    )
    divergence = [
        plain[0],
        jnp.where(ghost, mirrored[1], plain[1]),
        plain[2],
        jnp.where(ghost, mirrored[3], plain[3]),
    ]
    sto = four(PL_STO, storage[...], True)
    old = four(PL_SUR, surf[...], True)
    faces = [[FACE_SCALE * depth_of(planes2[4 * i + j]) for j in range(4)] for i in range(4)]
    diagonal = [
        jnp.maximum(sto[j] + faces[0][j] + faces[1][j] + faces[2][j] + faces[3][j], 0.1) for j in range(4)
    ]
    ocean = [planes2[16 + j] > 0.0 for j in range(4)]
    start = [jnp.where(ocean[j], old[j], 0.0) for j in range(4)]
    around = [east(start), west(start), north(start), south(start)]
    inverse = [1.0 / diagonal[j] for j in range(4)]
    basis = []
    for j in range(4):
        forcing = jnp.where(ocean[j], sto[j] * old[j] - FLUX_SCALE * divergence[j], 0.0)
        image = sto[j] * start[j]
        for i in range(4):
            image = image + faces[i][j] * (start[j] - around[i][j])
        basis.append((forcing - image) / diagonal[j])
    z0 = basis

    def spread(z):
        nb = [east(z), west(z), north(z), south(z)]
        return [
            (faces[0][j] * nb[0][j] + faces[1][j] * nb[1][j] + faces[2][j] * nb[2][j] + faces[3][j] * nb[3][j])
            * inverse[j]
            for j in range(4)
        ]

    z1 = spread(z0)
    z2 = spread(z1)
    zed[0] = start[0]
    zed[1] = z0[0]
    zed[2] = z1[0]
    zed[3] = z2[0]
    weighted = [diagonal[0] * z[0] for z in (z0, z1, z2)]
    north_weight = jnp.where(last, 1.0, 2.0)
    edge = z2[0] * (
        2.0 * faces[0][0] * east(z2)[0] + north_weight * faces[2][0] * north(z2)[0]
    )
    products = [
        weighted[0] * z0[0],
        weighted[0] * z1[0],
        weighted[1] * z1[0],
        weighted[1] * z2[0],
        weighted[2] * z2[0],
        edge,
    ]
    tile = zero
    for i, product in enumerate(products):
        total = jnp.sum(jnp.sum(product, axis=0, keepdims=True), axis=1, keepdims=True)
        tile = jnp.where(sub == i, total, tile)
    for i in range(moments.shape[0]):
        moments[i] = tile


def tracers(flags, state, diff, wet, around, rec_a, rec_b, far, near, mixed_in, out, gain, done):
    out[0 : 96 * 8, :] = mixed_in[...]
    odd = flags[0]
    odd_lon = flags[2]
    lane = lane_iota()
    sub = sub_iota()
    level_count = wet[...].astype(F32)
    counts = [around[i] for i in range(4)]
    zero = jnp.zeros((8, 128), F32)

    def forward(k, carry):
        above, prev_gain, prev = carry
        kf = k.astype(F32)
        thick = thickness_at(kf)
        coefficient = diff[jnp.minimum(k, 46)]
        below = jnp.where(kf + 1.0 < level_count, coefficient * spacing_at(kf), 0.0)
        inverse = 1.0 / (thick + above + below - above * prev_gain)
        new_gain = below * inverse
        gain[k] = new_gain
        open_face = [kf < c for c in counts]
        new = []
        for f in range(6):
            n = f * 48 + k
            q = state[pl.ds((96 + n) * 8, 8), :]
            row_a = rec_a[n // 8, pl.ds(n % 8, 1), :]
            row_b = rec_b[n // 8, pl.ds(n % 8, 1), :]
            row_n = jnp.broadcast_to(jnp.where(odd == 1, row_b, row_a), (8, 128))
            row_s = jnp.broadcast_to(jnp.where(odd == 1, row_a, row_b), (8, 128))
            j = n % 128
            a, b = far[LON_WIDE + n // 128], near[LON_WIDE + n // 128]
            side = lroll(jnp.where((lane == j).astype(jnp.int32) == odd_lon, a, b), (128 - j) % 128)
            nbs = (
                lroll(jnp.where(lane == 0, side, q), 127),
                lroll(jnp.where(lane == 127, side, q), 1),
                sroll(jnp.where(sub == 0, row_n, q), 7),
                sroll(jnp.where(sub == 7, row_s, q), 1),
            )
            change = zero
            for i in range(4):
                change = change + jnp.where(open_face[i], nbs[i] - q, 0.0)
            value = (thick * (q + HORIZONTAL_RATE * change) + above * prev[f]) * inverse
            done[n] = value
            new.append(value)
        return below, new_gain, new

    lax.fori_loop(0, 48, forward, (zero, zero, [zero] * 6), unroll=2)

    def backward(i, low):
        k = 47 - i
        g = gain[k]
        new = []
        for f in range(6):
            n = f * 48 + k
            value = done[n] + g * low[f]
            out[pl.ds((96 + n) * 8, 8), :] = value
            new.append(value)
        return new

    lax.fori_loop(0, 48, backward, [zero] * 6, unroll=4)


def finish(parts, zed, surface):
    total = parts[0]
    for i in range(1, parts.shape[0]):
        total = total + parts[i]
    nu = [jnp.broadcast_to(total[i : i + 1, :], (8, 128)) for i in range(6)]

    def inner(p, q, shift):
        out = None
        for i, a in enumerate(p):
            for j, b in enumerate(q):
                term = a * b * nu[i + j + shift]
                out = term if out is None else out + term
        return out

    one = jnp.ones((8, 128), F32)
    scaled = [one]
    direction = [one]
    product = nu[0]
    move = [jnp.zeros((8, 128), F32)] * 3
    for iteration in range(ITERS):
        curvature = inner(direction, direction, 0) - inner(direction, direction, 1)
        alpha = product / curvature
        for i, d in enumerate(direction):
            move[i] = move[i] + alpha * d
        if iteration + 1 < ITERS:
            longer = scaled + [jnp.zeros((8, 128), F32)]
            for i, d in enumerate(direction):
                longer[i] = longer[i] - alpha * d
                longer[i + 1] = longer[i + 1] + alpha * d
            scaled = longer
            following = inner(scaled, scaled, 0)
            beta = following / product
            direction = [
                scaled[i] + (beta * direction[i] if i < len(direction) else 0.0) for i in range(len(scaled))
            ]
            product = following
    surface[...] = zed[0] + move[0] * zed[1] + move[1] * zed[2] + move[2] * zed[3]


VMEM_LIMIT = 48 * 1024 * 1024


def kernel(body, outs, scratch=(), smem=1, operands=0, flops=0, nbytes=0):
    vmem = pl.BlockSpec(memory_space=pltpu.VMEM)
    return pl.pallas_call(
        body,
        out_shape=[jax.ShapeDtypeStruct(s, F32) for s in outs],
        in_specs=[pl.BlockSpec(memory_space=pltpu.SMEM)] * smem + [vmem] * operands,
        out_specs=[vmem] * len(outs),
        scratch_shapes=[pltpu.VMEM(s, F32) for s in scratch],
        compiler_params=pltpu.CompilerParams(vmem_limit_bytes=VMEM_LIMIT),
        cost_estimate=pl.CostEstimate(flops=flops, bytes_accessed=nbytes, transcendentals=0),
    )


def lat_pairs(lat, lon):
    first, second = [], []
    for l in range(lat):
        for p in range(lon):
            here = l * lon + p
            first.append((here, (l ^ 1) * lon + p))
            if l == lat - 1:
                second.append((here, l * lon + lon - 1 - p))
            elif l % 2 == 1:
                second.append((here, here + lon))
            elif l > 0:
                second.append((here, here - lon))
    return first, second


def lon_pairs(lon):
    far, near = [], []
    for p in range(lon):
        step = 1 if p % 2 else -1
        far.append((p, (p + step) % lon))
        near.append((p, p ^ 1))
    return far, near


def make_local(mesh_shape):
    lat, lon = mesh_shape["lat"], mesh_shape["lon"]
    pairs_a, pairs_b = lat_pairs(lat, lon)
    pairs_far, pairs_near = lon_pairs(lon)
    both = ("lat", "lon")
    stages = reduction_stages(lat, lon)

    def local(ocean_state, viscosity, diffusivity, wet_levels, storage, surface_old):
        band = lax.axis_index("lat")
        place = lax.axis_index("lon")
        flags = jnp.stack([band % 2, (band == lat - 1).astype(jnp.int32), place % 2]).astype(jnp.int32)
        state = ocean_state.reshape(8 * K * 8, 128)
        fixed = (viscosity, wet_levels, storage, surface_old)
        pay_a, pay_b = kernel(pack_lat, [(LAT_TILES, 8, 128)] * 2, operands=5)(flags, state, *fixed)
        rec_b = lax.ppermute(pay_b, both, pairs_b)
        rec_a = lax.ppermute(pay_a, both, pairs_a)
        rows, row_x, pay_far, pay_near = kernel(
            pack_lon,
            [(PLANES, 8, 128), (6, 8, 128), (LON_TILES, 8, 128), (LON_TILES, 8, 128)],
            operands=7,
        )(flags, state, *fixed, rec_a, rec_b)
        rec_far = lax.ppermute(pay_far, "lon", pairs_far)
        rec_near = lax.ppermute(pay_near, "lon", pairs_near)
        mixed, zed, around, moments = kernel(
            momentum_entry,
            [(2 * K * 8, 128), (4, 8, 128), (4, 8, 128), (stages[0][1], 8, 128)],
            scratch=[(96, 4, 8, 128), (48, 4, 8, 128), (48, 4, 8, 128), (96, 4, 8, 128), (28, 8, 128), (6, 8, 128)],
            operands=9,
        )(flags, state, *fixed, rows, row_x, rec_far, rec_near)
        parts = moments
        for i, (groups, size, following) in enumerate(stages):
            if i:
                parts = jnp.broadcast_to(jnp.sum(parts, axis=0)[None], (size, 8, 128))
            parts = lax.all_to_all(parts, both, 0, 0, axis_index_groups=groups, tiled=True)
        (mixed,) = kernel(
            tracers,
            [(8 * K * 8, 128)],
            scratch=[(48, 8, 128), (288, 8, 128)],
            operands=9,
            flops=20_000_000,
            nbytes=6_000_000,
        )(
            flags, state, diffusivity, wet_levels, around,
            rec_a[ROW_SCAL:], rec_b[ROW_SCAL:], rec_far, rec_near, mixed,
        )
        (surface,) = kernel(finish, [(8, 128)], smem=0, operands=2)(parts, zed)
        return mixed.reshape(8, K, 8, 128), surface

    return local


def momentum_entry(*refs):
    inputs, outputs, scratch = refs[:10], refs[10:14], refs[14:]
    mixed, zed, around, moments = outputs
    momentum(*inputs, mixed, zed, moments, *scratch)
    planes2 = scratch[4]
    for i in range(4):
        around[i] = planes2[4 * i]


def reduction_stages(lat, lon):
    index = np.arange(lat * lon)
    if lat == 32 and lon == 16:
        grid = index.reshape(8, 4, 4, 2, 2)
        along_z = grid.transpose(1, 2, 4, 3, 0).reshape(32, 16)
        rest = grid.transpose(0, 3, 1, 2, 4).reshape(16, 32)
    else:
        grid = index.reshape(lat, lon)
        along_z, rest = grid.T, grid
    return [(g.tolist(), g.shape[1], None) for g in (along_z, rest)]


def solution(mesh):
    placed = (
        P(None, None, "lat", "lon"),
        P(None, "lat", "lon"),
        P(None, "lat", "lon"),
        P("lat", "lon"),
        P("lat", "lon"),
        P("lat", "lon"),
    )
    return jax.shard_map(
        make_local(dict(mesh.shape)),
        mesh=mesh,
        in_specs=placed,
        out_specs=(P(None, None, "lat", "lon"), P("lat", "lon")),
        check_vma=False,
    )
```

time: 1190 us -> 109 us (0.09)
  blocking collectives: 528 us -> 24.9 us
  other arithmetic: 313 us -> 0.09 us
  starting transfers between devices: 217 us -> 51.1 us
  waiting for transfers between devices: 86.8 us -> 6.15 us
  Pallas kernels: 0 us -> 20.7 us
  local copies, waits for them, and re-layouts: 23.8 us -> 5.09 us
    psum x5 -> x0, blocking collectives: 528 us -> none  [the longest x3 315 us: residual_product(): return lax.psum(jnp.sum(residual * scaled), ('lat', 'lon'))]
    ppermute x46 -> x4, starting transfers between devices: 193 us -> 29.3 us  [the longest x1 21.3 us: local(): rec_far = lax.ppermute(pay_far, 'lon', pairs_far)]
    mul x37 -> x0, other arithmetic: 130 us -> none  [the longest x32 68.1 us: vertical(): lower_value = eliminated[depth_index] + gain_list[depth_index] * lower_value]
    div x11 -> x0, other arithmetic: 84.7 us -> none  [the longest x9 83.9 us: vertical(): 1.0 / (thickness[depth_index] + coupling_above + coupling_below - couplin...]
    ppermute x46 -> x4, waiting for transfers between devices: 86.8 us -> 6.14 us  [the longest x1 5.29 us: local(): rec_a = lax.ppermute(pay_a, both, pairs_a)]
    unnamed x48 -> x0, other arithmetic: 79.2 us -> none
    all_to_all x0 -> x1, blocking collectives: none -> 24.9 us  [local(): lax.all_to_all(parts, both, 0, 0, axis_index_groups=groups, tiled=True)]
    pallas_call x0 -> x5, Pallas kernels: none -> 20.7 us  [the longest x1 9.02 us: local(): kernel(tracers, [(8 * K * 8, 128)], scratch=[(48, 8, 128), (288, 8, 128)]...]
  transfers between devices with their start and end apart: 48 -> 5, of which waited for: 14 -> 2; matrix products, arithmetic and copies ran while one was open for 28% -> 0% of each run, Pallas kernels for 0% -> 8%
where the time goes in v1:
time: 109 us
  starting transfers between devices  51.1 us (47%)
  blocking collectives  24.9 us (23%)
  Pallas kernels  20.7 us (19%)
  waiting for transfers between devices  6.15 us (6%)
  local copies, waits for them, and re-layouts  5.09 us (5%)
    all_to_all x1, blocking collectives, local(): lax.all_to_all(parts, both, 0, 0, axis_index_groups=groups, tiled=True)  24.9 us
    all_to_all x1, starting transfers between devices, local(): lax.all_to_all(parts, both, 0, 0, axis_index_groups=groups, tiled=True)  21.8 us
    ppermute x1, starting transfers between devices, local(): rec_far = lax.ppermute(pay_far, 'lon', pairs_far)  21.3 us
    pallas_call x1, Pallas kernels, local(): kernel(tracers, [(8 * K * 8, 128)], scratch=[(48, 8, 128), (288, 8, 128)]...  9.02 us
    pallas_call x1, Pallas kernels, local(): kernel(momentum_entry, [(2 * K * 8, 128), (4, 8, 128), (4, 8, 128), (stag...  8.9 us
    ppermute x1, waiting for transfers between devices, local(): rec_a = lax.ppermute(pay_a, both, pairs_a)  5.29 us
    unnamed x16, local copies, waits for them, and re-layouts  4.4 us
    ppermute x1, starting transfers between devices, local(): rec_a = lax.ppermute(pay_a, both, pairs_a)  3.95 us
  transfers between devices with their start and end apart: 5, of which 2 were waited for; matrix products, arithmetic and copies ran while one was open for 0% of the time, Pallas kernels for 8%

profile of v1, /device:TPU:1, one launch (start us, length us, event | category | flops | bytes accessed | tf_op | source)
XLA Modules:
  0.0 108.9 jit_solution(12057359492120094)
XLA Ops:
  0.6 0.1 pad_add_fusion.flags.refs_0_
  0.7 1.4 %copy-done = f32[8,48,8,128]{3,2,1,0:T(8,128)S(1)} copy-done((f32[8,48,8,128]{3,2,1,0:T(8,128)S(1)}, f32[8,48,8,128]{3,2,1,0:T(8,128)}, u32[]{:S(2)}) %copy-start) | copy-done | bytes 1572888
  2.1 0.9 copy-done.2
  3.1 0.7 copy-done.4
  3.8 0.7 copy-done.6
  4.4 0.7 copy-done.7
  5.1 0.8 shard_map.77
  5.9 3.9 %collective-permute-start = (f32[115,8,128]{2,1,0:T(8,128)S(1)}, f32[115,8,128]{2,1,0:T(8,128)S(1)}, u32[]{:S(2)}, u32[]{:S(2)}) collective-permute-start(f32[115,8,128]{2,1,0:T(8,128)S(1)} %get-tuple-element.12), channel_id=1, source_target_pairs={{0,16},{1,17},{2,18},{3,19},{4,20},{5,21},{6,22},{7,23},{8,24},{9,... | collective-permute-start | bytes 1413128 | tf_op jit(solution)/shard_map/ppermute | solution.py:582
  9.9 0.7 collective-permute-start.1
  10.6 5.3 %collective-permute-done.rec_a = f32[115,8,128]{2,1,0:T(8,128)S(1)} collective-permute-done((f32[115,8,128]{2,1,0:T(8,128)S(1)}, f32[115,8,128]{2,1,0:T(8,128)S(1)}, u32[]{:S(2)}, u32[]{:S(2)}) %collective-permute-start) | collective-permute-done | bytes 471072 | tf_op jit(solution)/shard_map/ppermute | solution.py:582
  15.9 0.0 collective-permute-done.1.rec_b
  15.9 1.3 %shard_map.78 = (f32[146,8,128]{2,1,0:T(8,128)S(1)}, f32[6,8,128]{2,1,0:T(8,128)S(1)}, f32[13,8,128]{2,1,0:T(8,128)S(1)}, f32[13,8,128]{2,1,0:T(8,128)S(1)}) custom-call(s32[3]{0:T(128)S(1)} %pad_add_fusion.flags.refs_0_, f32[3072,128]{1,0:T(8,128)S(1)} %bitcast.6, f32[47,8,128]{2,1,0:T(8,128)S(1)} %copy-done.2, s32[8,128]{1,0:T(8,128)S(1)} %copy-done.4, ...), custom_call_target="tpu_custom_call" | custom-call | tf_op jit(solution)/shard_map/pallas_call | solution.py:583
  17.2 21.3 %collective-permute-start.2 = (f32[13,8,128]{2,1,0:T(8,128)S(1)}, f32[13,8,128]{2,1,0:T(8,128)S(1)}, u32[]{:S(2)}, u32[]{:S(2)}) collective-permute-start(f32[13,8,128]{2,1,0:T(8,128)S(1)} %get-tuple-element.16), channel_id=1, source_target_pairs={{0,15},{1,2},{2,1},{3,4},{4,3},{5,6},{6,5},{7,8},{8,7},{9,10},{10,... | collective-permute-start | bytes 159752 | tf_op jit(solution)/shard_map/ppermute | solution.py:588
  38.5 3.3 %collective-permute-start.3 = (f32[13,8,128]{2,1,0:T(8,128)S(1)}, f32[13,8,128]{2,1,0:T(8,128)S(1)}, u32[]{:S(2)}, u32[]{:S(2)}) collective-permute-start(f32[13,8,128]{2,1,0:T(8,128)S(1)} %get-tuple-element.17), channel_id=1, source_target_pairs={{0,1},{1,0},{2,3},{3,2},{4,5},{5,4},{6,7},{7,6},{8,9},{9,8},{10,11... | collective-permute-start | bytes 159752 | tf_op jit(solution)/shard_map/ppermute | solution.py:589
  41.8 0.0 collective-permute-done.2.refs_8_.far
  41.8 0.9 collective-permute-done.3.refs_9_.near
  42.7 8.9 %shard_map.79 = (f32[768,128]{1,0:T(8,128)S(1)}, f32[4,8,128]{2,1,0:T(8,128)S(1)}, f32[4,8,128]{2,1,0:T(8,128)S(1)}, f32[16,8,128]{2,1,0:T(8,128)S(1)}) custom-call(s32[3]{0:T(128)S(1)} %pad_add_fusion.flags.refs_0_, f32[3072,128]{1,0:T(8,128)S(1)} %bitcast.7, f32[47,8,128]{2,1,0:T(8,128)S(1)} %copy-done.2, s32[8,128]{1,0:T(8,128)S(1)} %copy-done.4, ...), custom_call_target="tpu_custom_call" | custom-call | tf_op jit(solution)/shard_map/pallas_call | solution.py:590
  51.6 24.9 %all_to_all.10 = f32[16,8,128]{2,1,0:T(8,128)S(1)} all-to-all(f32[16,8,128]{2,1,0:T(8,128)S(1)} %get-tuple-element.20), channel_id=1, replica_groups={{0,64,128,192,256,320,384,448,2,66,130,194,258,322,386,450},{1,65,129,1..., dimensions={0} | all-to-all | bytes 131072 | tf_op jit(solution)/shard_map/all_to_all | solution.py:600
  76.6 0.7 broadcast_in_dim.2
  77.2 21.8 %all-to-all-start.1 = ((f32[32,8,128]{2,1,0:T(8,128)}), f32[32,8,128]{2,1,0:T(8,128)S(1)}, u32[]{:S(2)}, u32[]{:S(2)}) async-start(f32[32,8,128]{2,1,0:T(8,128)} %broadcast_in_dim.2), calls=%async_computation.1 | async-start | bytes 262144 | tf_op jit(solution)/shard_map/all_to_all | solution.py:600
  99.1 0.0 copy-done.1
  99.1 9.0 %shard_map.80 = f32[3072,128]{1,0:T(8,128)} custom-call(s32[3]{0:T(128)S(1)} %pad_add_fusion.flags.refs_0_, f32[3072,128]{1,0:T(8,128)S(1)} %bitcast.8, f32[47,8,128]{2,1,0:T(8,128)S(1)} %copy-done.3, s32[8,128]{1,0:T(8,128)S(1)} %copy-done.5, f32[4,8,128]{2,1,0:T(8,128)S(1)} %get-tuple-element.18.around, f32[36,8,128]{2,1,0:T(8,128)S(1)} %slice.8.rec_a, ...), custom_call_target="tpu_custom_call" | custom-call | flops 20000000 | bytes 6000000 | tf_op jit(solution)/shard_map/pallas_call | solution.py:601
  108.2 0.0 all-to-all-done.1.parts
  108.2 0.7 shard_map.81
  (13 shorter events, 0.1 us)
Async XLA Ops:
  0.7 1.4 %copy-start = (f32[8,48,8,128]{3,2,1,0:T(8,128)S(1)}, f32[8,48,8,128]{3,2,1,0:T(8,128)}, u32[]{:S(2)}) copy-start(f32[8,48,8,128]{3,2,1,0:T(8,128)} %param.6) | copy-start | bytes 4718596
  2.1 0.9 copy-start.2
  3.1 0.7 copy-start.4
  3.7 0.7 copy-start.6
  4.4 0.7 copy-start.7
  5.9 9.9 %collective-permute-start = (f32[115,8,128]{2,1,0:T(8,128)S(1)}, f32[115,8,128]{2,1,0:T(8,128)S(1)}, u32[]{:S(2)}, u32[]{:S(2)}) collective-permute-start(f32[115,8,128]{2,1,0:T(8,128)S(1)} %get-tuple-element.12), channel_id=1, source_target_pairs={{0,16},{1,17},{2,18},{3,19},{4,20},{5,21},{6,22},{7,23},{8,24},{9,... | collective-permute-start | bytes 1413128 | tf_op jit(solution)/shard_map/ppermute | solution.py:582
  9.9 6.0 %collective-permute-start.1 = (f32[115,8,128]{2,1,0:T(8,128)S(1)}, f32[115,8,128]{2,1,0:T(8,128)S(1)}, u32[]{:S(2)}, u32[]{:S(2)}) collective-permute-start(f32[115,8,128]{2,1,0:T(8,128)S(1)} %get-tuple-element.13), channel_id=1, source_target_pairs={{16,32},{17,33},{18,34},{19,35},{20,36},{21,37},{22,38},{23,39},{2... | collective-permute-start | bytes 1413128 | tf_op jit(solution)/shard_map/ppermute | solution.py:581
  17.2 24.6 %collective-permute-start.2 = (f32[13,8,128]{2,1,0:T(8,128)S(1)}, f32[13,8,128]{2,1,0:T(8,128)S(1)}, u32[]{:S(2)}, u32[]{:S(2)}) collective-permute-start(f32[13,8,128]{2,1,0:T(8,128)S(1)} %get-tuple-element.16), channel_id=1, source_target_pairs={{0,15},{1,2},{2,1},{3,4},{4,3},{5,6},{6,5},{7,8},{8,7},{9,10},{10,... | collective-permute-start | bytes 159752 | tf_op jit(solution)/shard_map/ppermute | solution.py:588
  38.5 4.2 %collective-permute-start.3 = (f32[13,8,128]{2,1,0:T(8,128)S(1)}, f32[13,8,128]{2,1,0:T(8,128)S(1)}, u32[]{:S(2)}, u32[]{:S(2)}) collective-permute-start(f32[13,8,128]{2,1,0:T(8,128)S(1)} %get-tuple-element.17), channel_id=1, source_target_pairs={{0,1},{1,0},{2,3},{3,2},{4,5},{5,4},{6,7},{7,6},{8,9},{9,8},{10,11... | collective-permute-start | bytes 159752 | tf_op jit(solution)/shard_map/ppermute | solution.py:589
  42.7 56.4 %copy-start.1 = (f32[8,48,8,128]{3,2,1,0:T(8,128)S(1)}, f32[8,48,8,128]{3,2,1,0:T(8,128)}, u32[]{:S(2)}) copy-start(f32[8,48,8,128]{3,2,1,0:T(8,128)} %param.6) | copy-start | bytes 4718596
  42.7 56.4 %copy-start.3 = (f32[47,8,128]{2,1,0:T(8,128)S(1)}, f32[47,8,128]{2,1,0:T(8,128)}, u32[]{:S(2)}) copy-start(f32[47,8,128]{2,1,0:T(8,128)} %diff.1) | copy-start | bytes 577540
  42.7 56.4 %copy-start.5 = (s32[8,128]{1,0:T(8,128)S(1)}, s32[8,128]{1,0:T(8,128)}, u32[]{:S(2)}) copy-start(s32[8,128]{1,0:T(8,128)} %wet.5) | copy-start | bytes 12292
  77.2 30.9 %all-to-all-start.1 = ((f32[32,8,128]{2,1,0:T(8,128)}), f32[32,8,128]{2,1,0:T(8,128)S(1)}, u32[]{:S(2)}, u32[]{:S(2)}) async-start(f32[32,8,128]{2,1,0:T(8,128)} %broadcast_in_dim.2), calls=%async_computation.1 | async-start | bytes 262144 | tf_op jit(solution)/shard_map/all_to_all | solution.py:600

commit v2 on v1

v2 whole, which is shorter than its diff:
```python
import functools

import jax
import jax.numpy as jnp
import numpy as np
from jax import lax
from jax.experimental import pallas as pl
from jax.experimental.pallas import tpu as pltpu
from jax.sharding import PartitionSpec as P

ITERS = 3
K = 48
HORIZONTAL_RATE = 0.2
FLUX_SCALE = 0.02
FACE_SCALE = 0.25
F32 = jnp.float32

PAIR_UV = 0
PAIR_VISC = 48
PAIR_SURF = 72
ROW_X = 73
LAT_TILES = 79
ROW_TILES = 36
PL_U, PL_V, PL_VISC, PL_WET, PL_STO, PL_SUR = 0, 48, 96, 143, 144, 145
PLANES = 146
LON_WIDE = 10
LON_TILES = LON_WIDE + 3
CHUNK = 8


def sub_iota():
    return lax.broadcasted_iota(jnp.int32, (8, 128), 0)


def lane_iota():
    return lax.broadcasted_iota(jnp.int32, (8, 128), 1)


def lroll(x, shift):
    return pltpu.roll(x, shift, 1)


def sroll(x, shift):
    return pltpu.roll(x, shift, 0)


def flip_lanes(x):
    return jnp.take_along_axis(x, 127 - lane_iota(), axis=1)


def flip_rows(x):
    sub = sub_iota()
    x = sroll(x, 4)
    x = jnp.where((sub & 2) == 0, sroll(x, 6), sroll(x, 2))
    return jnp.where((sub & 1) == 0, sroll(x, 7), sroll(x, 1))


def thickness_at(level):
    return 0.5 + level * (1.0 / 48.0)


def spacing_at(level):
    return 96.0 / jnp.full((8, 128), 49.0 + 2.0 * level, F32)


def depth_of(count):
    return 0.5 * count + count * (count - 1.0) * (1.0 / 96.0)


def pack_lat(
    flags, state_any, visc_any, wet_any, storage_any, surf_any, pay_b, pay_a, state, visc, flat, wet, sems,
):
    half = 48 * 8
    copies = [
        pltpu.make_async_copy(state_any.at[pl.ds(0, half)], state.at[pl.ds(0, half)], sems.at[0]),
        pltpu.make_async_copy(state_any.at[pl.ds(half, half)], state.at[pl.ds(half, half)], sems.at[1]),
        pltpu.make_async_copy(visc_any, visc, sems.at[2]),
        pltpu.make_async_copy(wet_any, wet, sems.at[3]),
        pltpu.make_async_copy(storage_any, flat.at[1], sems.at[4]),
        pltpu.make_async_copy(surf_any, flat.at[2], sems.at[5]),
    ]
    for copy in copies:
        copy.start()
    for copy in copies:
        copy.wait()
    flat[0] = wet[...].astype(F32)
    odd = flags[0]
    sub = sub_iota()
    keep = (sub < 4).astype(jnp.int32) == odd
    wet_now = flat[0]
    least = jnp.broadcast_to(jnp.minimum(wet_now[3:4], wet_now[4:5]), (8, 128))

    def pairs():
        for k in range(48):
            yield k, state[k * 8 : k * 8 + 8, :], state[(k + 48) * 8 : (k + 48) * 8 + 8, :], -1.0
        for m in range(23):
            yield PAIR_VISC + m, visc[2 * m], visc[2 * m + 1], 1.0
        yield PAIR_VISC + 23, visc[46], wet_now, 1.0
        yield PAIR_SURF, flat[1], flat[2], 1.0

    def crossed():
        for m in range(6):
            start = (48 + 8 * m) * 8
            row3 = state[pl.ds(start + 3, 8, stride=8), :]
            row4 = state[pl.ds(start + 4, 8, stride=8), :]
            level = (sub + 8 * m).astype(F32)
            yield ROW_X + m, jnp.where(level < least, row3 - row4, 0.0)

    @pl.when(flags[1] == 0)
    def _():
        for tile, first, second, _ in pairs():
            rolled = sroll(second, 4)
            pay_a[tile] = jnp.where(keep, first, rolled)
            pay_b[tile] = jnp.where(keep, rolled, first)
        for tile, diff in crossed():
            pay_a[tile] = diff
            pay_b[tile] = diff

    @pl.when(flags[1] == 1)
    def _():
        for tile, first, second, sign in pairs():
            rolled = sroll(second, 4)
            pay_a[tile] = jnp.where(keep, first, rolled)
            turned = flip_rows(flip_lanes(jnp.where(keep, rolled, first)))
            pay_b[tile] = -turned if sign < 0 else turned
        for tile, diff in crossed():
            pay_a[tile] = diff
            pay_b[tile] = -flip_lanes(diff)


def pack_tracers(flags, state_any, pay_b, pay_a, far, near, tracer, sems):
    half = 144 * 8
    copies = [
        pltpu.make_async_copy(
            state_any.at[pl.ds((96 + 144 * i) * 8, half)], tracer.at[pl.ds(i * half, half)], sems.at[i]
        )
        for i in range(2)
    ]
    for copy in copies:
        copy.start()
    for copy in copies:
        copy.wait()
    odd = flags[0]
    odd_lon = flags[2]
    lane = lane_iota()

    def rows_of(t):
        start = 8 * t * 8
        return tracer[pl.ds(start, 8, stride=8), :], tracer[pl.ds(start + 7, 8, stride=8), :]

    for t in range(ROW_TILES):
        row0, row7 = rows_of(t)
        pay_a[t] = jnp.where(odd == 1, row0, row7)
        pay_b[t] = jnp.where(odd == 1, row7, row0)

    @pl.when(flags[1] == 1)
    def _():
        for t in range(ROW_TILES):
            pay_b[t] = flip_lanes(rows_of(t)[1])

    def scalar(n):
        return tracer[n * 8 : n * 8 + 8, :]

    for tile in range(3):
        planes = [functools.partial(scalar, n) for n in range(128 * tile, min(128 * tile + 128, 288))]
        east, west = pack_columns(lane, planes, 1)
        far[tile] = jnp.where(odd_lon == 1, east, west)
        near[tile] = jnp.where(odd_lon == 1, west, east)


def pack_columns(lane, planes, width):
    east = jnp.zeros((8, 128), F32)
    west = jnp.zeros((8, 128), F32)
    slots = 128 // width
    slot_of = lane // width
    for j, load in enumerate(planes):
        x = load()
        x = lroll(x, j * width) if j else x
        west = jnp.where(slot_of == j, x, west)
        east = jnp.where(slot_of == (j - 1) % slots, x, east)
    return east, west


def lon_planes(state, visc, flat, rows, row_x):
    def plane(n):
        if n < 96:
            return state[n * 8 : n * 8 + 8, :]
        if n < 143:
            return visc[n - 96]
        if n < 146:
            return flat[n - 143]
        if n < 292:
            return rows[n - 146]
        return row_x[n - 292]

    lane = lane_iota()
    for tile in range(LON_WIDE):
        planes = [functools.partial(plane, n) for n in range(32 * tile, min(32 * tile + 32, 298))]
        yield tile, pack_columns(lane, planes, 4)


def pack_lon(
    flags, state, visc, flat, rec_b, rec_a, far_tracers, near_tracers, rows, row_x, far, near
):
    odd = flags[0]
    odd_lon = flags[2]
    sub = sub_iota()
    keep = (sub < 4).astype(jnp.int32) != odd

    def unpair(tile):
        a, b = rec_a[tile], rec_b[tile]
        return jnp.where(keep, a, b), sroll(jnp.where(keep, b, a), 4)

    for k in range(48):
        first, second = unpair(k)
        rows[PL_U + k] = first
        rows[PL_V + k] = second
    for m in range(24):
        first, second = unpair(PAIR_VISC + m)
        rows[PL_VISC + 2 * m] = first
        rows[PL_VISC + 2 * m + 1] = second
    first, second = unpair(PAIR_SURF)
    rows[PL_STO] = first
    rows[PL_SUR] = second
    for m in range(6):
        row_x[m] = jnp.where(odd == 1, rec_b[ROW_X + m], rec_a[ROW_X + m])
    for tile, (east, west) in lon_planes(state, visc, flat, rows, row_x):
        far[tile] = jnp.where(odd_lon == 1, east, west)
        near[tile] = jnp.where(odd_lon == 1, west, east)
    for tile in range(3):
        far[LON_WIDE + tile] = far_tracers[tile]
        near[LON_WIDE + tile] = near_tracers[tile]


def momentum(
    flags, state, visc, flat, rows, row_x, far, near,
    mixed, zed, moments,
    gain, done, planes2, xs,
):
    odd_lon = flags[2]
    top = flags[1] == 1
    lane = lane_iota()
    sub = sub_iota()
    slot_of = lane // 4
    valid = jnp.logical_or(lane < 4, lane >= 124)

    def strip_at(tile, j):
        a, b = far[tile], near[tile]
        mine = (slot_of == j).astype(jnp.int32) == odd_lon
        return lroll(jnp.where(mine, a, b), (128 - 4 * j) % 128)

    def strip(n):
        return strip_at(n // 32, n % 32)

    def strip_in(chunk, first, i):
        n = first + CHUNK * chunk + i
        return strip_at(n // 32, n % 32)

    for m in range(6):
        xs[m] = strip(m + 292)

    def four(n, own, mask):
        out = [own, rows[n], strip(n), strip(n + 146)]
        if mask:
            out[2] = jnp.where(valid, out[2], 0.0)
            out[3] = jnp.where(valid, out[3], 0.0)
        return out

    def east(q):
        return [
            lroll(jnp.where(lane == 0, q[2], q[0]), 127),
            lroll(jnp.where(lane == 0, q[3], q[1]), 127),
            lroll(jnp.where(lane == 0, q[0], q[2]), 127),
            lroll(jnp.where(lane == 0, q[1], q[3]), 127),
        ]

    def west(q):
        return [
            lroll(jnp.where(lane == 127, q[2], q[0]), 1),
            lroll(jnp.where(lane == 127, q[3], q[1]), 1),
            lroll(jnp.where(lane == 127, q[0], q[2]), 1),
            lroll(jnp.where(lane == 127, q[1], q[3]), 1),
        ]

    def north(q):
        return [
            sroll(jnp.where(sub == 0, q[1], q[0]), 7),
            sroll(jnp.where(sub == 0, q[0], q[1]), 7),
            sroll(jnp.where(sub == 0, q[3], q[2]), 7),
            sroll(jnp.where(sub == 0, q[2], q[3]), 7),
        ]

    def south(q):
        return [
            sroll(jnp.where(sub == 7, q[1], q[0]), 1),
            sroll(jnp.where(sub == 7, q[0], q[1]), 1),
            sroll(jnp.where(sub == 7, q[3], q[2]), 1),
            sroll(jnp.where(sub == 7, q[2], q[3]), 1),
        ]

    def each(fn, *lists):
        return [fn(*items) for items in zip(*lists)]

    level_count = four(PL_WET, flat[0], True)
    counts = [each(jnp.minimum, level_count, shift(level_count)) for shift in (east, west, north, south)]
    for i, c in enumerate(counts):
        for j in range(4):
            planes2[4 * i + j] = c[j]
    for j in range(4):
        planes2[16 + j] = level_count[j]
    ghost = jnp.logical_and(top, sub < 4)
    planes2[20] = counts[0][0]
    planes2[21] = jnp.where(ghost, counts[1][1], counts[0][1])
    planes2[22] = counts[0][2]
    planes2[23] = jnp.where(ghost, counts[1][3], counts[0][3])
    planes2[24] = counts[2][0]
    planes2[25] = jnp.where(ghost, counts[3][1], counts[2][1])
    planes2[26] = counts[2][2]
    planes2[27] = jnp.where(ghost, counts[3][3], counts[2][3])

    zero = jnp.zeros((8, 128), F32)
    cross = jnp.logical_and(top, sub == 3)

    def blend(base, chunk, i, open_east, open_north):
        n = base + CHUNK * chunk + i
        q = [state[pl.ds(n * 8, 8), :], rows[n], strip_in(chunk, base, i), strip_in(chunk, base + 146, i)]
        over_east = each(lambda o, a, b: jnp.where(o, a - b, 0.0), open_east, east(q), q)
        over_north = each(lambda o, a, b: jnp.where(o, a - b, 0.0), open_north, north(q), q)
        if base == PL_V:
            for j, source in ((1, row_x), (3, xs)):
                extra = jnp.broadcast_to(source[chunk, i : i + 1, :], (8, 128))
                over_north[j] = jnp.where(cross, extra, over_north[j])
        return each(
            lambda c, a, b, d, e: c + HORIZONTAL_RATE * (a - b + d - e),
            q, over_east, west(over_east), over_north, south(over_north),
        )

    def forward(chunk, carry):
        above, prev_gain, prev_u, prev_v = carry
        for i in range(CHUNK):
            k = CHUNK * chunk + i
            kf = k.astype(F32)
            thick = thickness_at(kf)
            space = spacing_at(kf)
            coefficient = [
                visc[jnp.minimum(k, 46)],
                rows[PL_VISC + k],
                strip_in(chunk, PL_VISC, i),
                strip_in(chunk, PL_VISC + 146, i),
            ]
            below = [jnp.where(kf + 1.0 < planes2[16 + j], coefficient[j] * space, 0.0) for j in range(4)]
            open_east = [kf < planes2[j] for j in range(4)]
            open_north = [kf < planes2[8 + j] for j in range(4)]
            u = blend(PL_U, chunk, i, open_east, open_north)
            v = blend(PL_V, chunk, i, open_east, open_north)
            new_gain, new_u, new_v = [], [], []
            for j in range(4):
                inverse = 1.0 / (thick + above[j] + below[j] - above[j] * prev_gain[j])
                new_gain.append(below[j] * inverse)
                new_u.append((thick * u[j] + above[j] * prev_u[j]) * inverse)
                new_v.append((thick * v[j] + above[j] * prev_v[j]) * inverse)
                gain[chunk, i, j] = new_gain[j]
                done[0, chunk, i, j] = new_u[j]
                done[1, chunk, i, j] = new_v[j]
            above, prev_gain, prev_u, prev_v = below, new_gain, new_u, new_v
        return above, prev_gain, prev_u, prev_v

    zeros = [zero] * 4
    lax.fori_loop(0, K // CHUNK, forward, (zeros, zeros, zeros, zeros))

    def backward(step, carry):
        chunk = K // CHUNK - 1 - step
        low_u, low_v, flux_u, flux_v = carry
        for i in reversed(range(CHUNK)):
            k = CHUNK * chunk + i
            kf = k.astype(F32)
            thick = thickness_at(kf)
            new_u, new_v, out_u, out_v = [], [], [], []
            for j in range(4):
                g = gain[chunk, i, j]
                x_u = done[0, chunk, i, j] + g * low_u[j]
                x_v = done[1, chunk, i, j] + g * low_v[j]
                new_u.append(x_u)
                new_v.append(x_v)
                out_u.append(flux_u[j] + jnp.where(kf < planes2[20 + j], thick * x_u, 0.0))
                out_v.append(flux_v[j] + jnp.where(kf < planes2[24 + j], thick * x_v, 0.0))
            mixed[pl.ds(k * 8, 8), :] = new_u[0]
            mixed[pl.ds((k + 48) * 8, 8), :] = new_v[0]
            low_u, low_v, flux_u, flux_v = new_u, new_v, out_u, out_v
        return low_u, low_v, flux_u, flux_v

    _, _, flux_u, flux_v = lax.fori_loop(0, K // CHUNK, backward, (zeros, zeros, zeros, zeros))

    last = jnp.logical_and(top, sub == 7)
    first_ghost = jnp.logical_and(top, sub == 0)
    flux_v = [
        jnp.where(last, 0.0, flux_v[0]),
        jnp.where(first_ghost, 0.0, flux_v[1]),
        jnp.where(last, 0.0, flux_v[2]),
        jnp.where(first_ghost, 0.0, flux_v[3]),
    ]
    plain = each(
        lambda a, b, c, d: a - b + c - d, flux_u, west(flux_u), flux_v, south(flux_v)
    )
    mirrored = each(
        lambda a, b, c, d: a - b + c - d, east(flux_u), flux_u, north(flux_v), flux_v
    )
    divergence = [
        plain[0],
        jnp.where(ghost, mirrored[1], plain[1]),
        plain[2],
        jnp.where(ghost, mirrored[3], plain[3]),
    ]
    sto = four(PL_STO, flat[1], True)
    old = four(PL_SUR, flat[2], True)
    faces = [[FACE_SCALE * depth_of(planes2[4 * i + j]) for j in range(4)] for i in range(4)]
    diagonal = [
        jnp.maximum(sto[j] + faces[0][j] + faces[1][j] + faces[2][j] + faces[3][j], 0.1) for j in range(4)
    ]
    ocean = [planes2[16 + j] > 0.0 for j in range(4)]
    start = [jnp.where(ocean[j], old[j], 0.0) for j in range(4)]
    around = [east(start), west(start), north(start), south(start)]
    inverse = [1.0 / diagonal[j] for j in range(4)]
    basis = []
    for j in range(4):
        forcing = jnp.where(ocean[j], sto[j] * old[j] - FLUX_SCALE * divergence[j], 0.0)
        image = sto[j] * start[j]
        for i in range(4):
            image = image + faces[i][j] * (start[j] - around[i][j])
        basis.append((forcing - image) / diagonal[j])
    z0 = basis

    def spread(z):
        nb = [east(z), west(z), north(z), south(z)]
        return [
            (faces[0][j] * nb[0][j] + faces[1][j] * nb[1][j] + faces[2][j] * nb[2][j] + faces[3][j] * nb[3][j])
            * inverse[j]
            for j in range(4)
        ]

    z1 = spread(z0)
    z2 = spread(z1)
    zed[0] = start[0]
    zed[1] = z0[0]
    zed[2] = z1[0]
    zed[3] = z2[0]
    weighted = [diagonal[0] * z[0] for z in (z0, z1, z2)]
    north_weight = jnp.where(last, 1.0, 2.0)
    edge = z2[0] * (
        2.0 * faces[0][0] * east(z2)[0] + north_weight * faces[2][0] * north(z2)[0]
    )
    products = [
        weighted[0] * z0[0],
        weighted[0] * z1[0],
        weighted[1] * z1[0],
        weighted[1] * z2[0],
        weighted[2] * z2[0],
        edge,
    ]
    tile = zero
    for i, product in enumerate(products):
        total = jnp.sum(jnp.sum(product, axis=0, keepdims=True), axis=1, keepdims=True)
        tile = jnp.where(sub == i, total, tile)
    for i in range(moments.shape[0]):
        moments[i] = tile


def tracers_down(flags, state, diff, flat, around, rec_b, rec_a, far, near, gain, done):
    odd = flags[0]
    odd_lon = flags[2]
    lane = lane_iota()
    sub = sub_iota()
    level_count = flat[0]
    zero = jnp.zeros((8, 128), F32)

    def forward(chunk, carry):
        above, prev_gain, prev = carry
        for i in range(CHUNK):
            k = CHUNK * chunk + i
            kf = k.astype(F32)
            thick = thickness_at(kf)
            coefficient = diff[jnp.minimum(k, 46)]
            below = jnp.where(kf + 1.0 < level_count, coefficient * spacing_at(kf), 0.0)
            inverse = 1.0 / (thick + above + below - above * prev_gain)
            new_gain = below * inverse
            gain[chunk, i] = new_gain
            open_face = [kf < around[face] for face in range(4)]
            new = []
            for f in range(6):
                first = f * 48 + CHUNK * chunk
                q = state[pl.ds((first + i) * 8, 8), :]
                row_a = rec_a[f * 6 + chunk, i : i + 1, :]
                row_b = rec_b[f * 6 + chunk, i : i + 1, :]
                row_n = jnp.broadcast_to(jnp.where(odd == 1, row_b, row_a), (8, 128))
                row_s = jnp.broadcast_to(jnp.where(odd == 1, row_a, row_b), (8, 128))
                tile, j = first // 128, first % 128 + i
                a, b = far[LON_WIDE + tile], near[LON_WIDE + tile]
                side = lroll(jnp.where((lane == j).astype(jnp.int32) == odd_lon, a, b), (128 - j) % 128)
                change = jnp.where(open_face[0], lroll(jnp.where(lane == 0, side, q), 127) - q, 0.0)
                change += jnp.where(open_face[1], lroll(jnp.where(lane == 127, side, q), 1) - q, 0.0)
                change += jnp.where(open_face[2], sroll(jnp.where(sub == 0, row_n, q), 7) - q, 0.0)
                change += jnp.where(open_face[3], sroll(jnp.where(sub == 7, row_s, q), 1) - q, 0.0)
                value = (thick * (q + HORIZONTAL_RATE * change) + above * prev[f]) * inverse
                done[f, chunk, i] = value
                new.append(value)
            above, prev_gain, prev = below, new_gain, new
        return above, prev_gain, prev

    lax.fori_loop(0, K // CHUNK, forward, (zero, zero, [zero] * 6))


def tracers_up(gain, done, mixed_in, after, out):
    del after
    out[0 : 96 * 8, :] = mixed_in[...]
    zero = jnp.zeros((8, 128), F32)

    def backward(step, low):
        chunk = K // CHUNK - 1 - step
        for i in reversed(range(CHUNK)):
            g = gain[chunk, i]
            low = [done[f, chunk, i] + g * low[f] for f in range(6)]
            for f in range(6):
                out[pl.ds((96 + f * 48 + CHUNK * chunk + i) * 8, 8), :] = low[f]
        return low

    lax.fori_loop(0, K // CHUNK, backward, [zero] * 6)


def combine(parts, after, out):
    del after
    total = parts[0]
    for i in range(1, parts.shape[0]):
        total = total + parts[i]
    for i in range(out.shape[0]):
        out[i] = total


def finish(parts, zed, surface):
    total = parts[0]
    for i in range(1, parts.shape[0]):
        total = total + parts[i]
    nu = [jnp.broadcast_to(total[i : i + 1, :], (8, 128)) for i in range(6)]

    def inner(p, q, shift):
        out = None
        for i, a in enumerate(p):
            for j, b in enumerate(q):
                term = a * b * nu[i + j + shift]
                out = term if out is None else out + term
        return out

    one = jnp.ones((8, 128), F32)
    scaled = [one]
    direction = [one]
    product = nu[0]
    move = [jnp.zeros((8, 128), F32)] * 3
    for iteration in range(ITERS):
        curvature = inner(direction, direction, 0) - inner(direction, direction, 1)
        alpha = product / curvature
        for i, d in enumerate(direction):
            move[i] = move[i] + alpha * d
        if iteration + 1 < ITERS:
            longer = scaled + [jnp.zeros((8, 128), F32)]
            for i, d in enumerate(direction):
                longer[i] = longer[i] - alpha * d
                longer[i + 1] = longer[i + 1] + alpha * d
            scaled = longer
            following = inner(scaled, scaled, 0)
            beta = following / product
            direction = [
                scaled[i] + (beta * direction[i] if i < len(direction) else 0.0) for i in range(len(scaled))
            ]
            product = following
    surface[...] = zed[0] + move[0] * zed[1] + move[1] * zed[2] + move[2] * zed[3]


VMEM_LIMIT = 24 * 1024 * 1024
FIRST_LIMIT = 60 * 1024 * 1024
SMEM = pl.BlockSpec(memory_space=pltpu.SMEM)
VMEM = pl.BlockSpec(memory_space=pltpu.VMEM)
ANY = pl.BlockSpec(memory_space=pl.ANY)


def kernel(body, ins, outs, scratch=(), flops=0, nbytes=0, limit=VMEM_LIMIT):
    return pl.pallas_call(
        body,
        out_shape=[jax.ShapeDtypeStruct(s, F32) for s in outs],
        in_specs=ins,
        out_specs=[VMEM] * len(outs),
        scratch_shapes=[pltpu.VMEM(s, F32) if isinstance(s, tuple) else s for s in scratch],
        compiler_params=pltpu.CompilerParams(vmem_limit_bytes=limit),
        cost_estimate=pl.CostEstimate(flops=flops, bytes_accessed=nbytes, transcendentals=0),
    )


def lat_pairs(lat, lon):
    first, second = [], []
    for l in range(lat):
        for p in range(lon):
            here = l * lon + p
            first.append((here, (l ^ 1) * lon + p))
            if l == lat - 1:
                second.append((here, l * lon + lon - 1 - p))
            elif l % 2 == 1:
                second.append((here, here + lon))
            elif l > 0:
                second.append((here, here - lon))
    return first, second


def lon_pairs(lon):
    far, near = [], []
    for p in range(lon):
        step = 1 if p % 2 else -1
        far.append((p, (p + step) % lon))
        near.append((p, p ^ 1))
    return far, near


def make_local(mesh_shape):
    lat, lon = mesh_shape["lat"], mesh_shape["lon"]
    pairs_a, pairs_b = lat_pairs(lat, lon)
    pairs_far, pairs_near = lon_pairs(lon)
    both = ("lat", "lon")
    stages = reduction_stages(lat, lon)

    def local(ocean_state, viscosity, diffusivity, wet_levels, storage, surface_old):
        band = lax.axis_index("lat")
        place = lax.axis_index("lon")
        flags = jnp.stack([band % 2, (band == lat - 1).astype(jnp.int32), place % 2]).astype(jnp.int32)
        state = ocean_state.reshape(8 * K * 8, 128)
        pay_b, pay_a, uv, visc, flat = kernel(
            pack_lat,
            [SMEM] + [ANY] * 5,
            [(LAT_TILES, 8, 128)] * 2 + [(96 * 8, 128), (47, 8, 128), (3, 8, 128)],
            scratch=[pltpu.VMEM((8, 128), jnp.int32), pltpu.SemaphoreType.DMA((6,))],
            limit=FIRST_LIMIT,
        )(flags, state, viscosity, wet_levels, storage, surface_old)
        own = (uv, visc, flat)
        rec_b = lax.ppermute(pay_b, both, pairs_b)
        rec_a = lax.ppermute(pay_a, both, pairs_a)
        row_b, row_a, far_tracers, near_tracers, tracer = kernel(
            pack_tracers,
            [SMEM, ANY],
            [(ROW_TILES, 8, 128)] * 2 + [(3, 8, 128)] * 2 + [(288 * 8, 128)],
            scratch=[pltpu.SemaphoreType.DMA((2,))],
            flops=1_000_000,
            nbytes=2_000_000,
        )(flags, state)
        rec_row_b = lax.ppermute(row_b, both, pairs_b)
        rec_row_a = lax.ppermute(row_a, both, pairs_a)
        rows, row_x, pay_far, pay_near = kernel(
            pack_lon,
            [SMEM] + [VMEM] * 7,
            [(PLANES, 8, 128), (6, 8, 128), (LON_TILES, 8, 128), (LON_TILES, 8, 128)],
        )(flags, *own, rec_b, rec_a, far_tracers, near_tracers)
        rec_far = lax.ppermute(pay_far, "lon", pairs_far)
        rec_near = lax.ppermute(pay_near, "lon", pairs_near)
        chunked = (K // CHUNK, CHUNK)
        mixed, zed, around, moments = kernel(
            momentum_entry,
            [SMEM] + [VMEM] * 7 + [ANY] * 2,
            [(2 * K * 8, 128), (4, 8, 128), (4, 8, 128), (stages[0][1], 8, 128)],
            scratch=[(*chunked, 4, 8, 128), (2, *chunked, 4, 8, 128), (28, 8, 128), (6, 8, 128)],
        )(flags, *own, rows, row_x, rec_far, rec_near, rec_row_b, rec_row_a)
        (first_groups, _), (second_groups, second_size) = stages
        parts = lax.all_to_all(moments, both, 0, 0, axis_index_groups=first_groups, tiled=True)
        gain, done = kernel(
            tracers_down,
            [SMEM] + [VMEM] * 8,
            [(*chunked, 8, 128), (6, *chunked, 8, 128)],
            flops=10_000_000,
            nbytes=6_000_000,
        )(flags, tracer, diffusivity, flat, around, rec_row_b, rec_row_a, rec_far, rec_near)
        (parts,) = kernel(combine, [VMEM, ANY], [(second_size, 8, 128)])(parts, gain)
        sent = parts
        parts = lax.all_to_all(parts, both, 0, 0, axis_index_groups=second_groups, tiled=True)
        (mixed,) = kernel(
            tracers_up, [VMEM] * 3 + [ANY], [(8 * K * 8, 128)], flops=10_000_000, nbytes=6_000_000
        )(gain, done, mixed, sent)
        (surface,) = kernel(finish, [VMEM] * 2, [(8, 128)])(parts, zed)
        return mixed.reshape(8, K, 8, 128), surface

    return local


def momentum_entry(*refs):
    inputs, outputs, scratch = refs[:8], refs[10:14], refs[14:]
    mixed, zed, around, moments = outputs
    momentum(*inputs, mixed, zed, moments, *scratch)
    counts = scratch[2]
    for face in range(4):
        around[face] = counts[4 * face]


def reduction_stages(lat, lon):
    index = np.arange(lat * lon)
    if lat == 32 and lon == 16:
        grid = index.reshape(8, 4, 4, 2, 2)
        along_z = grid.transpose(1, 2, 4, 3, 0).reshape(32, 16)
        rest = grid.transpose(0, 3, 1, 2, 4).reshape(16, 32)
    else:
        grid = index.reshape(lat, lon)
        along_z, rest = grid.T, grid
    return [(g.tolist(), g.shape[1]) for g in (along_z, rest)]


def solution(mesh):
    placed = (
        P(None, None, "lat", "lon"),
        P(None, "lat", "lon"),
        P(None, "lat", "lon"),
        P("lat", "lon"),
        P("lat", "lon"),
        P("lat", "lon"),
    )
    return jax.shard_map(
        make_local(dict(mesh.shape)),
        mesh=mesh,
        in_specs=placed,
        out_specs=(P(None, None, "lat", "lon"), P("lat", "lon")),
        check_vma=False,
    )
```

time: 109 us -> 92.8 us (0.85)
  blocking collectives: 24.9 us -> 0 us
  waiting for transfers between devices: 6.15 us -> 15 us
  starting transfers between devices: 51.1 us -> 58.3 us
  local copies, waits for them, and re-layouts: 5.09 us -> 0.95 us
  Pallas kernels: 20.7 us -> 16.7 us
    all_to_all x1 -> x0, blocking collectives: 24.9 us -> none  [local(): lax.all_to_all(parts, both, 0, 0, axis_index_groups=groups, tiled=True)]
    all_to_all x1 -> x2, waiting for transfers between devices: 0.01 us -> 14.1 us  [the longest x1 7.71 us: local(): lax.all_to_all(moments, both, 0, 0, axis_index_groups=first_groups, tiled...]
    ppermute x0 -> x2, starting transfers between devices: none -> 6.29 us  [the longest x1 5.62 us: local(): rec_row_a = lax.ppermute(row_a, both, pairs_a)]
    ppermute x1, waiting for transfers between devices: 5.29 us -> 0.01 us  [local(): rec_a = lax.ppermute(pay_a, both, pairs_a)]
    ppermute x1, starting transfers between devices: 21.3 us -> 16.9 us  [local(): rec_far = lax.ppermute(pay_far, 'lon', pairs_far)]
    pallas_call x5 -> x8, Pallas kernels: 20.7 us -> 16.7 us  [the longest x1 5.95 us: local(): kernel(momentum_entry, [SMEM] + [VMEM] * 7 + [ANY] * 2, [(2 * K * 8, 128)...]
    unnamed x16 -> x12, local copies, waits for them, and re-layouts: 4.4 us -> 0.95 us
    all_to_all x1 -> x2, starting transfers between devices: 21.8 us -> 25 us  [the longest x1 16.8 us: local(): lax.all_to_all(moments, both, 0, 0, axis_index_groups=first_groups, tiled...]
  transfers between devices with their start and end apart: 5 -> 8, of which waited for: 2 -> 3; matrix products, arithmetic and copies ran while one was open for 0% -> 0% of each run, Pallas kernels for 8% -> 7%
where the time goes in v2:
time: 92.8 us; the launch traced here: 92.3 us
  starting transfers between devices  58.3 us (63%)
  Pallas kernels  16.7 us (18%)
  waiting for transfers between devices  15 us (16%)
  local copies, waits for them, and re-layouts  0.95 us (1%)
    ppermute x1, starting transfers between devices, local(): rec_far = lax.ppermute(pay_far, 'lon', pairs_far)  16.9 us
    all_to_all x1, starting transfers between devices, local(): lax.all_to_all(moments, both, 0, 0, axis_index_groups=first_groups, tiled...  16.8 us
    all_to_all x1, starting transfers between devices, local(): lax.all_to_all(parts, both, 0, 0, axis_index_groups=second_groups, tiled=...  8.22 us
    all_to_all x1, waiting for transfers between devices, local(): lax.all_to_all(moments, both, 0, 0, axis_index_groups=first_groups, tiled...  7.71 us
    all_to_all x1, waiting for transfers between devices, local(): lax.all_to_all(parts, both, 0, 0, axis_index_groups=second_groups, tiled=...  6.4 us
    ppermute x1, starting transfers between devices, local(): rec_a = lax.ppermute(pay_a, both, pairs_a)  6.39 us
    pallas_call x1, Pallas kernels, local(): kernel(momentum_entry, [SMEM] + [VMEM] * 7 + [ANY] * 2, [(2 * K * 8, 128)...  5.95 us
    ppermute x1, starting transfers between devices, local(): rec_row_a = lax.ppermute(row_a, both, pairs_a)  5.62 us
  transfers between devices with their start and end apart: 8, of which 3 were waited for; matrix products, arithmetic and copies ran while one was open for 0% of the time, Pallas kernels for 7%

profile of v2, /device:TPU:1, one launch (start us, length us, event | category | flops | bytes accessed | tf_op | source)
XLA Modules:
  0.0 92.3 jit_solution(16582624358522139300)
XLA Ops:
  0.6 0.0 copy-start
  0.7 0.6 pad_add_fusion.flags.refs_0_
  1.3 3.0 %shard_map.78 = (f32[79,8,128]{2,1,0:T(8,128)}, f32[79,8,128]{2,1,0:T(8,128)}, f32[768,128]{1,0:T(8,128)}, f32[47,8,128]{2,1,0:T(8,128)}, f32[3,8,128]{2,1,0:T(8,128)}) custom-call(s32[3]{0:T(128)} %pad_add_fusion.flags.refs_0_, f32[3072,128]{1,0:T(8,128)} %bitcast.5, f32[47,8,128]{2,1,0:T(8,128)} %visc_any.1, s32[8,128]{1,0:T(8,128)} %wet_any.1, ...), custom_call_target="tpu_custom_call" | custom-call | tf_op jit(solution)/shard_map/pallas_call | solution.py:632
  4.3 0.0 copy-start.1
  4.3 0.8 collective-permute-start
  5.1 6.4 %collective-permute-start.1 = (f32[79,8,128]{2,1,0:T(8,128)}, f32[79,8,128]{2,1,0:T(8,128)S(1)}, u32[]{:S(2)}, u32[]{:S(2)}) collective-permute-start(f32[79,8,128]{2,1,0:T(8,128)} %get-tuple-element.27), channel_id=1, source_target_pairs={{0,16},{1,17},{2,18},{3,19},{4,20},{5,21},{6,22},{7,23},{8,24},{9,... | collective-permute-start | bytes 970760 | tf_op jit(solution)/shard_map/ppermute | solution.py:641
  11.5 1.2 %shard_map.77 = (f32[36,8,128]{2,1,0:T(8,128)S(1)}, f32[36,8,128]{2,1,0:T(8,128)S(1)}, f32[3,8,128]{2,1,0:T(8,128)S(1)}, f32[3,8,128]{2,1,0:T(8,128)S(1)}, f32[2304,128]{1,0:T(8,128)S(1)}) custom-call(s32[3]{0:T(128)S(1)} %copy-done.5, f32[3072,128]{1,0:T(8,128)S(1)} %bitcast.6), custom_call_target="tpu_custom_call" | custom-call | flops 1000000 | bytes 2000000 | tf_op jit(solution)/shard_map/pallas_call | solution.py:642
  12.8 0.7 collective-permute-start.4
  13.4 5.6 %collective-permute-start.5 = (f32[36,8,128]{2,1,0:T(8,128)S(1)}, f32[36,8,128]{2,1,0:T(8,128)S(1)}, u32[]{:S(2)}, u32[]{:S(2)}) collective-permute-start(f32[36,8,128]{2,1,0:T(8,128)S(1)} %get-tuple-element.35), channel_id=1, source_target_pairs={{0,16},{1,17},{2,18},{3,19},{4,20},{5,21},{6,22},{7,23},{8,24},{9,... | collective-permute-start | bytes 442376 | tf_op jit(solution)/shard_map/ppermute | solution.py:651
  19.1 0.9 shard_map.79
  20.0 16.9 %collective-permute-start.2 = (f32[13,8,128]{2,1,0:T(8,128)S(1)}, f32[13,8,128]{2,1,0:T(8,128)S(1)}, u32[]{:S(2)}, u32[]{:S(2)}) collective-permute-start(f32[13,8,128]{2,1,0:T(8,128)S(1)} %get-tuple-element.32), channel_id=1, source_target_pairs={{0,15},{1,2},{2,1},{3,4},{4,3},{5,6},{6,5},{7,8},{8,7},{9,10},{10,... | collective-permute-start | bytes 159752 | tf_op jit(solution)/shard_map/ppermute | solution.py:657
  37.0 2.9 %collective-permute-start.3 = (f32[13,8,128]{2,1,0:T(8,128)S(1)}, f32[13,8,128]{2,1,0:T(8,128)S(1)}, u32[]{:S(2)}, u32[]{:S(2)}) collective-permute-start(f32[13,8,128]{2,1,0:T(8,128)S(1)} %get-tuple-element.33), channel_id=1, source_target_pairs={{0,1},{1,0},{2,3},{3,2},{4,5},{5,4},{6,7},{7,6},{8,9},{9,8},{10,11... | collective-permute-start | bytes 159752 | tf_op jit(solution)/shard_map/ppermute | solution.py:658
  39.9 0.8 collective-permute-done.3.refs_7_.near
  40.8 5.9 %shard_map.80 = (f32[768,128]{1,0:T(8,128)S(1)}, f32[4,8,128]{2,1,0:T(8,128)S(1)}, f32[4,8,128]{2,1,0:T(8,128)S(1)}, f32[16,8,128]{2,1,0:T(8,128)}) custom-call(s32[3]{0:T(128)S(1)} %copy-done.5, f32[768,128]{1,0:T(8,128)S(1)} %copy-done.1, f32[47,8,128]{2,1,0:T(8,128)S(1)} %copy-done.2, f32[3,8,128]{2,1,0:T(8,128)S(1)} %copy-done.4, ...), custom_call_target="tpu_custom_call" | custom-call | tf_op jit(solution)/shard_map/pallas_call | solution.py:660
  46.7 16.8 %all-to-all-start = ((f32[16,8,128]{2,1,0:T(8,128)}), f32[16,8,128]{2,1,0:T(8,128)S(1)}, u32[]{:S(2)}, u32[]{:S(2)}) async-start(f32[16,8,128]{2,1,0:T(8,128)} %get-tuple-element.40), calls=%async_computation | async-start | bytes 131072 | tf_op jit(solution)/shard_map/all_to_all | solution.py:667
  63.5 0.0 copy-start.3
  63.5 0.9 copy-done.3
  64.4 2.9 %shard_map.81 = (f32[6,8,8,128]{3,2,1,0:T(8,128)S(1)}, f32[6,6,8,8,128]{4,3,2,1,0:T(8,128)S(1)}) custom-call(s32[3]{0:T(128)S(1)} %copy-done.5, f32[2304,128]{1,0:T(8,128)S(1)} %get-tuple-element.22.state, f32[47,8,128]{2,1,0:T(8,128)S(1)} %copy-done.3, f32[3,8,128]{2,1,0:T(8,128)S(1)} %copy-done.4, f32[4,8,128]{2,1,0:T(8,128)S(1)} %get-tuple-element.36.around, ...), custom_call_target="tpu_custom_call" | custom-call | flops 10000000 | bytes 6000000 | tf_op jit(solution)/shard_map/pallas_call | solution.py:668
  67.3 7.7 %all-to-all-done.parts = f32[16,8,128]{2,1,0:T(8,128)S(1)} async-done(((f32[16,8,128]{2,1,0:T(8,128)}), f32[16,8,128]{2,1,0:T(8,128)S(1)}, u32[]{:S(2)}, u32[]{:S(2)}) %all-to-all-start) | async-done | bytes 65568 | tf_op jit(solution)/shard_map/all_to_all | solution.py:667
  75.0 0.7 shard_map.82.after
  75.7 8.2 %all-to-all-start.1 = ((f32[32,8,128]{2,1,0:T(8,128)}), f32[32,8,128]{2,1,0:T(8,128)S(1)}, u32[]{:S(2)}, u32[]{:S(2)}) async-start(f32[32,8,128]{2,1,0:T(8,128)} %shard_map.82.after), calls=%async_computation.1 | async-start | bytes 262144 | tf_op jit(solution)/shard_map/all_to_all | solution.py:677
  83.9 1.3 %shard_map.83 = f32[3072,128]{1,0:T(8,128)} custom-call(f32[6,8,8,128]{3,2,1,0:T(8,128)S(1)} %get-tuple-element.37.after.gain, f32[6,6,8,8,128]{4,3,2,1,0:T(8,128)S(1)} %get-tuple-element.38.done, f32[768,128]{1,0:T(8,128)S(1)} %get-tuple-element.39.mixed_in, f32[32,8,128]{2,1,0:T(8,128)} %shard_map.82.after), custom_call_target="tpu_custom_call" | custom-call | flops 10000000 | bytes 6000000 | tf_op jit(solution)/shard_map/pallas_call | solution.py:678
  85.2 6.4 %all-to-all-done.1.parts = f32[32,8,128]{2,1,0:T(8,128)S(1)} async-done(((f32[32,8,128]{2,1,0:T(8,128)}), f32[32,8,128]{2,1,0:T(8,128)S(1)}, u32[]{:S(2)}, u32[]{:S(2)}) %all-to-all-start.1) | async-done | bytes 131104 | tf_op jit(solution)/shard_map/all_to_all | solution.py:677
  91.6 0.7 shard_map.84
  (13 shorter events, 0.0 us)
Async XLA Ops:
  0.6 10.9 %copy-start = (f32[8,48,8,128]{3,2,1,0:T(8,128)S(1)}, f32[8,48,8,128]{3,2,1,0:T(8,128)}, u32[]{:S(2)}) copy-start(f32[8,48,8,128]{3,2,1,0:T(8,128)} %param.6) | copy-start | bytes 4718596
  1.3 10.3 %copy-start.5 = (s32[3]{0:T(128)S(1)}, s32[3]{0:T(128)}, u32[]{:S(2)}) copy-start(s32[3]{0:T(128)} %pad_add_fusion.flags.refs_0_) | copy-start | bytes 40
  4.3 14.8 %copy-start.1 = (f32[768,128]{1,0:T(8,128)S(1)}, f32[768,128]{1,0:T(8,128)}, u32[]{:S(2)}) copy-start(f32[768,128]{1,0:T(8,128)} %get-tuple-element.24.state.refs_1_) | copy-start | bytes 1179652
  4.3 14.8 %copy-start.2 = (f32[47,8,128]{2,1,0:T(8,128)S(1)}, f32[47,8,128]{2,1,0:T(8,128)}, u32[]{:S(2)}) copy-start(f32[47,8,128]{2,1,0:T(8,128)} %get-tuple-element.25.visc.refs_2_) | copy-start | bytes 577540
  4.3 14.8 %copy-start.4 = (f32[3,8,128]{2,1,0:T(8,128)S(1)}, f32[3,8,128]{2,1,0:T(8,128)}, u32[]{:S(2)}) copy-start(f32[3,8,128]{2,1,0:T(8,128)} %get-tuple-element.23.flat.refs_3_) | copy-start | bytes 36868
  4.3 14.8 %collective-permute-start = (f32[79,8,128]{2,1,0:T(8,128)}, f32[79,8,128]{2,1,0:T(8,128)S(1)}, u32[]{:S(2)}, u32[]{:S(2)}) collective-permute-start(f32[79,8,128]{2,1,0:T(8,128)} %get-tuple-element.26), channel_id=1, source_target_pairs={{16,32},{17,33},{18,34},{19,35},{20,36},{21,37},{22,38},{23,39},{2... | collective-permute-start | bytes 970760 | tf_op jit(solution)/shard_map/ppermute | solution.py:640
  5.1 14.0 %collective-permute-start.1 = (f32[79,8,128]{2,1,0:T(8,128)}, f32[79,8,128]{2,1,0:T(8,128)S(1)}, u32[]{:S(2)}, u32[]{:S(2)}) collective-permute-start(f32[79,8,128]{2,1,0:T(8,128)} %get-tuple-element.27), channel_id=1, source_target_pairs={{0,16},{1,17},{2,18},{3,19},{4,20},{5,21},{6,22},{7,23},{8,24},{9,... | collective-permute-start | bytes 970760 | tf_op jit(solution)/shard_map/ppermute | solution.py:641
  12.8 27.1 %collective-permute-start.4 = (f32[36,8,128]{2,1,0:T(8,128)S(1)}, f32[36,8,128]{2,1,0:T(8,128)S(1)}, u32[]{:S(2)}, u32[]{:S(2)}) collective-permute-start(f32[36,8,128]{2,1,0:T(8,128)S(1)} %get-tuple-element.34), channel_id=1, source_target_pairs={{16,32},{17,33},{18,34},{19,35},{20,36},{21,37},{22,38},{23,39},{2... | collective-permute-start | bytes 442376 | tf_op jit(solution)/shard_map/ppermute | solution.py:650
  13.4 26.5 %collective-permute-start.5 = (f32[36,8,128]{2,1,0:T(8,128)S(1)}, f32[36,8,128]{2,1,0:T(8,128)S(1)}, u32[]{:S(2)}, u32[]{:S(2)}) collective-permute-start(f32[36,8,128]{2,1,0:T(8,128)S(1)} %get-tuple-element.35), channel_id=1, source_target_pairs={{0,16},{1,17},{2,18},{3,19},{4,20},{5,21},{6,22},{7,23},{8,24},{9,... | collective-permute-start | bytes 442376 | tf_op jit(solution)/shard_map/ppermute | solution.py:651
  20.0 19.9 %collective-permute-start.2 = (f32[13,8,128]{2,1,0:T(8,128)S(1)}, f32[13,8,128]{2,1,0:T(8,128)S(1)}, u32[]{:S(2)}, u32[]{:S(2)}) collective-permute-start(f32[13,8,128]{2,1,0:T(8,128)S(1)} %get-tuple-element.32), channel_id=1, source_target_pairs={{0,15},{1,2},{2,1},{3,4},{4,3},{5,6},{6,5},{7,8},{8,7},{9,10},{10,... | collective-permute-start | bytes 159752 | tf_op jit(solution)/shard_map/ppermute | solution.py:657
  37.0 3.8 %collective-permute-start.3 = (f32[13,8,128]{2,1,0:T(8,128)S(1)}, f32[13,8,128]{2,1,0:T(8,128)S(1)}, u32[]{:S(2)}, u32[]{:S(2)}) collective-permute-start(f32[13,8,128]{2,1,0:T(8,128)S(1)} %get-tuple-element.33), channel_id=1, source_target_pairs={{0,1},{1,0},{2,3},{3,2},{4,5},{5,4},{6,7},{7,6},{8,9},{9,8},{10,11... | collective-permute-start | bytes 159752 | tf_op jit(solution)/shard_map/ppermute | solution.py:658
  46.7 28.3 %all-to-all-start = ((f32[16,8,128]{2,1,0:T(8,128)}), f32[16,8,128]{2,1,0:T(8,128)S(1)}, u32[]{:S(2)}, u32[]{:S(2)}) async-start(f32[16,8,128]{2,1,0:T(8,128)} %get-tuple-element.40), calls=%async_computation | async-start | bytes 131072 | tf_op jit(solution)/shard_map/all_to_all | solution.py:667
  63.5 0.9 %copy-start.3 = (f32[47,8,128]{2,1,0:T(8,128)S(1)}, f32[47,8,128]{2,1,0:T(8,128)}, u32[]{:S(2)}) copy-start(f32[47,8,128]{2,1,0:T(8,128)} %diff.1) | copy-start | bytes 577540
  75.7 15.9 %all-to-all-start.1 = ((f32[32,8,128]{2,1,0:T(8,128)}), f32[32,8,128]{2,1,0:T(8,128)S(1)}, u32[]{:S(2)}, u32[]{:S(2)}) async-start(f32[32,8,128]{2,1,0:T(8,128)} %shard_map.82.after), calls=%async_computation.1 | async-start | bytes 262144 | tf_op jit(solution)/shard_map/all_to_all | solution.py:677

commit v3 on v2

v3 whole, which is shorter than its diff:
```python
import functools

import jax
import jax.numpy as jnp
import numpy as np
from jax import lax
from jax.experimental import pallas as pl
from jax.experimental.pallas import tpu as pltpu
from jax.sharding import PartitionSpec as P

ITERS = 3
K = 48
HORIZONTAL_RATE = 0.2
FLUX_SCALE = 0.02
FACE_SCALE = 0.25
F32 = jnp.float32

PAIR_UV = 0
PAIR_VISC = 48
PAIR_SURF = 72
ROW_X = 73
LAT_TILES = 79
ROW_TILES = 36
PL_U, PL_V, PL_VISC, PL_WET, PL_STO, PL_SUR = 0, 48, 96, 143, 144, 145
PLANES = 146
HALO, CROSS = 152, 298
LON_WIDE = 10
LON_TILES = LON_WIDE + 3
CHUNK = 8
ZED, AROUND = 96, 100


def whereabouts():
    band = lax.axis_index("lat")
    return lax.rem(band, 2), band == lax.axis_size("lat") - 1, lax.rem(lax.axis_index("lon"), 2)


def sub_iota():
    return lax.broadcasted_iota(jnp.int32, (8, 128), 0)


def lane_iota():
    return lax.broadcasted_iota(jnp.int32, (8, 128), 1)


def lroll(x, shift):
    return pltpu.roll(x, shift, 1)


def sroll(x, shift):
    return pltpu.roll(x, shift, 0)


def flip_lanes(x):
    return jnp.take_along_axis(x, 127 - lane_iota(), axis=1)


def flip_rows(x):
    sub = sub_iota()
    x = sroll(x, 4)
    x = jnp.where((sub & 2) == 0, sroll(x, 6), sroll(x, 2))
    return jnp.where((sub & 1) == 0, sroll(x, 7), sroll(x, 1))


def thickness_at(level):
    return 0.5 + level * (1.0 / 48.0)


def spacing_at(level):
    return 96.0 / jnp.full((8, 128), 49.0 + 2.0 * level, F32)


def depth_of(count):
    return 0.5 * count + count * (count - 1.0) * (1.0 / 96.0)


def pack_lat(
    state_any, visc_any, wet_any, storage_any, surf_any,
    out_b, out_a, out_state, out_visc, out_flat,
    pay_b, pay_a, state, visc, flat, wet, sems, out_sems,
):
    odd, top, _ = whereabouts()
    half = 48 * 8
    copies = [
        pltpu.make_async_copy(state_any.at[pl.ds(0, half)], state.at[pl.ds(0, half)], sems.at[0]),
        pltpu.make_async_copy(state_any.at[pl.ds(half, half)], state.at[pl.ds(half, half)], sems.at[1]),
        pltpu.make_async_copy(visc_any, visc, sems.at[2]),
        pltpu.make_async_copy(wet_any, wet, sems.at[3]),
        pltpu.make_async_copy(storage_any, flat.at[1], sems.at[4]),
        pltpu.make_async_copy(surf_any, flat.at[2], sems.at[5]),
    ]
    for copy in copies:
        copy.start()
    sub = sub_iota()
    keep = (sub < 4).astype(jnp.int32) == odd

    def pack(tiles):
        @pl.when(jnp.logical_not(top))
        def _():
            for tile, first, second, _ in tiles():
                rolled = sroll(second, 4)
                pay_a[tile] = jnp.where(keep, first, rolled)
                pay_b[tile] = jnp.where(keep, rolled, first)

        @pl.when(top)
        def _():
            for tile, first, second, sign in tiles():
                rolled = sroll(second, 4)
                pay_a[tile] = jnp.where(keep, first, rolled)
                turned = flip_rows(flip_lanes(jnp.where(keep, rolled, first)))
                pay_b[tile] = -turned if sign < 0 else turned

    def velocities():
        for k in range(48):
            yield k, state[k * 8 : k * 8 + 8, :], state[(k + 48) * 8 : (k + 48) * 8 + 8, :], -1.0

    def others():
        for m in range(23):
            yield PAIR_VISC + m, visc[2 * m], visc[2 * m + 1], 1.0
        yield PAIR_VISC + 23, visc[46], flat[0], 1.0
        yield PAIR_SURF, flat[1], flat[2], 1.0

    def send(source, target, sem):
        copy = pltpu.make_async_copy(source, target, out_sems.at[sem])
        copy.start()
        return copy

    copies[0].wait()
    copies[1].wait()
    leaving = [send(state, out_state, 0)]
    pack(velocities)
    first = pl.ds(0, PAIR_VISC)
    leaving += [send(pay_b.at[first], out_b.at[first], 1), send(pay_a.at[first], out_a.at[first], 2)]
    for copy in copies[2:]:
        copy.wait()
    flat[0] = wet[...].astype(F32)
    leaving += [send(visc, out_visc, 3), send(flat, out_flat, 4)]
    pack(others)
    least = jnp.broadcast_to(jnp.minimum(flat[0, 3:4, :], flat[0, 4:5, :]), (8, 128))
    for m in range(6):
        start = (48 + 8 * m) * 8
        row3 = state[pl.ds(start + 3, 8, stride=8), :]
        row4 = state[pl.ds(start + 4, 8, stride=8), :]
        level = (sub + 8 * m).astype(F32)
        diff = jnp.where(level < least, row3 - row4, 0.0)
        pay_a[ROW_X + m] = diff
        pay_b[ROW_X + m] = -flip_lanes(diff)
    rest = pl.ds(PAIR_VISC, LAT_TILES - PAIR_VISC)
    leaving += [send(pay_b.at[rest], out_b.at[rest], 5), send(pay_a.at[rest], out_a.at[rest], 6)]
    for copy in leaving:
        copy.wait()


def pack_tracers(state_any, pay_b, pay_a, far, near, tracer, sems):
    half = 144 * 8
    copies = [
        pltpu.make_async_copy(
            state_any.at[pl.ds((96 + 144 * i) * 8, half)], tracer.at[pl.ds(i * half, half)], sems.at[i]
        )
        for i in range(2)
    ]
    for copy in copies:
        copy.start()
    for copy in copies:
        copy.wait()
    odd, top, odd_lon = whereabouts()
    lane = lane_iota()

    def rows_of(t):
        start = 8 * t * 8
        return tracer[pl.ds(start, 8, stride=8), :], tracer[pl.ds(start + 7, 8, stride=8), :]

    for t in range(ROW_TILES):
        row0, row7 = rows_of(t)
        pay_a[t] = jnp.where(odd == 1, row0, row7)
        pay_b[t] = jnp.where(odd == 1, row7, row0)

    @pl.when(top)
    def _():
        for t in range(ROW_TILES):
            pay_b[t] = flip_lanes(rows_of(t)[1])

    def scalar(n):
        return tracer[n * 8 : n * 8 + 8, :]

    for tile in range(3):
        planes = [functools.partial(scalar, n) for n in range(128 * tile, min(128 * tile + 128, 288))]
        east, west = pack_columns(lane, planes, 1)
        far[tile] = jnp.where(odd_lon == 1, east, west)
        near[tile] = jnp.where(odd_lon == 1, west, east)


def pack_columns(lane, planes, width):
    east = jnp.zeros((8, 128), F32)
    west = jnp.zeros((8, 128), F32)
    slots = 128 // width
    slot_of = lane // width
    for j, load in enumerate(planes):
        x = load()
        x = lroll(x, j * width) if j else x
        west = jnp.where(slot_of == j, x, west)
        east = jnp.where(slot_of == (j - 1) % slots, x, east)
    return east, west


def lon_planes(state, visc, flat, rows, row_x):
    def plane(n):
        if n < 96:
            return state[n * 8 : n * 8 + 8, :]
        if n < 143:
            return visc[n - 96]
        if n < 146:
            return flat[n - 143]
        if n < HALO:
            return flat[0]
        if n < CROSS:
            return rows[n - HALO]
        return row_x[n - CROSS]

    lane = lane_iota()
    for tile in range(LON_WIDE):
        planes = [functools.partial(plane, n) for n in range(32 * tile, min(32 * tile + 32, CROSS + 6))]
        east, west = pack_columns(lane, planes, 4)
        yield tile, (lroll(east, 64), west)


def pack_lon(
    state, visc, flat, rec_b, rec_a, far_tracers, near_tracers, rows, row_x, far, near
):
    odd, _, odd_lon = whereabouts()
    sub = sub_iota()
    keep = (sub < 4).astype(jnp.int32) != odd

    def unpair(tile):
        a, b = rec_a[tile], rec_b[tile]
        return jnp.where(keep, a, b), sroll(jnp.where(keep, b, a), 4)

    for k in range(48):
        first, second = unpair(k)
        rows[PL_U + k] = first
        rows[PL_V + k] = second
    for m in range(24):
        first, second = unpair(PAIR_VISC + m)
        rows[PL_VISC + 2 * m] = first
        rows[PL_VISC + 2 * m + 1] = second
    first, second = unpair(PAIR_SURF)
    rows[PL_STO] = first
    rows[PL_SUR] = second
    for m in range(6):
        row_x[m] = jnp.where(odd == 1, rec_b[ROW_X + m], rec_a[ROW_X + m])
    for tile, (east, west) in lon_planes(state, visc, flat, rows, row_x):
        far[tile] = jnp.where(odd_lon == 1, east, west)
        near[tile] = jnp.where(odd_lon == 1, west, east)
    for tile in range(3):
        far[LON_WIDE + tile] = far_tracers[tile]
        near[LON_WIDE + tile] = near_tracers[tile]


def each(fn, *lists):
    return [fn(*items) for items in zip(*lists)]


def north_pair(q):
    sub = sub_iota()
    return [sroll(jnp.where(sub == 0, q[1], q[0]), 7), sroll(jnp.where(sub == 0, q[0], q[1]), 7)]


def south_pair(q):
    sub = sub_iota()
    return [sroll(jnp.where(sub == 7, q[1], q[0]), 1), sroll(jnp.where(sub == 7, q[0], q[1]), 1)]


def east_within(q):
    return [lroll(x, 127) for x in q]


def west_within(q):
    return [lroll(x, 1) for x in q]


def columns(load, cross_row, coefficient_at, level_count, top, counts, gain, done, keep):
    sub = sub_iota()
    zero = jnp.zeros((8, 128), F32)
    cross = jnp.logical_and(top, sub == 3)
    ghost = jnp.logical_and(top, sub < 4)
    face_east = each(jnp.minimum, level_count, east_within(level_count))
    face_west = each(jnp.minimum, level_count, west_within(level_count))
    face_north = each(jnp.minimum, level_count, north_pair(level_count))
    face_south = each(jnp.minimum, level_count, south_pair(level_count))
    sums = [
        face_east[0], jnp.where(ghost, face_west[1], face_east[1]),
        face_north[0], jnp.where(ghost, face_south[1], face_north[1]),
    ]
    for i, tile in enumerate(face_east + face_north + level_count + sums):
        counts[i] = tile

    def blend(field, chunk, i, open_east, open_north):
        q = load(field, chunk, i)
        over_east = each(lambda o, a, b: jnp.where(o, a - b, 0.0), open_east, east_within(q), q)
        over_north = each(lambda o, a, b: jnp.where(o, a - b, 0.0), open_north, north_pair(q), q)
        if field == 1:
            over_north[1] = jnp.where(cross, cross_row(chunk, i), over_north[1])
        return each(
            lambda c, a, b, d, e: c + HORIZONTAL_RATE * (a - b + d - e),
            q, over_east, west_within(over_east), over_north, south_pair(over_north),
        )

    def forward(chunk, carry):
        above, prev_gain, prev = carry
        for i in range(CHUNK):
            kf = (CHUNK * chunk + i).astype(F32)
            thick = thickness_at(kf)
            space = spacing_at(kf)
            coefficient = coefficient_at(chunk, i)
            below = [jnp.where(kf + 1.0 < counts[4 + j], coefficient[j] * space, 0.0) for j in range(2)]
            open_east = [kf < counts[j] for j in range(2)]
            open_north = [kf < counts[2 + j] for j in range(2)]
            inverse = [1.0 / (thick + above[j] + below[j] - above[j] * prev_gain[j]) for j in range(2)]
            new_gain = [below[j] * inverse[j] for j in range(2)]
            new = []
            for field in range(2):
                value = blend(field, chunk, i, open_east, open_north)
                new.append([(thick * value[j] + above[j] * prev[field][j]) * inverse[j] for j in range(2)])
            for j in range(2):
                gain[chunk, i, j] = new_gain[j]
                done[0, chunk, i, j] = new[0][j]
                done[1, chunk, i, j] = new[1][j]
            above, prev_gain, prev = below, new_gain, new
        return above, prev_gain, prev

    zeros = [zero, zero]
    lax.fori_loop(0, K // CHUNK, forward, (zeros, zeros, [zeros, zeros]))

    def backward(step, carry):
        chunk = K // CHUNK - 1 - step
        low, flux = carry
        for i in reversed(range(CHUNK)):
            k = CHUNK * chunk + i
            kf = k.astype(F32)
            thick = thickness_at(kf)
            low = [
                [done[field, chunk, i, j] + gain[chunk, i, j] * low[field][j] for j in range(2)] for field in range(2)
            ]
            flux = [
                [
                    flux[field][j] + jnp.where(kf < counts[6 + 2 * field + j], thick * low[field][j], 0.0)
                    for j in range(2)
                ]
                for field in range(2)
            ]
            for field in range(2):
                keep(field, k, low[field][0])
        return low, flux

    _, flux = lax.fori_loop(0, K // CHUNK, backward, ([zeros, zeros], [zeros, zeros]))
    return flux


def momentum_inner(state, visc, flat, rows, row_x, mixed, flux_out, gain, done, counts):
    _, top, _ = whereabouts()

    def load(field, chunk, i):
        n = 48 * field + CHUNK * chunk + i
        return [state[pl.ds(n * 8, 8), :], rows[n]]

    def coefficient_at(chunk, i):
        k = CHUNK * chunk + i
        return [visc[jnp.minimum(k, 46)], rows[PL_VISC + k]]

    def cross_row(chunk, i):
        return jnp.broadcast_to(row_x[chunk, i : i + 1, :], (8, 128))

    def keep(field, k, tile):
        mixed[48 * field + k] = tile

    flux = columns(load, cross_row, coefficient_at, [flat[0], rows[PL_WET]], top, counts, gain, done, keep)
    for field in range(2):
        for j in range(2):
            flux_out[2 * field + j] = flux[field][j]


def momentum(
    state, visc, flat, rows, row_x, flux_inner, far, near,
    mixed, moments,
    gain, done, counts, planes2, xs,
):
    _, top, odd_lon = whereabouts()
    lane = lane_iota()
    sub = sub_iota()
    slot_of = lane // 4
    from_halo = jnp.logical_or(lane < 4, slot_of == 15)
    from_start = slot_of == 16
    zero = jnp.zeros((8, 128), F32)

    def strip_at(tile, j):
        a, b = far[tile], near[tile]
        mine = (slot_of == j).astype(jnp.int32) == odd_lon
        return lroll(jnp.where(mine, a, b), (128 - 4 * j) & 127)

    def strip(n):
        return strip_at(n // 32, n % 32)

    def around_edges(own, halo):
        return jnp.where(from_halo, halo, jnp.where(from_start, lroll(own, 64), own))

    def edges_at(own, chunk, first, i):
        base = first + CHUNK * chunk
        return around_edges(own, strip_at(base >> 5, (base & 31) + i))

    def spread_out(x):
        return jnp.where(lane < 64, x, lroll(x, 64))

    for m in range(6):
        xs[m] = around_edges(row_x[m], strip(m + CROSS))

    def load(field, chunk, i):
        n = 48 * field + CHUNK * chunk + i
        return [
            edges_at(state[pl.ds(n * 8, 8), :], chunk, 48 * field, i),
            edges_at(rows[n], chunk, 48 * field + HALO, i),
        ]

    def coefficient_at(chunk, i):
        k = CHUNK * chunk + i
        return [
            edges_at(visc[jnp.minimum(k, 46)], chunk, PL_VISC, i),
            edges_at(rows[PL_VISC + k], chunk, PL_VISC + HALO, i),
        ]

    def cross_row(chunk, i):
        return jnp.broadcast_to(xs[chunk, i : i + 1, :], (8, 128))

    def keep(field, k, tile):
        mixed[48 * field + k] = tile

    here = jnp.logical_or(from_halo, jnp.logical_or(from_start, lane >= 124))
    wet_edges = [
        jnp.where(here, around_edges(flat[0], strip(PL_WET)), 0.0),
        jnp.where(here, around_edges(rows[PL_WET], strip(PL_WET + HALO)), 0.0),
    ]
    edge_flux = columns(load, cross_row, coefficient_at, wet_edges, top, counts, gain, done, keep)

    def put_together(inner, edge):
        own = [
            jnp.where(lane == 127, e, jnp.where(lane == 0, lroll(e, 64), q)) for q, e in zip(inner, edge)
        ]
        return own + [spread_out(e) for e in edge]

    flux_u = put_together([flux_inner[0], flux_inner[1]], edge_flux[0])
    flux_v = put_together([flux_inner[2], flux_inner[3]], edge_flux[1])

    valid = jnp.logical_or(lane < 4, lane >= 124)

    def four(n, own):
        halo = [jnp.where(valid, spread_out(strip(m)), 0.0) for m in (n, n + HALO)]
        return [own, rows[n]] + halo

    def east(q):
        return [
            lroll(jnp.where(lane == 0, q[2], q[0]), 127),
            lroll(jnp.where(lane == 0, q[3], q[1]), 127),
            lroll(jnp.where(lane == 0, q[0], q[2]), 127),
            lroll(jnp.where(lane == 0, q[1], q[3]), 127),
        ]

    def west(q):
        return [
            lroll(jnp.where(lane == 127, q[2], q[0]), 1),
            lroll(jnp.where(lane == 127, q[3], q[1]), 1),
            lroll(jnp.where(lane == 127, q[0], q[2]), 1),
            lroll(jnp.where(lane == 127, q[1], q[3]), 1),
        ]

    def north(q):
        return north_pair(q[:2]) + north_pair(q[2:])

    def south(q):
        return south_pair(q[:2]) + south_pair(q[2:])

    level_count = four(PL_WET, flat[0])
    around = [each(jnp.minimum, level_count, shift(level_count)) for shift in (east, west, north, south)]
    for i, c in enumerate(around):
        for j in range(4):
            planes2[4 * i + j] = c[j]
    for j in range(4):
        planes2[16 + j] = level_count[j]
    ghost = jnp.logical_and(top, sub < 4)

    last = jnp.logical_and(top, sub == 7)
    first_ghost = jnp.logical_and(top, sub == 0)
    flux_v = [
        jnp.where(last, 0.0, flux_v[0]),
        jnp.where(first_ghost, 0.0, flux_v[1]),
        jnp.where(last, 0.0, flux_v[2]),
        jnp.where(first_ghost, 0.0, flux_v[3]),
    ]
    plain = each(
        lambda a, b, c, d: a - b + c - d, flux_u, west(flux_u), flux_v, south(flux_v)
    )
    mirrored = each(
        lambda a, b, c, d: a - b + c - d, east(flux_u), flux_u, north(flux_v), flux_v
    )
    divergence = [
        plain[0],
        jnp.where(ghost, mirrored[1], plain[1]),
        plain[2],
        jnp.where(ghost, mirrored[3], plain[3]),
    ]
    sto = four(PL_STO, flat[1])
    old = four(PL_SUR, flat[2])
    faces = [[FACE_SCALE * depth_of(planes2[4 * i + j]) for j in range(4)] for i in range(4)]
    diagonal = [
        jnp.maximum(sto[j] + faces[0][j] + faces[1][j] + faces[2][j] + faces[3][j], 0.1) for j in range(4)
    ]
    ocean = [planes2[16 + j] > 0.0 for j in range(4)]
    start = [jnp.where(ocean[j], old[j], 0.0) for j in range(4)]
    around = [east(start), west(start), north(start), south(start)]
    inverse = [1.0 / diagonal[j] for j in range(4)]
    basis = []
    for j in range(4):
        forcing = jnp.where(ocean[j], sto[j] * old[j] - FLUX_SCALE * divergence[j], 0.0)
        image = sto[j] * start[j]
        for i in range(4):
            image = image + faces[i][j] * (start[j] - around[i][j])
        basis.append((forcing - image) / diagonal[j])
    z0 = basis

    def spread(z):
        nb = [east(z), west(z), north(z), south(z)]
        return [
            (faces[0][j] * nb[0][j] + faces[1][j] * nb[1][j] + faces[2][j] * nb[2][j] + faces[3][j] * nb[3][j])
            * inverse[j]
            for j in range(4)
        ]

    z1 = spread(z0)
    z2 = spread(z1)
    mixed[ZED + 0] = start[0]
    mixed[ZED + 1] = z0[0]
    mixed[ZED + 2] = z1[0]
    mixed[ZED + 3] = z2[0]
    weighted = [diagonal[0] * z[0] for z in (z0, z1, z2)]
    north_weight = jnp.where(last, 1.0, 2.0)
    edge = z2[0] * (
        2.0 * faces[0][0] * east(z2)[0] + north_weight * faces[2][0] * north(z2)[0]
    )
    products = [
        weighted[0] * z0[0],
        weighted[0] * z1[0],
        weighted[1] * z1[0],
        weighted[1] * z2[0],
        weighted[2] * z2[0],
        edge,
    ]
    row = jnp.zeros((1, 128), F32)
    for i, product in enumerate(products):
        total = jnp.sum(jnp.sum(product, axis=0, keepdims=True), axis=1, keepdims=True)
        row = jnp.where(lane[:1] == i, total, row)
    moments[...] = jnp.broadcast_to(row, moments.shape)


def tracers_down(state, diff, flat, mixed, rec_b, rec_a, far, near, gain, done):
    odd, _, odd_lon = whereabouts()
    lane = lane_iota()
    sub = sub_iota()
    level_count = flat[0]
    zero = jnp.zeros((8, 128), F32)

    def forward(chunk, carry):
        above, prev_gain, prev = carry
        for i in range(CHUNK):
            k = CHUNK * chunk + i
            kf = k.astype(F32)
            thick = thickness_at(kf)
            coefficient = diff[jnp.minimum(k, 46)]
            below = jnp.where(kf + 1.0 < level_count, coefficient * spacing_at(kf), 0.0)
            inverse = 1.0 / (thick + above + below - above * prev_gain)
            new_gain = below * inverse
            gain[chunk, i] = new_gain
            open_face = [kf < mixed[AROUND + face] for face in range(4)]
            new = []
            for f in range(6):
                first = f * 48 + CHUNK * chunk
                q = state[pl.ds((first + i) * 8, 8), :]
                row_a = rec_a[f * 6 + chunk, i : i + 1, :]
                row_b = rec_b[f * 6 + chunk, i : i + 1, :]
                row_n = jnp.broadcast_to(jnp.where(odd == 1, row_b, row_a), (8, 128))
                row_s = jnp.broadcast_to(jnp.where(odd == 1, row_a, row_b), (8, 128))
                tile, j = first >> 7, (first & 127) + i
                a, b = far[LON_WIDE + tile], near[LON_WIDE + tile]
                side = lroll(jnp.where((lane == j).astype(jnp.int32) == odd_lon, a, b), (128 - j) & 127)
                change = jnp.where(open_face[0], lroll(jnp.where(lane == 0, side, q), 127) - q, 0.0)
                change += jnp.where(open_face[1], lroll(jnp.where(lane == 127, side, q), 1) - q, 0.0)
                change += jnp.where(open_face[2], sroll(jnp.where(sub == 0, row_n, q), 7) - q, 0.0)
                change += jnp.where(open_face[3], sroll(jnp.where(sub == 7, row_s, q), 1) - q, 0.0)
                value = (thick * (q + HORIZONTAL_RATE * change) + above * prev[f]) * inverse
                done[f, chunk, i] = value
                new.append(value)
            above, prev_gain, prev = below, new_gain, new
        return above, prev_gain, prev

    lax.fori_loop(0, K // CHUNK, forward, (zero, zero, [zero] * 6))


def tracers_up(gain, done, inner, mixed, after, out):
    del after
    lane = lane_iota()
    for n in range(96):
        edge = mixed[n]
        out[n] = jnp.where(lane == 127, edge, jnp.where(lane == 0, lroll(edge, 64), inner[n]))
    zero = jnp.zeros((8, 128), F32)

    def backward(step, low):
        chunk = K // CHUNK - 1 - step
        for i in reversed(range(CHUNK)):
            g = gain[chunk, i]
            low = [done[f, chunk, i] + g * low[f] for f in range(6)]
            for f in range(6):
                out[96 + f * 48 + CHUNK * chunk + i] = low[f]
        return low

    lax.fori_loop(0, K // CHUNK, backward, [zero] * 6)


def combine(parts, after, out):
    del after
    out[...] = jnp.broadcast_to(jnp.sum(parts[...], axis=0, keepdims=True), out.shape)


def finish(parts, mixed, surface):
    total = jnp.sum(parts[...], axis=0, keepdims=True)
    nu = [jnp.broadcast_to(total[:, i : i + 1], (8, 128)) for i in range(6)]

    def inner(p, q, shift):
        out = None
        for i, a in enumerate(p):
            for j, b in enumerate(q):
                term = a * b * nu[i + j + shift]
                out = term if out is None else out + term
        return out

    one = jnp.ones((8, 128), F32)
    scaled = [one]
    direction = [one]
    product = nu[0]
    move = [jnp.zeros((8, 128), F32)] * 3
    for iteration in range(ITERS):
        curvature = inner(direction, direction, 0) - inner(direction, direction, 1)
        alpha = product / curvature
        for i, d in enumerate(direction):
            move[i] = move[i] + alpha * d
        if iteration + 1 < ITERS:
            longer = scaled + [jnp.zeros((8, 128), F32)]
            for i, d in enumerate(direction):
                longer[i] = longer[i] - alpha * d
                longer[i + 1] = longer[i + 1] + alpha * d
            scaled = longer
            following = inner(scaled, scaled, 0)
            beta = following / product
            direction = [
                scaled[i] + (beta * direction[i] if i < len(direction) else 0.0) for i in range(len(scaled))
            ]
            product = following
    surface[...] = sum((move[i] * mixed[ZED + 1 + i] for i in range(3)), mixed[ZED])


VMEM_LIMIT = 24 * 1024 * 1024
FIRST_LIMIT = 60 * 1024 * 1024
VMEM = pl.BlockSpec(memory_space=pltpu.VMEM)
ANY = pl.BlockSpec(memory_space=pl.ANY)


def kernel(body, ins, outs, scratch=(), flops=0, nbytes=0, limit=VMEM_LIMIT, out_spec=VMEM):
    return pl.pallas_call(
        body,
        out_shape=[jax.ShapeDtypeStruct(s, F32) for s in outs],
        in_specs=ins,
        out_specs=[out_spec] * len(outs),
        scratch_shapes=[pltpu.VMEM(s, F32) if isinstance(s, tuple) else s for s in scratch],
        compiler_params=pltpu.CompilerParams(vmem_limit_bytes=limit),
        cost_estimate=pl.CostEstimate(flops=flops, bytes_accessed=nbytes, transcendentals=0),
    )


def lat_pairs(lat, lon):
    first, second = [], []
    for l in range(lat):
        for p in range(lon):
            here = l * lon + p
            first.append((here, (l ^ 1) * lon + p))
            if l == lat - 1:
                second.append((here, l * lon + lon - 1 - p))
            elif l % 2 == 1:
                second.append((here, here + lon))
            elif l > 0:
                second.append((here, here - lon))
    return first, second


def lon_pairs(lon):
    far, near = [], []
    for p in range(lon):
        step = 1 if p % 2 else -1
        far.append((p, (p + step) % lon))
        near.append((p, p ^ 1))
    return far, near


def make_local(mesh_shape):
    lat, lon = mesh_shape["lat"], mesh_shape["lon"]
    pairs_a, pairs_b = lat_pairs(lat, lon)
    pairs_far, pairs_near = lon_pairs(lon)
    both = ("lat", "lon")
    stages = reduction_stages(lat, lon)

    def local(ocean_state, viscosity, diffusivity, wet_levels, storage, surface_old):
        state = ocean_state.reshape(8 * K * 8, 128)
        pay_b, pay_a, uv, visc, flat = kernel(
            pack_lat,
            [ANY] * 5,
            [(LAT_TILES, 8, 128)] * 2 + [(96 * 8, 128), (47, 8, 128), (3, 8, 128)],
            scratch=[(LAT_TILES, 8, 128)] * 2 + [
                (96 * 8, 128), (47, 8, 128), (3, 8, 128),
                pltpu.VMEM((8, 128), jnp.int32), pltpu.SemaphoreType.DMA((6,)), pltpu.SemaphoreType.DMA((7,)),
            ],
            out_spec=ANY,
            limit=FIRST_LIMIT,
        )(state, viscosity, wet_levels, storage, surface_old)
        own = (uv, visc, flat)
        rec_b = lax.ppermute(pay_b, both, pairs_b)
        rec_a = lax.ppermute(pay_a, both, pairs_a)
        row_b, row_a, far_tracers, near_tracers, tracer = kernel(
            pack_tracers,
            [ANY],
            [(ROW_TILES, 8, 128)] * 2 + [(3, 8, 128)] * 2 + [(288 * 8, 128)],
            scratch=[pltpu.SemaphoreType.DMA((2,))],
            flops=1_000_000,
            nbytes=2_000_000,
        )(state)
        rec_row_b = lax.ppermute(row_b, both, pairs_b)
        rec_row_a = lax.ppermute(row_a, both, pairs_a)
        rows, row_x, pay_far, pay_near = kernel(
            pack_lon,
            [VMEM] * 7,
            [(PLANES, 8, 128), (6, 8, 128), (LON_TILES, 8, 128), (LON_TILES, 8, 128)],
        )(*own, rec_b, rec_a, far_tracers, near_tracers)
        rec_far = lax.ppermute(pay_far, "lon", pairs_far)
        rec_near = lax.ppermute(pay_near, "lon", pairs_near)
        chunked = (K // CHUNK, CHUNK)
        scratch = [(*chunked, 2, 8, 128), (2, *chunked, 2, 8, 128), (10, 8, 128)]
        inner, flux_inner = kernel(
            momentum_inner,
            [VMEM] * 5,
            [(2 * K, 8, 128), (4, 8, 128)],
            scratch=scratch,
            flops=10_000_000,
            nbytes=6_000_000,
        )(*own, rows, row_x)
        mixed, moments = kernel(
            momentum_entry,
            [VMEM] * 8 + [ANY] * 2,
            [(2 * K + 8, 8, 128), (stages[0][1], 128)],
            scratch=scratch + [(20, 8, 128), (6, 8, 128)],
        )(*own, rows, row_x, flux_inner, rec_far, rec_near, rec_row_b, rec_row_a)
        (first_groups, _), (second_groups, second_size) = stages
        parts = lax.all_to_all(moments, both, 0, 0, axis_index_groups=first_groups, tiled=True)
        gain, done = kernel(
            tracers_down,
            [VMEM] * 8,
            [(*chunked, 8, 128), (6, *chunked, 8, 128)],
            flops=10_000_000,
            nbytes=6_000_000,
        )(tracer, diffusivity, flat, mixed, rec_row_b, rec_row_a, rec_far, rec_near)
        (parts,) = kernel(combine, [VMEM, ANY], [(second_size, 128)])(parts, gain)
        sent = parts
        parts = lax.all_to_all(parts, both, 0, 0, axis_index_groups=second_groups, tiled=True)
        (state_out,) = kernel(
            tracers_up, [VMEM] * 4 + [ANY], [(8 * K, 8, 128)], flops=10_000_000, nbytes=6_000_000
        )(gain, done, inner, mixed, sent)
        (surface,) = kernel(finish, [VMEM] * 2, [(8, 128)])(parts, mixed)
        return state_out.reshape(8, K, 8, 128), surface

    return local


def momentum_entry(*refs):
    inputs, outputs, scratch = refs[:8], refs[10:12], refs[12:]
    mixed, moments = outputs
    momentum(*inputs, mixed, moments, *scratch)
    planes2 = scratch[3]
    for face in range(4):
        mixed[AROUND + face] = planes2[4 * face]


def reduction_stages(lat, lon):
    index = np.arange(lat * lon)
    if lat == 32 and lon == 16:
        grid = index.reshape(8, 4, 4, 2, 2)
        along_z = grid.transpose(1, 2, 4, 3, 0).reshape(32, 16)
        rest = grid.transpose(0, 3, 1, 2, 4).reshape(16, 32)
    else:
        grid = index.reshape(lat, lon)
        along_z, rest = grid.T, grid
    return [(g.tolist(), g.shape[1]) for g in (along_z, rest)]


def solution(mesh):
    placed = (
        P(None, None, "lat", "lon"),
        P(None, "lat", "lon"),
        P(None, "lat", "lon"),
        P("lat", "lon"),
        P("lat", "lon"),
        P("lat", "lon"),
    )
    return jax.shard_map(
        make_local(dict(mesh.shape)),
        mesh=mesh,
        in_specs=placed,
        out_specs=(P(None, None, "lat", "lon"), P("lat", "lon")),
        check_vma=False,
    )
```

time: 92.8 us -> 87.2 us (0.940)
  Pallas kernels: 16.7 us -> 13.2 us
  waiting for transfers between devices: 15 us -> 13 us
  local copies, waits for them, and re-layouts: 0.95 us -> 2.67 us
  starting transfers between devices: 58.3 us -> 57 us
    pallas_call x8 -> x9, Pallas kernels: 16.7 us -> 13.2 us  [the longest x1 3.43 us: local(): kernel(momentum_entry, [VMEM] * 8 + [ANY] * 2, [(2 * K + 8, 8, 128), (sta...]
    all_to_all x1, waiting for transfers between devices: 6.4 us -> 4.51 us  [local(): lax.all_to_all(parts, both, 0, 0, axis_index_groups=second_groups, tiled=...]
    unnamed x12 -> x14, local copies, waits for them, and re-layouts: 0.95 us -> 2.67 us
    all_to_all x1, starting transfers between devices: 16.8 us -> 15.2 us  [local(): lax.all_to_all(moments, both, 0, 0, axis_index_groups=first_groups, tiled...]
    ppermute x1, starting transfers between devices: 16.9 us -> 18 us  [local(): rec_far = lax.ppermute(pay_far, 'lon', pairs_far)]
  transfers between devices with their start and end apart: 8 -> 8, of which waited for: 3 -> 2; matrix products, arithmetic and copies ran while one was open for 0% -> 0% of each run, Pallas kernels for 7% -> 7%
where the time goes in v3:
time: 87.2 us; the launch traced here: 86.7 us
  starting transfers between devices  57 us (65%)
  Pallas kernels  13.2 us (15%)
  waiting for transfers between devices  13 us (15%)
  local copies, waits for them, and re-layouts  2.67 us (3%)
    ppermute x1, starting transfers between devices, local(): rec_far = lax.ppermute(pay_far, 'lon', pairs_far)  18 us
    all_to_all x1, starting transfers between devices, local(): lax.all_to_all(moments, both, 0, 0, axis_index_groups=first_groups, tiled...  15.2 us
    all_to_all x1, waiting for transfers between devices, local(): lax.all_to_all(moments, both, 0, 0, axis_index_groups=first_groups, tiled...  8.52 us
    all_to_all x1, starting transfers between devices, local(): lax.all_to_all(parts, both, 0, 0, axis_index_groups=second_groups, tiled=...  7.91 us
    ppermute x1, starting transfers between devices, local(): rec_a = lax.ppermute(pay_a, both, pairs_a)  6.39 us
    ppermute x1, starting transfers between devices, local(): rec_row_a = lax.ppermute(row_a, both, pairs_a)  5.62 us
    all_to_all x1, waiting for transfers between devices, local(): lax.all_to_all(parts, both, 0, 0, axis_index_groups=second_groups, tiled=...  4.51 us
    pallas_call x1, Pallas kernels, local(): kernel(momentum_entry, [VMEM] * 8 + [ANY] * 2, [(2 * K + 8, 8, 128), (sta...  3.43 us
  transfers between devices with their start and end apart: 8, of which 2 were waited for; matrix products, arithmetic and copies ran while one was open for 0% of the time, Pallas kernels for 7%

profile of v3, /device:TPU:1, one launch (start us, length us, event | category | flops | bytes accessed | tf_op | source)
XLA Modules:
  0.0 86.7 jit_solution(11797717340761739475)
XLA Ops:
  0.6 2.3 %shard_map.78 = (f32[79,8,128]{2,1,0:T(8,128)}, f32[79,8,128]{2,1,0:T(8,128)}, f32[768,128]{1,0:T(8,128)}, f32[47,8,128]{2,1,0:T(8,128)}, f32[3,8,128]{2,1,0:T(8,128)}) custom-call(f32[3072,128]{1,0:T(8,128)} %bitcast.10, f32[47,8,128]{2,1,0:T(8,128)} %visc_any.1, s32[8,128]{1,0:T(8,128)} %wet_any.1, f32[8,128]{1,0:T(8,128)} %storage_any.1, f32[8,128]{1,0:T(8,128)} %surf_any.1), custom_call_target="tpu_custom_call" | custom-call | tf_op jit(solution)/shard_map/pallas_call | solution.py:718
  2.9 0.0 copy-start.1
  3.0 0.8 collective-permute-start
  3.8 6.4 %collective-permute-start.1 = (f32[79,8,128]{2,1,0:T(8,128)}, f32[79,8,128]{2,1,0:T(8,128)S(1)}, u32[]{:S(2)}, u32[]{:S(2)}) collective-permute-start(f32[79,8,128]{2,1,0:T(8,128)} %get-tuple-element.27), channel_id=1, source_target_pairs={{0,16},{1,17},{2,18},{3,19},{4,20},{5,21},{6,22},{7,23},{8,24},{9,... | collective-permute-start | bytes 970760 | tf_op jit(solution)/shard_map/ppermute | solution.py:731
  10.2 0.7 shard_map.77
  10.9 0.7 collective-permute-start.4
  11.6 5.6 %collective-permute-start.5 = (f32[36,8,128]{2,1,0:T(8,128)S(1)}, f32[36,8,128]{2,1,0:T(8,128)S(1)}, u32[]{:S(2)}, u32[]{:S(2)}) collective-permute-start(f32[36,8,128]{2,1,0:T(8,128)S(1)} %get-tuple-element.36), channel_id=1, source_target_pairs={{0,16},{1,17},{2,18},{3,19},{4,20},{5,21},{6,22},{7,23},{8,24},{9,... | collective-permute-start | bytes 442376 | tf_op jit(solution)/shard_map/ppermute | solution.py:741
  17.2 0.8 shard_map.79
  18.0 18.0 %collective-permute-start.2 = (f32[13,8,128]{2,1,0:T(8,128)S(1)}, f32[13,8,128]{2,1,0:T(8,128)S(1)}, u32[]{:S(2)}, u32[]{:S(2)}) collective-permute-start(f32[13,8,128]{2,1,0:T(8,128)S(1)} %get-tuple-element.33), channel_id=1, source_target_pairs={{0,15},{1,2},{2,1},{3,4},{4,3},{5,6},{6,5},{7,8},{8,7},{9,10},{10,... | collective-permute-start | bytes 159752 | tf_op jit(solution)/shard_map/ppermute | solution.py:747
  36.0 2.4 %collective-permute-start.3 = (f32[13,8,128]{2,1,0:T(8,128)S(1)}, f32[13,8,128]{2,1,0:T(8,128)S(1)}, u32[]{:S(2)}, u32[]{:S(2)}) collective-permute-start(f32[13,8,128]{2,1,0:T(8,128)S(1)} %get-tuple-element.34), channel_id=1, source_target_pairs={{0,1},{1,0},{2,3},{3,2},{4,5},{5,4},{6,7},{7,6},{8,9},{9,8},{10,11... | collective-permute-start | bytes 159752 | tf_op jit(solution)/shard_map/ppermute | solution.py:748
  38.4 1.4 %shard_map.80 = (f32[96,8,128]{2,1,0:T(8,128)S(1)}, f32[4,8,128]{2,1,0:T(8,128)S(1)}) custom-call(f32[768,128]{1,0:T(8,128)S(1)} %copy-done.1, f32[47,8,128]{2,1,0:T(8,128)S(1)} %copy-done.2, f32[3,8,128]{2,1,0:T(8,128)S(1)} %copy-done.5, f32[146,8,128]{2,1,0:T(8,128)S(1)} %get-tuple-element.30.rows.refs_3_, f32[6,8,128]{2,1,0:T(8,128)S(1)} %get-tuple-element.31.row_x.refs_4_), custom_call_target="tpu_custom_call" | custom-call | flops 10000000 | bytes 6000000 | tf_op jit(solution)/shard_map/pallas_call | solution.py:751
  39.8 0.7 copy-done.3
  40.6 3.4 %shard_map.81 = (f32[104,8,128]{2,1,0:T(8,128)S(1)}, f32[16,128]{1,0:T(8,128)}) custom-call(f32[768,128]{1,0:T(8,128)S(1)} %copy-done.1, f32[47,8,128]{2,1,0:T(8,128)S(1)} %copy-done.2, f32[3,8,128]{2,1,0:T(8,128)S(1)} %copy-done.5, f32[146,8,128]{2,1,0:T(8,128)S(1)} %get-tuple-element.30.rows.refs_3_, f32[6,8,128]{2,1,0:T(8,128)S(1)} %get-tuple-element.31.row_x.refs_4_, ...), custom_call_target="tpu_custom_call" | custom-call | tf_op jit(solution)/shard_map/pallas_call | solution.py:759
  44.0 15.2 %all-to-all-start = ((f32[16,1,128]{2,1,0:T(1,128)}), f32[16,1,128]{2,1,0:T(1,128)S(1)}, u32[]{:S(2)}, u32[]{:S(2)}) async-start(f32[16,1,128]{2,1,0:T(1,128)} %bitcast.2), calls=%async_computation | async-start | bytes 16384 | tf_op jit(solution)/shard_map/all_to_all | solution.py:766
  59.2 0.9 %copy-done.6 = f32[47,8,128]{2,1,0:T(8,128)S(1)} copy-done((f32[47,8,128]{2,1,0:T(8,128)S(1)}, f32[47,8,128]{2,1,0:T(8,128)}, u32[]{:S(2)}) %copy-start.6) | copy-done | bytes 192536
  60.2 1.8 %shard_map.82 = (f32[6,8,8,128]{3,2,1,0:T(8,128)S(1)}, f32[6,6,8,8,128]{4,3,2,1,0:T(8,128)S(1)}) custom-call(f32[2304,128]{1,0:T(8,128)S(1)} %get-tuple-element.22.state, f32[47,8,128]{2,1,0:T(8,128)S(1)} %copy-done.6, f32[3,8,128]{2,1,0:T(8,128)S(1)} %copy-done.5, f32[104,8,128]{2,1,0:T(8,128)S(1)} %get-tuple-element.37.mixed, ...), custom_call_target="tpu_custom_call" | custom-call | flops 10000000 | bytes 6000000 | tf_op jit(solution)/shard_map/pallas_call | solution.py:767
  62.0 8.5 %all-to-all-done = f32[16,1,128]{2,1,0:T(1,128)S(1)} async-done(((f32[16,1,128]{2,1,0:T(1,128)}), f32[16,1,128]{2,1,0:T(1,128)S(1)}, u32[]{:S(2)}, u32[]{:S(2)}) %all-to-all-start) | async-done | bytes 8224 | tf_op jit(solution)/shard_map/all_to_all | solution.py:766
  70.5 0.6 shard_map.83.after
  71.1 7.9 %all-to-all-start.1 = ((f32[32,1,128]{2,1,0:T(1,128)}), f32[32,1,128]{2,1,0:T(1,128)S(1)}, u32[]{:S(2)}, u32[]{:S(2)}) async-start(f32[32,1,128]{2,1,0:T(1,128)} %bitcast.6), calls=%async_computation.1 | async-start | bytes 32768 | tf_op jit(solution)/shard_map/all_to_all | solution.py:776
  79.1 0.0 copy-start.4
  79.1 1.0 %copy-done.4 = f32[96,8,128]{2,1,0:T(8,128)S(1)} copy-done((f32[96,8,128]{2,1,0:T(8,128)S(1)}, f32[96,8,128]{2,1,0:T(8,128)}, u32[]{:S(2)}) %copy-start.4) | copy-done | bytes 393240
  80.1 1.4 %shard_map.84 = f32[384,8,128]{2,1,0:T(8,128)} custom-call(f32[6,8,8,128]{3,2,1,0:T(8,128)S(1)} %get-tuple-element.38.after.gain, f32[6,6,8,8,128]{4,3,2,1,0:T(8,128)S(1)} %get-tuple-element.39.done, f32[96,8,128]{2,1,0:T(8,128)S(1)} %copy-done.4, f32[104,8,128]{2,1,0:T(8,128)S(1)} %get-tuple-element.37.mixed, f32[32,128]{1,0:T(8,128)} %shard_map.83.after), custom_call_target="tpu_custom_call" | custom-call | flops 10000000 | bytes 6000000 | tf_op jit(solution)/shard_map/pallas_call | solution.py:777
  81.5 4.5 %all-to-all-done.1 = f32[32,1,128]{2,1,0:T(1,128)S(1)} async-done(((f32[32,1,128]{2,1,0:T(1,128)}), f32[32,1,128]{2,1,0:T(1,128)S(1)}, u32[]{:S(2)}, u32[]{:S(2)}) %all-to-all-start.1) | async-done | bytes 16416 | tf_op jit(solution)/shard_map/all_to_all | solution.py:776
  86.0 0.7 shard_map.85
  (15 shorter events, 0.0 us)
Async XLA Ops:
  0.6 9.5 %copy-start = (f32[8,48,8,128]{3,2,1,0:T(8,128)S(1)}, f32[8,48,8,128]{3,2,1,0:T(8,128)}, u32[]{:S(2)}) copy-start(f32[8,48,8,128]{3,2,1,0:T(8,128)} %param.6) | copy-start | bytes 4718596
  2.9 14.3 %copy-start.1 = (f32[768,128]{1,0:T(8,128)S(1)}, f32[768,128]{1,0:T(8,128)}, u32[]{:S(2)}) copy-start(f32[768,128]{1,0:T(8,128)} %get-tuple-element.24.state.refs_0_) | copy-start | bytes 1179652
  2.9 14.3 %copy-start.2 = (f32[47,8,128]{2,1,0:T(8,128)S(1)}, f32[47,8,128]{2,1,0:T(8,128)}, u32[]{:S(2)}) copy-start(f32[47,8,128]{2,1,0:T(8,128)} %get-tuple-element.25.visc.refs_1_) | copy-start | bytes 577540
  2.9 14.3 %copy-start.5 = (f32[3,8,128]{2,1,0:T(8,128)S(1)}, f32[3,8,128]{2,1,0:T(8,128)}, u32[]{:S(2)}) copy-start(f32[3,8,128]{2,1,0:T(8,128)} %get-tuple-element.23.flat.refs_2_) | copy-start | bytes 36868
  3.0 14.2 %collective-permute-start = (f32[79,8,128]{2,1,0:T(8,128)}, f32[79,8,128]{2,1,0:T(8,128)S(1)}, u32[]{:S(2)}, u32[]{:S(2)}) collective-permute-start(f32[79,8,128]{2,1,0:T(8,128)} %get-tuple-element.26), channel_id=1, source_target_pairs={{16,32},{17,33},{18,34},{19,35},{20,36},{21,37},{22,38},{23,39},{2... | collective-permute-start | bytes 970760 | tf_op jit(solution)/shard_map/ppermute | solution.py:730
  3.8 13.4 %collective-permute-start.1 = (f32[79,8,128]{2,1,0:T(8,128)}, f32[79,8,128]{2,1,0:T(8,128)S(1)}, u32[]{:S(2)}, u32[]{:S(2)}) collective-permute-start(f32[79,8,128]{2,1,0:T(8,128)} %get-tuple-element.27), channel_id=1, source_target_pairs={{0,16},{1,17},{2,18},{3,19},{4,20},{5,21},{6,22},{7,23},{8,24},{9,... | collective-permute-start | bytes 970760 | tf_op jit(solution)/shard_map/ppermute | solution.py:731
  10.9 29.7 %collective-permute-start.4 = (f32[36,8,128]{2,1,0:T(8,128)S(1)}, f32[36,8,128]{2,1,0:T(8,128)S(1)}, u32[]{:S(2)}, u32[]{:S(2)}) collective-permute-start(f32[36,8,128]{2,1,0:T(8,128)S(1)} %get-tuple-element.35), channel_id=1, source_target_pairs={{16,32},{17,33},{18,34},{19,35},{20,36},{21,37},{22,38},{23,39},{2... | collective-permute-start | bytes 442376 | tf_op jit(solution)/shard_map/ppermute | solution.py:740
  11.6 29.0 %collective-permute-start.5 = (f32[36,8,128]{2,1,0:T(8,128)S(1)}, f32[36,8,128]{2,1,0:T(8,128)S(1)}, u32[]{:S(2)}, u32[]{:S(2)}) collective-permute-start(f32[36,8,128]{2,1,0:T(8,128)S(1)} %get-tuple-element.36), channel_id=1, source_target_pairs={{0,16},{1,17},{2,18},{3,19},{4,20},{5,21},{6,22},{7,23},{8,24},{9,... | collective-permute-start | bytes 442376 | tf_op jit(solution)/shard_map/ppermute | solution.py:741
  18.0 22.5 %collective-permute-start.2 = (f32[13,8,128]{2,1,0:T(8,128)S(1)}, f32[13,8,128]{2,1,0:T(8,128)S(1)}, u32[]{:S(2)}, u32[]{:S(2)}) collective-permute-start(f32[13,8,128]{2,1,0:T(8,128)S(1)} %get-tuple-element.33), channel_id=1, source_target_pairs={{0,15},{1,2},{2,1},{3,4},{4,3},{5,6},{6,5},{7,8},{8,7},{9,10},{10,... | collective-permute-start | bytes 159752 | tf_op jit(solution)/shard_map/ppermute | solution.py:747
  36.0 4.5 %collective-permute-start.3 = (f32[13,8,128]{2,1,0:T(8,128)S(1)}, f32[13,8,128]{2,1,0:T(8,128)S(1)}, u32[]{:S(2)}, u32[]{:S(2)}) collective-permute-start(f32[13,8,128]{2,1,0:T(8,128)S(1)} %get-tuple-element.34), channel_id=1, source_target_pairs={{0,1},{1,0},{2,3},{3,2},{4,5},{5,4},{6,7},{7,6},{8,9},{9,8},{10,11... | collective-permute-start | bytes 159752 | tf_op jit(solution)/shard_map/ppermute | solution.py:748
  39.8 0.7 copy-start.3
  44.0 26.5 %all-to-all-start = ((f32[16,1,128]{2,1,0:T(1,128)}), f32[16,1,128]{2,1,0:T(1,128)S(1)}, u32[]{:S(2)}, u32[]{:S(2)}) async-start(f32[16,1,128]{2,1,0:T(1,128)} %bitcast.2), calls=%async_computation | async-start | bytes 16384 | tf_op jit(solution)/shard_map/all_to_all | solution.py:766
  59.2 0.9 %copy-start.6 = (f32[47,8,128]{2,1,0:T(8,128)S(1)}, f32[47,8,128]{2,1,0:T(8,128)}, u32[]{:S(2)}) copy-start(f32[47,8,128]{2,1,0:T(8,128)} %diff.1) | copy-start | bytes 577540
  71.1 14.9 %all-to-all-start.1 = ((f32[32,1,128]{2,1,0:T(1,128)}), f32[32,1,128]{2,1,0:T(1,128)S(1)}, u32[]{:S(2)}, u32[]{:S(2)}) async-start(f32[32,1,128]{2,1,0:T(1,128)} %bitcast.6), calls=%async_computation.1 | async-start | bytes 32768 | tf_op jit(solution)/shard_map/all_to_all | solution.py:776
  79.1 1.0 %copy-start.4 = (f32[96,8,128]{2,1,0:T(8,128)S(1)}, f32[96,8,128]{2,1,0:T(8,128)}, u32[]{:S(2)}) copy-start(f32[96,8,128]{2,1,0:T(8,128)} %copy-done.3) | copy-start | bytes 1179652

commit v4 on v3

--- a/solution.py
+++ b/solution.py
@@ -143,10 +143,9 @@
         row4 = state[pl.ds(start + 4, 8, stride=8), :]
         level = (sub + 8 * m).astype(F32)
         diff = jnp.where(level < least, row3 - row4, 0.0)
-        pay_a[ROW_X + m] = diff
         pay_b[ROW_X + m] = -flip_lanes(diff)
-    rest = pl.ds(PAIR_VISC, LAT_TILES - PAIR_VISC)
-    leaving += [send(pay_b.at[rest], out_b.at[rest], 5), send(pay_a.at[rest], out_a.at[rest], 6)]
+    rest_b, rest_a = (pl.ds(PAIR_VISC, count - PAIR_VISC) for count in (LAT_TILES, ROW_X))
+    leaving += [send(pay_b.at[rest_b], out_b.at[rest_b], 5), send(pay_a.at[rest_a], out_a.at[rest_a], 6)]
     for copy in leaving:
         copy.wait()
 
@@ -247,7 +246,7 @@
     rows[PL_STO] = first
     rows[PL_SUR] = second
     for m in range(6):
-        row_x[m] = jnp.where(odd == 1, rec_b[ROW_X + m], rec_a[ROW_X + m])
+        row_x[m] = rec_b[ROW_X + m]
     for tile, (east, west) in lon_planes(state, visc, flat, rows, row_x):
         far[tile] = jnp.where(odd_lon == 1, east, west)
         near[tile] = jnp.where(odd_lon == 1, west, east)
@@ -382,7 +381,7 @@
 def momentum(
     state, visc, flat, rows, row_x, flux_inner, far, near,
     mixed, moments,
-    gain, done, counts, planes2, xs,
+    gain, done, counts, planes2, xs, sides,
 ):
     _, top, odd_lon = whereabouts()
     lane = lane_iota()
@@ -392,10 +391,13 @@
     from_start = slot_of == 16
     zero = jnp.zeros((8, 128), F32)
 
+    for tile in range(LON_WIDE):
+        a, b = far[tile], near[tile]
+        sides[0, tile] = jnp.where(odd_lon == 1, a, b)
+        sides[1, tile] = jnp.where(odd_lon == 1, b, a)
+
     def strip_at(tile, j):
-        a, b = far[tile], near[tile]
-        mine = (slot_of == j).astype(jnp.int32) == odd_lon
-        return lroll(jnp.where(mine, a, b), (128 - 4 * j) & 127)
+        return lroll(jnp.where(slot_of == j, sides[0, tile], sides[1, tile]), (128 - 4 * j) & 127)
 
     def strip(n):
         return strip_at(n // 32, n % 32)
@@ -646,7 +648,7 @@
     move = [jnp.zeros((8, 128), F32)] * 3
     for iteration in range(ITERS):
         curvature = inner(direction, direction, 0) - inner(direction, direction, 1)
-        alpha = product / curvature
+        alpha = jnp.where(curvature > 0.0, product / curvature, 0.0)
         for i, d in enumerate(direction):
             move[i] = move[i] + alpha * d
         if iteration + 1 < ITERS:
@@ -656,7 +658,7 @@
                 longer[i + 1] = longer[i + 1] + alpha * d
             scaled = longer
             following = inner(scaled, scaled, 0)
-            beta = following / product
+            beta = jnp.where(product > 0.0, following / product, 0.0)
             direction = [
                 scaled[i] + (beta * direction[i] if i < len(direction) else 0.0) for i in range(len(scaled))
             ]
@@ -718,8 +720,9 @@
         pay_b, pay_a, uv, visc, flat = kernel(
             pack_lat,
             [ANY] * 5,
-            [(LAT_TILES, 8, 128)] * 2 + [(96 * 8, 128), (47, 8, 128), (3, 8, 128)],
-            scratch=[(LAT_TILES, 8, 128)] * 2 + [
+            [(LAT_TILES, 8, 128), (ROW_X, 8, 128), (96 * 8, 128), (47, 8, 128), (3, 8, 128)],
+            scratch=[
+                (LAT_TILES, 8, 128), (ROW_X, 8, 128),
                 (96 * 8, 128), (47, 8, 128), (3, 8, 128),
                 pltpu.VMEM((8, 128), jnp.int32), pltpu.SemaphoreType.DMA((6,)), pltpu.SemaphoreType.DMA((7,)),
             ],
@@ -760,7 +763,7 @@
             momentum_entry,
             [VMEM] * 8 + [ANY] * 2,
             [(2 * K + 8, 8, 128), (stages[0][1], 128)],
-            scratch=scratch + [(20, 8, 128), (6, 8, 128)],
+            scratch=scratch + [(20, 8, 128), (6, 8, 128), (2, LON_WIDE, 8, 128)],
         )(*own, rows, row_x, flux_inner, rec_far, rec_near, rec_row_b, rec_row_a)
         (first_groups, _), (second_groups, second_size) = stages
         parts = lax.all_to_all(moments, both, 0, 0, axis_index_groups=first_groups, tiled=True)
@@ -801,7 +804,7 @@
     else:
         grid = index.reshape(lat, lon)
         along_z, rest = grid.T, grid
-    return [(g.tolist(), g.shape[1]) for g in (along_z, rest)]
+    return [(g.tolist(), g.shape[1]) for g in (rest, along_z)]
 
 
 def solution(mesh):

time: 87.2 us -> 85.8 us (0.984)
  starting transfers between devices: 57 us -> 55.6 us
    all_to_all x1, starting transfers between devices: 15.2 us -> 6.81 us  [local(): lax.all_to_all(moments, both, 0, 0, axis_index_groups=first_groups, tiled...]
    all_to_all x1, starting transfers between devices: 7.91 us -> 15.5 us  [local(): lax.all_to_all(parts, both, 0, 0, axis_index_groups=second_groups, tiled=...]
    all_to_all x1, waiting for transfers between devices: 8.52 us -> 4.16 us  [local(): lax.all_to_all(moments, both, 0, 0, axis_index_groups=first_groups, tiled...]
    all_to_all x1, waiting for transfers between devices: 4.51 us -> 8.87 us  [local(): lax.all_to_all(parts, both, 0, 0, axis_index_groups=second_groups, tiled=...]
    ppermute x1, starting transfers between devices: 18 us -> 17 us  [local(): rec_far = lax.ppermute(pay_far, 'lon', pairs_far)]
where the time goes in v4:
time: 85.8 us; the launch traced here: 85.4 us
  starting transfers between devices  55.6 us (65%)
  Pallas kernels  13.2 us (15%)
  waiting for transfers between devices  13 us (15%)
  local copies, waits for them, and re-layouts  2.67 us (3%)
    ppermute x1, starting transfers between devices, local(): rec_far = lax.ppermute(pay_far, 'lon', pairs_far)  17 us
    all_to_all x1, starting transfers between devices, local(): lax.all_to_all(parts, both, 0, 0, axis_index_groups=second_groups, tiled=...  15.5 us
    all_to_all x1, waiting for transfers between devices, local(): lax.all_to_all(parts, both, 0, 0, axis_index_groups=second_groups, tiled=...  8.87 us
    all_to_all x1, starting transfers between devices, local(): lax.all_to_all(moments, both, 0, 0, axis_index_groups=first_groups, tiled...  6.81 us
    ppermute x1, starting transfers between devices, local(): rec_a = lax.ppermute(pay_a, both, pairs_a)  6.39 us
    ppermute x1, starting transfers between devices, local(): rec_row_a = lax.ppermute(row_a, both, pairs_a)  5.62 us
    all_to_all x1, waiting for transfers between devices, local(): lax.all_to_all(moments, both, 0, 0, axis_index_groups=first_groups, tiled...  4.16 us
    pallas_call x1, Pallas kernels, local(): kernel(momentum_entry, [VMEM] * 8 + [ANY] * 2, [(2 * K + 8, 8, 128), (sta...  3.44 us
  transfers between devices with their start and end apart: 8, of which 2 were waited for; matrix products, arithmetic and copies ran while one was open for 0% of the time, Pallas kernels for 7%

profile of v4, /device:TPU:1, one launch (start us, length us, event | category | flops | bytes accessed | tf_op | source)
XLA Modules:
  0.0 85.4 jit_solution(3739015699848241000)
XLA Ops:
  0.6 2.3 %shard_map.78 = (f32[79,8,128]{2,1,0:T(8,128)}, f32[73,8,128]{2,1,0:T(8,128)}, f32[768,128]{1,0:T(8,128)}, f32[47,8,128]{2,1,0:T(8,128)}, f32[3,8,128]{2,1,0:T(8,128)}) custom-call(f32[3072,128]{1,0:T(8,128)} %bitcast.10, f32[47,8,128]{2,1,0:T(8,128)} %visc_any.1, s32[8,128]{1,0:T(8,128)} %wet_any.1, f32[8,128]{1,0:T(8,128)} %storage_any.1, f32[8,128]{1,0:T(8,128)} %surf_any.1), custom_call_target="tpu_custom_call" | custom-call | tf_op jit(solution)/shard_map/pallas_call | solution.py:720
  2.9 0.0 copy-start.1
  2.9 0.8 collective-permute-start
  3.8 6.4 %collective-permute-start.1 = (f32[73,8,128]{2,1,0:T(8,128)}, f32[73,8,128]{2,1,0:T(8,128)S(1)}, u32[]{:S(2)}, u32[]{:S(2)}) collective-permute-start(f32[73,8,128]{2,1,0:T(8,128)} %get-tuple-element.27), channel_id=1, source_target_pairs={{0,16},{1,17},{2,18},{3,19},{4,20},{5,21},{6,22},{7,23},{8,24},{9,... | collective-permute-start | bytes 897032 | tf_op jit(solution)/shard_map/ppermute | solution.py:734
  10.2 0.7 shard_map.77
  10.9 0.7 collective-permute-start.4
  11.5 5.6 %collective-permute-start.5 = (f32[36,8,128]{2,1,0:T(8,128)S(1)}, f32[36,8,128]{2,1,0:T(8,128)S(1)}, u32[]{:S(2)}, u32[]{:S(2)}) collective-permute-start(f32[36,8,128]{2,1,0:T(8,128)S(1)} %get-tuple-element.36), channel_id=1, source_target_pairs={{0,16},{1,17},{2,18},{3,19},{4,20},{5,21},{6,22},{7,23},{8,24},{9,... | collective-permute-start | bytes 442376 | tf_op jit(solution)/shard_map/ppermute | solution.py:744
  17.2 0.8 shard_map.79
  18.0 17.0 %collective-permute-start.2 = (f32[13,8,128]{2,1,0:T(8,128)S(1)}, f32[13,8,128]{2,1,0:T(8,128)S(1)}, u32[]{:S(2)}, u32[]{:S(2)}) collective-permute-start(f32[13,8,128]{2,1,0:T(8,128)S(1)} %get-tuple-element.33), channel_id=1, source_target_pairs={{0,15},{1,2},{2,1},{3,4},{4,3},{5,6},{6,5},{7,8},{8,7},{9,10},{10,... | collective-permute-start | bytes 159752 | tf_op jit(solution)/shard_map/ppermute | solution.py:750
  35.0 2.9 %collective-permute-start.3 = (f32[13,8,128]{2,1,0:T(8,128)S(1)}, f32[13,8,128]{2,1,0:T(8,128)S(1)}, u32[]{:S(2)}, u32[]{:S(2)}) collective-permute-start(f32[13,8,128]{2,1,0:T(8,128)S(1)} %get-tuple-element.34), channel_id=1, source_target_pairs={{0,1},{1,0},{2,3},{3,2},{4,5},{5,4},{6,7},{7,6},{8,9},{9,8},{10,11... | collective-permute-start | bytes 159752 | tf_op jit(solution)/shard_map/ppermute | solution.py:751
  37.8 1.4 %shard_map.80 = (f32[96,8,128]{2,1,0:T(8,128)S(1)}, f32[4,8,128]{2,1,0:T(8,128)S(1)}) custom-call(f32[768,128]{1,0:T(8,128)S(1)} %copy-done.1, f32[47,8,128]{2,1,0:T(8,128)S(1)} %copy-done.2, f32[3,8,128]{2,1,0:T(8,128)S(1)} %copy-done.5, f32[146,8,128]{2,1,0:T(8,128)S(1)} %get-tuple-element.30.rows.refs_3_, f32[6,8,128]{2,1,0:T(8,128)S(1)} %get-tuple-element.31.row_x.refs_4_), custom_call_target="tpu_custom_call" | custom-call | flops 10000000 | bytes 6000000 | tf_op jit(solution)/shard_map/pallas_call | solution.py:754
  39.3 0.0 copy-start.3
  39.3 0.7 copy-done.3
  40.0 3.4 %shard_map.81 = (f32[104,8,128]{2,1,0:T(8,128)S(1)}, f32[32,128]{1,0:T(8,128)}) custom-call(f32[768,128]{1,0:T(8,128)S(1)} %copy-done.1, f32[47,8,128]{2,1,0:T(8,128)S(1)} %copy-done.2, f32[3,8,128]{2,1,0:T(8,128)S(1)} %copy-done.5, f32[146,8,128]{2,1,0:T(8,128)S(1)} %get-tuple-element.30.rows.refs_3_, f32[6,8,128]{2,1,0:T(8,128)S(1)} %get-tuple-element.31.row_x.refs_4_, ...), custom_call_target="tpu_custom_call" | custom-call | tf_op jit(solution)/shard_map/pallas_call | solution.py:762
  43.5 6.8 %all-to-all-start = ((f32[32,1,128]{2,1,0:T(1,128)}), f32[32,1,128]{2,1,0:T(1,128)S(1)}, u32[]{:S(2)}, u32[]{:S(2)}) async-start(f32[32,1,128]{2,1,0:T(1,128)} %bitcast.2), calls=%async_computation | async-start | bytes 32768 | tf_op jit(solution)/shard_map/all_to_all | solution.py:769
  50.3 0.9 %copy-done.6 = f32[47,8,128]{2,1,0:T(8,128)S(1)} copy-done((f32[47,8,128]{2,1,0:T(8,128)S(1)}, f32[47,8,128]{2,1,0:T(8,128)}, u32[]{:S(2)}) %copy-start.6) | copy-done | bytes 192536
  51.2 1.8 %shard_map.82 = (f32[6,8,8,128]{3,2,1,0:T(8,128)S(1)}, f32[6,6,8,8,128]{4,3,2,1,0:T(8,128)S(1)}) custom-call(f32[2304,128]{1,0:T(8,128)S(1)} %get-tuple-element.22.state, f32[47,8,128]{2,1,0:T(8,128)S(1)} %copy-done.6, f32[3,8,128]{2,1,0:T(8,128)S(1)} %copy-done.5, f32[104,8,128]{2,1,0:T(8,128)S(1)} %get-tuple-element.37.mixed, ...), custom_call_target="tpu_custom_call" | custom-call | flops 10000000 | bytes 6000000 | tf_op jit(solution)/shard_map/pallas_call | solution.py:770
  53.1 4.2 %all-to-all-done = f32[32,1,128]{2,1,0:T(1,128)S(1)} async-done(((f32[32,1,128]{2,1,0:T(1,128)}), f32[32,1,128]{2,1,0:T(1,128)S(1)}, u32[]{:S(2)}, u32[]{:S(2)}) %all-to-all-start) | async-done | bytes 16416 | tf_op jit(solution)/shard_map/all_to_all | solution.py:769
  57.2 0.6 shard_map.83.after
  57.8 15.5 %all-to-all-start.1 = ((f32[16,1,128]{2,1,0:T(1,128)}), f32[16,1,128]{2,1,0:T(1,128)S(1)}, u32[]{:S(2)}, u32[]{:S(2)}) async-start(f32[16,1,128]{2,1,0:T(1,128)} %bitcast.6), calls=%async_computation.1 | async-start | bytes 16384 | tf_op jit(solution)/shard_map/all_to_all | solution.py:779
  73.4 1.0 %copy-done.4 = f32[96,8,128]{2,1,0:T(8,128)S(1)} copy-done((f32[96,8,128]{2,1,0:T(8,128)S(1)}, f32[96,8,128]{2,1,0:T(8,128)}, u32[]{:S(2)}) %copy-start.4) | copy-done | bytes 393240
  74.3 1.4 %shard_map.84 = f32[384,8,128]{2,1,0:T(8,128)} custom-call(f32[6,8,8,128]{3,2,1,0:T(8,128)S(1)} %get-tuple-element.38.after.gain, f32[6,6,8,8,128]{4,3,2,1,0:T(8,128)S(1)} %get-tuple-element.39.done, f32[96,8,128]{2,1,0:T(8,128)S(1)} %copy-done.4, f32[104,8,128]{2,1,0:T(8,128)S(1)} %get-tuple-element.37.mixed, f32[16,128]{1,0:T(8,128)} %shard_map.83.after), custom_call_target="tpu_custom_call" | custom-call | flops 10000000 | bytes 6000000 | tf_op jit(solution)/shard_map/pallas_call | solution.py:780
  75.8 8.9 %all-to-all-done.1 = f32[16,1,128]{2,1,0:T(1,128)S(1)} async-done(((f32[16,1,128]{2,1,0:T(1,128)}), f32[16,1,128]{2,1,0:T(1,128)S(1)}, u32[]{:S(2)}, u32[]{:S(2)}) %all-to-all-start.1) | async-done | bytes 8224 | tf_op jit(solution)/shard_map/all_to_all | solution.py:779
  84.6 0.7 shard_map.85
  (15 shorter events, 0.0 us)
Async XLA Ops:
  0.6 9.5 %copy-start = (f32[8,48,8,128]{3,2,1,0:T(8,128)S(1)}, f32[8,48,8,128]{3,2,1,0:T(8,128)}, u32[]{:S(2)}) copy-start(f32[8,48,8,128]{3,2,1,0:T(8,128)} %param.6) | copy-start | bytes 4718596
  2.9 14.3 %copy-start.1 = (f32[768,128]{1,0:T(8,128)S(1)}, f32[768,128]{1,0:T(8,128)}, u32[]{:S(2)}) copy-start(f32[768,128]{1,0:T(8,128)} %get-tuple-element.24.state.refs_0_) | copy-start | bytes 1179652
  2.9 14.3 %copy-start.2 = (f32[47,8,128]{2,1,0:T(8,128)S(1)}, f32[47,8,128]{2,1,0:T(8,128)}, u32[]{:S(2)}) copy-start(f32[47,8,128]{2,1,0:T(8,128)} %get-tuple-element.25.visc.refs_1_) | copy-start | bytes 577540
  2.9 14.3 %copy-start.5 = (f32[3,8,128]{2,1,0:T(8,128)S(1)}, f32[3,8,128]{2,1,0:T(8,128)}, u32[]{:S(2)}) copy-start(f32[3,8,128]{2,1,0:T(8,128)} %get-tuple-element.23.flat.refs_2_) | copy-start | bytes 36868
  2.9 14.2 %collective-permute-start = (f32[79,8,128]{2,1,0:T(8,128)}, f32[79,8,128]{2,1,0:T(8,128)S(1)}, u32[]{:S(2)}, u32[]{:S(2)}) collective-permute-start(f32[79,8,128]{2,1,0:T(8,128)} %get-tuple-element.26), channel_id=1, source_target_pairs={{16,32},{17,33},{18,34},{19,35},{20,36},{21,37},{22,38},{23,39},{2... | collective-permute-start | bytes 970760 | tf_op jit(solution)/shard_map/ppermute | solution.py:733
  3.8 13.4 %collective-permute-start.1 = (f32[73,8,128]{2,1,0:T(8,128)}, f32[73,8,128]{2,1,0:T(8,128)S(1)}, u32[]{:S(2)}, u32[]{:S(2)}) collective-permute-start(f32[73,8,128]{2,1,0:T(8,128)} %get-tuple-element.27), channel_id=1, source_target_pairs={{0,16},{1,17},{2,18},{3,19},{4,20},{5,21},{6,22},{7,23},{8,24},{9,... | collective-permute-start | bytes 897032 | tf_op jit(solution)/shard_map/ppermute | solution.py:734
  10.9 29.1 %collective-permute-start.4 = (f32[36,8,128]{2,1,0:T(8,128)S(1)}, f32[36,8,128]{2,1,0:T(8,128)S(1)}, u32[]{:S(2)}, u32[]{:S(2)}) collective-permute-start(f32[36,8,128]{2,1,0:T(8,128)S(1)} %get-tuple-element.35), channel_id=1, source_target_pairs={{16,32},{17,33},{18,34},{19,35},{20,36},{21,37},{22,38},{23,39},{2... | collective-permute-start | bytes 442376 | tf_op jit(solution)/shard_map/ppermute | solution.py:743
  11.5 28.5 %collective-permute-start.5 = (f32[36,8,128]{2,1,0:T(8,128)S(1)}, f32[36,8,128]{2,1,0:T(8,128)S(1)}, u32[]{:S(2)}, u32[]{:S(2)}) collective-permute-start(f32[36,8,128]{2,1,0:T(8,128)S(1)} %get-tuple-element.36), channel_id=1, source_target_pairs={{0,16},{1,17},{2,18},{3,19},{4,20},{5,21},{6,22},{7,23},{8,24},{9,... | collective-permute-start | bytes 442376 | tf_op jit(solution)/shard_map/ppermute | solution.py:744
  18.0 22.0 %collective-permute-start.2 = (f32[13,8,128]{2,1,0:T(8,128)S(1)}, f32[13,8,128]{2,1,0:T(8,128)S(1)}, u32[]{:S(2)}, u32[]{:S(2)}) collective-permute-start(f32[13,8,128]{2,1,0:T(8,128)S(1)} %get-tuple-element.33), channel_id=1, source_target_pairs={{0,15},{1,2},{2,1},{3,4},{4,3},{5,6},{6,5},{7,8},{8,7},{9,10},{10,... | collective-permute-start | bytes 159752 | tf_op jit(solution)/shard_map/ppermute | solution.py:750
  35.0 5.1 %collective-permute-start.3 = (f32[13,8,128]{2,1,0:T(8,128)S(1)}, f32[13,8,128]{2,1,0:T(8,128)S(1)}, u32[]{:S(2)}, u32[]{:S(2)}) collective-permute-start(f32[13,8,128]{2,1,0:T(8,128)S(1)} %get-tuple-element.34), channel_id=1, source_target_pairs={{0,1},{1,0},{2,3},{3,2},{4,5},{5,4},{6,7},{7,6},{8,9},{9,8},{10,11... | collective-permute-start | bytes 159752 | tf_op jit(solution)/shard_map/ppermute | solution.py:751
  39.3 0.7 copy-start.3
  43.5 13.8 %all-to-all-start = ((f32[32,1,128]{2,1,0:T(1,128)}), f32[32,1,128]{2,1,0:T(1,128)S(1)}, u32[]{:S(2)}, u32[]{:S(2)}) async-start(f32[32,1,128]{2,1,0:T(1,128)} %bitcast.2), calls=%async_computation | async-start | bytes 32768 | tf_op jit(solution)/shard_map/all_to_all | solution.py:769
  50.3 0.9 %copy-start.6 = (f32[47,8,128]{2,1,0:T(8,128)S(1)}, f32[47,8,128]{2,1,0:T(8,128)}, u32[]{:S(2)}) copy-start(f32[47,8,128]{2,1,0:T(8,128)} %diff.1) | copy-start | bytes 577540
  57.8 26.8 %all-to-all-start.1 = ((f32[16,1,128]{2,1,0:T(1,128)}), f32[16,1,128]{2,1,0:T(1,128)S(1)}, u32[]{:S(2)}, u32[]{:S(2)}) async-start(f32[16,1,128]{2,1,0:T(1,128)} %bitcast.6), calls=%async_computation.1 | async-start | bytes 16384 | tf_op jit(solution)/shard_map/all_to_all | solution.py:779
  73.3 1.0 %copy-start.4 = (f32[96,8,128]{2,1,0:T(8,128)S(1)}, f32[96,8,128]{2,1,0:T(8,128)}, u32[]{:S(2)}) copy-start(f32[96,8,128]{2,1,0:T(8,128)} %copy-done.3) | copy-start | bytes 1179652

commit v5 on v4

--- a/solution.py
+++ b/solution.py
@@ -24,6 +24,7 @@
 PL_U, PL_V, PL_VISC, PL_WET, PL_STO, PL_SUR = 0, 48, 96, 143, 144, 145
 PLANES = 146
 HALO, CROSS = 152, 298
+GROUPS = 38
 LON_WIDE = 10
 LON_TILES = LON_WIDE + 3
 CHUNK = 8
@@ -195,6 +196,8 @@
     slots = 128 // width
     slot_of = lane // width
     for j, load in enumerate(planes):
+        if load is None:
+            continue
         x = load()
         x = lroll(x, j * width) if j else x
         west = jnp.where(slot_of == j, x, west)
@@ -218,9 +221,9 @@
 
     lane = lane_iota()
     for tile in range(LON_WIDE):
-        planes = [functools.partial(plane, n) for n in range(32 * tile, min(32 * tile + 32, CROSS + 6))]
-        east, west = pack_columns(lane, planes, 4)
-        yield tile, (lroll(east, 64), west)
+        order = [32 * tile + 8 * (j % 4) + j // 4 for j in range(32)]
+        planes = [functools.partial(plane, n) if n < CROSS + 6 else None for n in order]
+        yield tile, pack_columns(lane, planes, 4)
 
 
 def pack_lon(
@@ -378,84 +381,131 @@
             flux_out[2 * field + j] = flux[field][j]
 
 
+def to_last(x):
+    return lroll(x, 124)
+
+
+def to_first(x):
+    return lroll(x, 116)
+
+
 def momentum(
-    state, visc, flat, rows, row_x, flux_inner, far, near,
+    flat, rows, flux_inner, pay_far, pay_near, far, near,
     mixed, moments,
-    gain, done, counts, planes2, xs, sides,
+    windows, below_all, scaled_all, gain, done, planes2,
 ):
     _, top, odd_lon = whereabouts()
     lane = lane_iota()
     sub = sub_iota()
-    slot_of = lane // 4
-    from_halo = jnp.logical_or(lane < 4, slot_of == 15)
-    from_start = slot_of == 16
     zero = jnp.zeros((8, 128), F32)
+    ghost = jnp.logical_and(top, sub < 4)
 
     for tile in range(LON_WIDE):
-        a, b = far[tile], near[tile]
-        sides[0, tile] = jnp.where(odd_lon == 1, a, b)
-        sides[1, tile] = jnp.where(odd_lon == 1, b, a)
-
-    def strip_at(tile, j):
-        return lroll(jnp.where(slot_of == j, sides[0, tile], sides[1, tile]), (128 - 4 * j) & 127)
-
-    def strip(n):
-        return strip_at(n // 32, n % 32)
-
-    def around_edges(own, halo):
-        return jnp.where(from_halo, halo, jnp.where(from_start, lroll(own, 64), own))
-
-    def edges_at(own, chunk, first, i):
-        base = first + CHUNK * chunk
-        return around_edges(own, strip_at(base >> 5, (base & 31) + i))
-
-    def spread_out(x):
-        return jnp.where(lane < 64, x, lroll(x, 64))
-
-    for m in range(6):
-        xs[m] = around_edges(row_x[m], strip(m + CROSS))
-
-    def load(field, chunk, i):
-        n = 48 * field + CHUNK * chunk + i
-        return [
-            edges_at(state[pl.ds(n * 8, 8), :], chunk, 48 * field, i),
-            edges_at(rows[n], chunk, 48 * field + HALO, i),
+        sent = [pay_far[tile], pay_near[tile]]
+        came = [far[tile], near[tile]]
+        own_east, own_west = (jnp.where(odd_lon == 1, *pair) for pair in (sent, sent[::-1]))
+        halo_east, halo_west = (jnp.where(odd_lon == 1, *pair) for pair in (came, came[::-1]))
+        for g in range(min(4, GROUPS - 4 * tile)):
+            here = ((lane - 4 * g) & 15) < 4
+            first = lroll(jnp.where(here, halo_east, own_east), (4 - 4 * g) & 127)
+            second = lroll(jnp.where(here, own_west, halo_west), (12 - 4 * g) & 127)
+            windows[4 * tile + g] = jnp.where((lane & 15) < 8, first, second)
+
+    def window(n):
+        shift = (128 - 16 * (n % 8)) & 127
+        return lroll(windows[n // 8], shift) if shift else windows[n // 8]
+
+    def everywhere(x):
+        x = jnp.where(lane < 16, x, 0.0)
+        for step in (16, 32, 64):
+            x = x + lroll(x, step)
+        return x
+
+    wet_window = [everywhere(window(PL_WET)), everywhere(window(PL_WET + HALO))]
+    face_east = each(jnp.minimum, wet_window, east_within(wet_window))
+    face_west = each(jnp.minimum, wet_window, west_within(wet_window))
+    face_north = each(jnp.minimum, wet_window, north_pair(wet_window))
+    face_south = each(jnp.minimum, wet_window, south_pair(wet_window))
+    sum_u = [face_east[0], jnp.where(ghost, face_west[1], face_east[1])]
+    sum_v = [face_north[0], jnp.where(ghost, face_south[1], face_north[1])]
+    cross = jnp.logical_and(top, sub == 3)
+    part = lane // 16
+
+    for chunk in range(K // CHUNK):
+        level = (part + CHUNK * chunk).astype(F32)
+        thick = thickness_at(level)
+        space = 96.0 / (49.0 + 2.0 * level)
+        open_east = [level < c for c in face_east]
+        open_north = [level < c for c in face_north]
+        group = PL_VISC // CHUNK + chunk
+        for j, shift in enumerate((0, HALO // CHUNK)):
+            below_all[chunk, j] = jnp.where(level + 1.0 < wet_window[j], windows[group + shift] * space, 0.0)
+        for field in range(2):
+            group = K // CHUNK * field + chunk
+            q = [windows[group], windows[group + HALO // CHUNK]]
+            over_east = each(lambda o, a, b: jnp.where(o, a - b, 0.0), open_east, east_within(q), q)
+            over_north = each(lambda o, a, b: jnp.where(o, a - b, 0.0), open_north, north_pair(q), q)
+            if field == 1:
+                levels = jnp.where(part == sub, everywhere(window(CROSS + chunk)), 0.0)
+                extra = jnp.broadcast_to(jnp.sum(levels, axis=0, keepdims=True), (8, 128))
+                over_north[1] = jnp.where(cross, extra, over_north[1])
+            blended = each(
+                lambda c, a, b, d, e: c + HORIZONTAL_RATE * (a - b + d - e),
+                q, over_east, west_within(over_east), over_north, south_pair(over_north),
+            )
+            for j in range(2):
+                scaled_all[field, chunk, j] = thick * blended[j]
+
+    def at_level(tile, k):
+        shift = (128 - 16 * (k % CHUNK)) & 127
+        return lroll(tile, shift) if shift else tile
+
+    above = prev_gain = [zero, zero]
+    prev = [[zero, zero], [zero, zero]]
+    for k in range(K):
+        thick = 0.5 + k / 48.0
+        below = [at_level(below_all[k // CHUNK, j], k) for j in range(2)]
+        inverse = [1.0 / (thick + above[j] + below[j] - above[j] * prev_gain[j]) for j in range(2)]
+        prev_gain = [below[j] * inverse[j] for j in range(2)]
+        prev = [
+            [
+                (at_level(scaled_all[field, k // CHUNK, j], k) + above[j] * prev[field][j]) * inverse[j]
+                for j in range(2)
+            ]
+            for field in range(2)
         ]
-
-    def coefficient_at(chunk, i):
-        k = CHUNK * chunk + i
-        return [
-            edges_at(visc[jnp.minimum(k, 46)], chunk, PL_VISC, i),
-            edges_at(rows[PL_VISC + k], chunk, PL_VISC + HALO, i),
+        for j in range(2):
+            gain[k, j] = prev_gain[j]
+            for field in range(2):
+                done[field, k, j] = prev[field][j]
+        above = below
+    low = flux = [[zero, zero], [zero, zero]]
+    for k in reversed(range(K)):
+        thick = 0.5 + k / 48.0
+        low = [[done[field, k, j] + gain[k, j] * low[field][j] for j in range(2)] for field in range(2)]
+        flux = [
+            [flux[field][j] + jnp.where(k < counts[j], thick * low[field][j], 0.0) for j in range(2)]
+            for field, counts in enumerate((sum_u, sum_v))
         ]
-
-    def cross_row(chunk, i):
-        return jnp.broadcast_to(xs[chunk, i : i + 1, :], (8, 128))
-
-    def keep(field, k, tile):
-        mixed[48 * field + k] = tile
-
-    here = jnp.logical_or(from_halo, jnp.logical_or(from_start, lane >= 124))
-    wet_edges = [
-        jnp.where(here, around_edges(flat[0], strip(PL_WET)), 0.0),
-        jnp.where(here, around_edges(rows[PL_WET], strip(PL_WET + HALO)), 0.0),
-    ]
-    edge_flux = columns(load, cross_row, coefficient_at, wet_edges, top, counts, gain, done, keep)
+        for field in range(2):
+            mixed[48 * field + k] = low[field][0]
 
     def put_together(inner, edge):
         own = [
-            jnp.where(lane == 127, e, jnp.where(lane == 0, lroll(e, 64), q)) for q, e in zip(inner, edge)
+            jnp.where(lane == 127, to_last(e), jnp.where(lane == 0, to_first(e), q)) for q, e in zip(inner, edge)
         ]
-        return own + [spread_out(e) for e in edge]
-
-    flux_u = put_together([flux_inner[0], flux_inner[1]], edge_flux[0])
-    flux_v = put_together([flux_inner[2], flux_inner[3]], edge_flux[1])
+        return own + [jnp.where(lane < 64, to_last(e), to_first(e)) for e in edge]
+
+    flux_u = put_together([flux_inner[0], flux_inner[1]], flux[0])
+    flux_v = put_together([flux_inner[2], flux_inner[3]], flux[1])
 
     valid = jnp.logical_or(lane < 4, lane >= 124)
 
     def four(n, own):
-        halo = [jnp.where(valid, spread_out(strip(m)), 0.0) for m in (n, n + HALO)]
-        return [own, rows[n]] + halo
+        pair = [window(n), window(n + HALO)]
+        return [own, rows[n]] + [
+            jnp.where(valid, jnp.where(lane < 64, to_last(e), to_first(e)), 0.0) for e in pair
+        ]
 
     def east(q):
         return [
@@ -486,8 +536,6 @@
             planes2[4 * i + j] = c[j]
     for j in range(4):
         planes2[16 + j] = level_count[j]
-    ghost = jnp.logical_and(top, sub < 4)
-
     last = jnp.logical_and(top, sub == 7)
     first_ghost = jnp.logical_and(top, sub == 0)
     flux_v = [
@@ -561,7 +609,8 @@
     moments[...] = jnp.broadcast_to(row, moments.shape)
 
 
-def tracers_down(state, diff, flat, mixed, rec_b, rec_a, far, near, gain, done):
+def tracers_down(state, diff, flat, mixed, rec_b, rec_a, far, near, after, gain, done):
+    del after
     odd, _, odd_lon = whereabouts()
     lane = lane_iota()
     sub = sub_iota()
@@ -604,12 +653,11 @@
     lax.fori_loop(0, K // CHUNK, forward, (zero, zero, [zero] * 6))
 
 
-def tracers_up(gain, done, inner, mixed, after, out):
-    del after
+def tracers_up(gain, done, inner, mixed, out):
     lane = lane_iota()
     for n in range(96):
         edge = mixed[n]
-        out[n] = jnp.where(lane == 127, edge, jnp.where(lane == 0, lroll(edge, 64), inner[n]))
+        out[n] = jnp.where(lane == 127, to_last(edge), jnp.where(lane == 0, to_first(edge), inner[n]))
     zero = jnp.zeros((8, 128), F32)
 
     def backward(step, low):
@@ -624,8 +672,7 @@
     lax.fori_loop(0, K // CHUNK, backward, [zero] * 6)
 
 
-def combine(parts, after, out):
-    del after
+def combine(parts, out):
     out[...] = jnp.broadcast_to(jnp.sum(parts[...], axis=0, keepdims=True), out.shape)
 
 
@@ -750,36 +797,38 @@
         rec_far = lax.ppermute(pay_far, "lon", pairs_far)
         rec_near = lax.ppermute(pay_near, "lon", pairs_near)
         chunked = (K // CHUNK, CHUNK)
-        scratch = [(*chunked, 2, 8, 128), (2, *chunked, 2, 8, 128), (10, 8, 128)]
         inner, flux_inner = kernel(
             momentum_inner,
             [VMEM] * 5,
             [(2 * K, 8, 128), (4, 8, 128)],
-            scratch=scratch,
+            scratch=[(*chunked, 2, 8, 128), (2, *chunked, 2, 8, 128), (10, 8, 128)],
             flops=10_000_000,
             nbytes=6_000_000,
         )(*own, rows, row_x)
         mixed, moments = kernel(
             momentum_entry,
-            [VMEM] * 8 + [ANY] * 2,
+            [VMEM] * 7 + [ANY] * 2,
             [(2 * K + 8, 8, 128), (stages[0][1], 128)],
-            scratch=scratch + [(20, 8, 128), (6, 8, 128), (2, LON_WIDE, 8, 128)],
-        )(*own, rows, row_x, flux_inner, rec_far, rec_near, rec_row_b, rec_row_a)
+            scratch=[
+                (GROUPS, 8, 128), (K // CHUNK, 2, 8, 128), (2, K // CHUNK, 2, 8, 128),
+                (K, 2, 8, 128), (2, K, 2, 8, 128), (20, 8, 128),
+            ],
+        )(flat, rows, flux_inner, pay_far, pay_near, rec_far, rec_near, rec_row_b, rec_row_a)
         (first_groups, _), (second_groups, second_size) = stages
         parts = lax.all_to_all(moments, both, 0, 0, axis_index_groups=first_groups, tiled=True)
+        (parts,) = kernel(combine, [VMEM], [(second_size, 128)])(parts)
+        sent = parts
+        parts = lax.all_to_all(parts, both, 0, 0, axis_index_groups=second_groups, tiled=True)
         gain, done = kernel(
             tracers_down,
-            [VMEM] * 8,
+            [VMEM] * 8 + [ANY],
             [(*chunked, 8, 128), (6, *chunked, 8, 128)],
             flops=10_000_000,
             nbytes=6_000_000,
-        )(tracer, diffusivity, flat, mixed, rec_row_b, rec_row_a, rec_far, rec_near)
-        (parts,) = kernel(combine, [VMEM, ANY], [(second_size, 128)])(parts, gain)
-        sent = parts
-        parts = lax.all_to_all(parts, both, 0, 0, axis_index_groups=second_groups, tiled=True)
+        )(tracer, diffusivity, flat, mixed, rec_row_b, rec_row_a, rec_far, rec_near, sent)
         (state_out,) = kernel(
-            tracers_up, [VMEM] * 4 + [ANY], [(8 * K, 8, 128)], flops=10_000_000, nbytes=6_000_000
-        )(gain, done, inner, mixed, sent)
+            tracers_up, [VMEM] * 4, [(8 * K, 8, 128)], flops=10_000_000, nbytes=6_000_000
+        )(gain, done, inner, mixed)
         (surface,) = kernel(finish, [VMEM] * 2, [(8, 128)])(parts, mixed)
         return state_out.reshape(8, K, 8, 128), surface
 
@@ -787,10 +836,10 @@
 
 
 def momentum_entry(*refs):
-    inputs, outputs, scratch = refs[:8], refs[10:12], refs[12:]
+    inputs, outputs, scratch = refs[:7], refs[9:11], refs[11:]
     mixed, moments = outputs
     momentum(*inputs, mixed, moments, *scratch)
-    planes2 = scratch[3]
+    planes2 = scratch[5]
     for face in range(4):
         mixed[AROUND + face] = planes2[4 * face]
 

time: 85.8 us -> 83.6 us (0.974)
  blocking collectives: 0 us -> 13.6 us
  starting transfers between devices: 55.6 us -> 49.6 us
  waiting for transfers between devices: 13 us -> 7.91 us
  local copies, waits for them, and re-layouts: 2.67 us -> 0.03 us
  Pallas kernels: 13.2 us -> 11.3 us
    all_to_all x0 -> x1, blocking collectives: none -> 13.6 us  [local(): lax.all_to_all(moments, both, 0, 0, axis_index_groups=first_groups, tiled...]
    all_to_all x1 -> x0, starting transfers between devices: 6.81 us -> none  [local(): lax.all_to_all(moments, both, 0, 0, axis_index_groups=first_groups, tiled...]
    all_to_all x1 -> x0, waiting for transfers between devices: 4.16 us -> none  [local(): lax.all_to_all(moments, both, 0, 0, axis_index_groups=first_groups, tiled...]
    unnamed x14 -> x10, local copies, waits for them, and re-layouts: 2.67 us -> 0.03 us
    pallas_call x4, Pallas kernels: 7.33 us -> 5.8 us  [the longest x1 1.85 us: local(): kernel(tracers_down, [VMEM] * 8 + [ANY], [(*chunked, 8, 128), (6, *chunke...]
    all_to_all x1, waiting for transfers between devices: 8.87 us -> 7.9 us  [local(): lax.all_to_all(parts, both, 0, 0, axis_index_groups=second_groups, tiled=...]
  transfers between devices with their start and end apart: 8 -> 7, of which waited for: 2 -> 1; matrix products, arithmetic and copies ran while one was open for 0% -> 0% of each run, Pallas kernels for 7% -> 7%
where the time goes in v5:
time: 83.6 us; the launch traced here: 83.2 us
  starting transfers between devices  49.6 us (59%)
  blocking collectives  13.6 us (16%)
  Pallas kernels  11.3 us (14%)
  waiting for transfers between devices  7.91 us (9%)
  between operations  0.85 us (1%)
    ppermute x1, starting transfers between devices, local(): rec_far = lax.ppermute(pay_far, 'lon', pairs_far)  17 us
    all_to_all x1, starting transfers between devices, local(): lax.all_to_all(parts, both, 0, 0, axis_index_groups=second_groups, tiled=...  16.2 us
    all_to_all x1, blocking collectives, local(): lax.all_to_all(moments, both, 0, 0, axis_index_groups=first_groups, tiled...  13.6 us
    all_to_all x1, waiting for transfers between devices, local(): lax.all_to_all(parts, both, 0, 0, axis_index_groups=second_groups, tiled=...  7.9 us
    ppermute x1, starting transfers between devices, local(): rec_a = lax.ppermute(pay_a, both, pairs_a)  6.39 us
    ppermute x1, starting transfers between devices, local(): rec_row_a = lax.ppermute(row_a, both, pairs_a)  5.62 us
    ppermute x1, starting transfers between devices, local(): rec_near = lax.ppermute(pay_near, 'lon', pairs_near)  2.88 us
    pallas_call x1, Pallas kernels, local(): kernel(pack_lat, [ANY] * 5, [(LAT_TILES, 8, 128), (ROW_X, 8, 128), (96 *...  2.27 us
  transfers between devices with their start and end apart: 7, of which 1 were waited for; matrix products, arithmetic and copies ran while one was open for 0% of the time, Pallas kernels for 7%

profile of v5, /device:TPU:1, one launch (start us, length us, event | category | flops | bytes accessed | tf_op | source)
XLA Modules:
  0.0 83.2 jit_solution(12439864880709586428)
XLA Ops:
  0.6 2.3 %shard_map.78 = (f32[79,8,128]{2,1,0:T(8,128)}, f32[73,8,128]{2,1,0:T(8,128)}, f32[768,128]{1,0:T(8,128)}, f32[47,8,128]{2,1,0:T(8,128)}, f32[3,8,128]{2,1,0:T(8,128)}) custom-call(f32[3072,128]{1,0:T(8,128)} %bitcast.10, f32[47,8,128]{2,1,0:T(8,128)} %visc_any.1, s32[8,128]{1,0:T(8,128)} %wet_any.1, f32[8,128]{1,0:T(8,128)} %storage_any.1, f32[8,128]{1,0:T(8,128)} %surf_any.1), custom_call_target="tpu_custom_call" | custom-call | tf_op jit(solution)/shard_map/pallas_call | solution.py:767
  2.9 0.0 copy-start.1
  2.9 0.8 collective-permute-start
  3.8 6.4 %collective-permute-start.1 = (f32[73,8,128]{2,1,0:T(8,128)}, f32[73,8,128]{2,1,0:T(8,128)S(1)}, u32[]{:S(2)}, u32[]{:S(2)}) collective-permute-start(f32[73,8,128]{2,1,0:T(8,128)} %get-tuple-element.27), channel_id=1, source_target_pairs={{0,16},{1,17},{2,18},{3,19},{4,20},{5,21},{6,22},{7,23},{8,24},{9,... | collective-permute-start | bytes 897032 | tf_op jit(solution)/shard_map/ppermute | solution.py:781
  10.2 0.7 shard_map.77
  10.9 0.7 collective-permute-start.4
  11.5 5.6 %collective-permute-start.5 = (f32[36,8,128]{2,1,0:T(8,128)S(1)}, f32[36,8,128]{2,1,0:T(8,128)S(1)}, u32[]{:S(2)}, u32[]{:S(2)}) collective-permute-start(f32[36,8,128]{2,1,0:T(8,128)S(1)} %get-tuple-element.36), channel_id=1, source_target_pairs={{0,16},{1,17},{2,18},{3,19},{4,20},{5,21},{6,22},{7,23},{8,24},{9,... | collective-permute-start | bytes 442376 | tf_op jit(solution)/shard_map/ppermute | solution.py:791
  17.2 0.0 collective-permute-done.1.rec_a
  17.2 0.0 collective-permute-done.rec_b
  17.2 0.0 copy-start.4
  17.2 0.4 shard_map.79
  17.6 17.0 %collective-permute-start.2 = (f32[13,8,128]{2,1,0:T(8,128)S(1)}, f32[13,8,128]{2,1,0:T(8,128)S(1)}, u32[]{:S(2)}, u32[]{:S(2)}) collective-permute-start(f32[13,8,128]{2,1,0:T(8,128)S(1)} %get-tuple-element.33.refs_3_), channel_id=1, source_target_pairs={{0,15},{1,2},{2,1},{3,4},{4,3},{5,6},{6,5},{7,8},{8,7},{9,10},{10,... | collective-permute-start | bytes 159752 | tf_op jit(solution)/shard_map/ppermute | solution.py:797
  34.6 2.9 %collective-permute-start.3 = (f32[13,8,128]{2,1,0:T(8,128)S(1)}, f32[13,8,128]{2,1,0:T(8,128)S(1)}, u32[]{:S(2)}, u32[]{:S(2)}) collective-permute-start(f32[13,8,128]{2,1,0:T(8,128)S(1)} %get-tuple-element.34.refs_4_), channel_id=1, source_target_pairs={{0,1},{1,0},{2,3},{3,2},{4,5},{5,4},{6,7},{7,6},{8,9},{9,8},{10,11... | collective-permute-start | bytes 159752 | tf_op jit(solution)/shard_map/ppermute | solution.py:798
  37.5 1.4 %shard_map.80 = (f32[96,8,128]{2,1,0:T(8,128)S(1)}, f32[4,8,128]{2,1,0:T(8,128)S(1)}) custom-call(f32[768,128]{1,0:T(8,128)S(1)} %copy-done.1, f32[47,8,128]{2,1,0:T(8,128)S(1)} %copy-done.2, f32[3,8,128]{2,1,0:T(8,128)S(1)} %copy-done.3, f32[146,8,128]{2,1,0:T(8,128)S(1)} %get-tuple-element.30.rows.refs_1_, f32[6,8,128]{2,1,0:T(8,128)S(1)} %get-tuple-element.31.row_x), custom_call_target="tpu_custom_call" | custom-call | flops 10000000 | bytes 6000000 | tf_op jit(solution)/shard_map/pallas_call | solution.py:800
  38.9 0.0 collective-permute-done.5.refs_8_.rec_a
  38.9 0.0 collective-permute-done.2.refs_5_.far
  38.9 1.8 %shard_map.81 = (f32[104,8,128]{2,1,0:T(8,128)S(1)}, f32[32,128]{1,0:T(8,128)S(1)}) custom-call(f32[3,8,128]{2,1,0:T(8,128)S(1)} %copy-done.3, f32[146,8,128]{2,1,0:T(8,128)S(1)} %get-tuple-element.30.rows.refs_1_, f32[4,8,128]{2,1,0:T(8,128)S(1)} %get-tuple-element.32.refs_2_, f32[13,8,128]{2,1,0:T(8,128)S(1)} %get-tuple-element.33.refs_3_, ...), custom_call_target="tpu_custom_call" | custom-call | tf_op jit(solution)/shard_map/pallas_call | solution.py:808
  40.8 13.6 %all_to_all.22 = f32[32,1,128]{2,1,0:T(1,128)S(1)} all-to-all(f32[32,1,128]{2,1,0:T(1,128)S(1)} %bitcast.14), channel_id=1, replica_groups={{0,1,4,5,8,9,12,13,16,17,20,21,24,25,28,29,32,33,36,37,40,41,44,45,48,4..., dimensions={0} | all-to-all | bytes 32768 | tf_op jit(solution)/shard_map/all_to_all | solution.py:818
  54.3 0.6 shard_map.82.after
  54.9 16.2 %all-to-all-start.1 = ((f32[16,1,128]{2,1,0:T(1,128)}), f32[16,1,128]{2,1,0:T(1,128)S(1)}, u32[]{:S(2)}, u32[]{:S(2)}) async-start(f32[16,1,128]{2,1,0:T(1,128)} %bitcast.6), calls=%async_computation.1 | async-start | bytes 16384 | tf_op jit(solution)/shard_map/all_to_all | solution.py:821
  71.2 1.9 %shard_map.83 = (f32[6,8,8,128]{3,2,1,0:T(8,128)S(1)}, f32[6,6,8,8,128]{4,3,2,1,0:T(8,128)S(1)}) custom-call(f32[2304,128]{1,0:T(8,128)S(1)} %get-tuple-element.22.state, f32[47,8,128]{2,1,0:T(8,128)S(1)} %copy-done.4, f32[3,8,128]{2,1,0:T(8,128)S(1)} %copy-done.3, f32[104,8,128]{2,1,0:T(8,128)S(1)} %get-tuple-element.37.mixed, ...), custom_call_target="tpu_custom_call" | custom-call | flops 10000000 | bytes 6000000 | tf_op jit(solution)/shard_map/pallas_call | solution.py:822
  73.0 1.5 %shard_map.84 = f32[384,8,128]{2,1,0:T(8,128)} custom-call(f32[6,8,8,128]{3,2,1,0:T(8,128)S(1)} %get-tuple-element.39.gain, f32[6,6,8,8,128]{4,3,2,1,0:T(8,128)S(1)} %get-tuple-element.40.done, f32[96,8,128]{2,1,0:T(8,128)S(1)} %get-tuple-element.41.inner, f32[104,8,128]{2,1,0:T(8,128)S(1)} %get-tuple-element.37.mixed), custom_call_target="tpu_custom_call" | custom-call | flops 10000000 | bytes 6000000 | tf_op jit(solution)/shard_map/pallas_call | solution.py:829
  74.6 7.9 %all-to-all-done.1 = f32[16,1,128]{2,1,0:T(1,128)S(1)} async-done(((f32[16,1,128]{2,1,0:T(1,128)}), f32[16,1,128]{2,1,0:T(1,128)S(1)}, u32[]{:S(2)}, u32[]{:S(2)}) %all-to-all-start.1) | async-done | bytes 8224 | tf_op jit(solution)/shard_map/all_to_all | solution.py:821
  82.5 0.7 shard_map.85
  (10 shorter events, 0.0 us)
Async XLA Ops:
  0.6 9.5 %copy-start = (f32[8,48,8,128]{3,2,1,0:T(8,128)S(1)}, f32[8,48,8,128]{3,2,1,0:T(8,128)}, u32[]{:S(2)}) copy-start(f32[8,48,8,128]{3,2,1,0:T(8,128)} %param.6) | copy-start | bytes 4718596
  2.9 14.3 %copy-start.1 = (f32[768,128]{1,0:T(8,128)S(1)}, f32[768,128]{1,0:T(8,128)}, u32[]{:S(2)}) copy-start(f32[768,128]{1,0:T(8,128)} %get-tuple-element.24.state) | copy-start | bytes 1179652
  2.9 14.3 %copy-start.2 = (f32[47,8,128]{2,1,0:T(8,128)S(1)}, f32[47,8,128]{2,1,0:T(8,128)}, u32[]{:S(2)}) copy-start(f32[47,8,128]{2,1,0:T(8,128)} %get-tuple-element.25.visc) | copy-start | bytes 577540
  2.9 14.3 %copy-start.3 = (f32[3,8,128]{2,1,0:T(8,128)S(1)}, f32[3,8,128]{2,1,0:T(8,128)}, u32[]{:S(2)}) copy-start(f32[3,8,128]{2,1,0:T(8,128)} %get-tuple-element.23.flat.refs_0_) | copy-start | bytes 36868
  2.9 14.2 %collective-permute-start = (f32[79,8,128]{2,1,0:T(8,128)}, f32[79,8,128]{2,1,0:T(8,128)S(1)}, u32[]{:S(2)}, u32[]{:S(2)}) collective-permute-start(f32[79,8,128]{2,1,0:T(8,128)} %get-tuple-element.26), channel_id=1, source_target_pairs={{16,32},{17,33},{18,34},{19,35},{20,36},{21,37},{22,38},{23,39},{2... | collective-permute-start | bytes 970760 | tf_op jit(solution)/shard_map/ppermute | solution.py:780
  3.8 13.4 %collective-permute-start.1 = (f32[73,8,128]{2,1,0:T(8,128)}, f32[73,8,128]{2,1,0:T(8,128)S(1)}, u32[]{:S(2)}, u32[]{:S(2)}) collective-permute-start(f32[73,8,128]{2,1,0:T(8,128)} %get-tuple-element.27), channel_id=1, source_target_pairs={{0,16},{1,17},{2,18},{3,19},{4,20},{5,21},{6,22},{7,23},{8,24},{9,... | collective-permute-start | bytes 897032 | tf_op jit(solution)/shard_map/ppermute | solution.py:781
  10.9 28.0 %collective-permute-start.4 = (f32[36,8,128]{2,1,0:T(8,128)S(1)}, f32[36,8,128]{2,1,0:T(8,128)S(1)}, u32[]{:S(2)}, u32[]{:S(2)}) collective-permute-start(f32[36,8,128]{2,1,0:T(8,128)S(1)} %get-tuple-element.35), channel_id=1, source_target_pairs={{16,32},{17,33},{18,34},{19,35},{20,36},{21,37},{22,38},{23,39},{2... | collective-permute-start | bytes 442376 | tf_op jit(solution)/shard_map/ppermute | solution.py:790
  11.5 27.4 %collective-permute-start.5 = (f32[36,8,128]{2,1,0:T(8,128)S(1)}, f32[36,8,128]{2,1,0:T(8,128)S(1)}, u32[]{:S(2)}, u32[]{:S(2)}) collective-permute-start(f32[36,8,128]{2,1,0:T(8,128)S(1)} %get-tuple-element.36), channel_id=1, source_target_pairs={{0,16},{1,17},{2,18},{3,19},{4,20},{5,21},{6,22},{7,23},{8,24},{9,... | collective-permute-start | bytes 442376 | tf_op jit(solution)/shard_map/ppermute | solution.py:791
  17.2 53.9 %copy-start.4 = (f32[47,8,128]{2,1,0:T(8,128)S(1)}, f32[47,8,128]{2,1,0:T(8,128)}, u32[]{:S(2)}) copy-start(f32[47,8,128]{2,1,0:T(8,128)} %diff.1) | copy-start | bytes 577540
  17.6 21.3 %collective-permute-start.2 = (f32[13,8,128]{2,1,0:T(8,128)S(1)}, f32[13,8,128]{2,1,0:T(8,128)S(1)}, u32[]{:S(2)}, u32[]{:S(2)}) collective-permute-start(f32[13,8,128]{2,1,0:T(8,128)S(1)} %get-tuple-element.33.refs_3_), channel_id=1, source_target_pairs={{0,15},{1,2},{2,1},{3,4},{4,3},{5,6},{6,5},{7,8},{8,7},{9,10},{10,... | collective-permute-start | bytes 159752 | tf_op jit(solution)/shard_map/ppermute | solution.py:797
  34.6 4.3 %collective-permute-start.3 = (f32[13,8,128]{2,1,0:T(8,128)S(1)}, f32[13,8,128]{2,1,0:T(8,128)S(1)}, u32[]{:S(2)}, u32[]{:S(2)}) collective-permute-start(f32[13,8,128]{2,1,0:T(8,128)S(1)} %get-tuple-element.34.refs_4_), channel_id=1, source_target_pairs={{0,1},{1,0},{2,3},{3,2},{4,5},{5,4},{6,7},{7,6},{8,9},{9,8},{10,11... | collective-permute-start | bytes 159752 | tf_op jit(solution)/shard_map/ppermute | solution.py:798
  54.9 27.5 %all-to-all-start.1 = ((f32[16,1,128]{2,1,0:T(1,128)}), f32[16,1,128]{2,1,0:T(1,128)S(1)}, u32[]{:S(2)}, u32[]{:S(2)}) async-start(f32[16,1,128]{2,1,0:T(1,128)} %bitcast.6), calls=%async_computation.1 | async-start | bytes 16384 | tf_op jit(solution)/shard_map/all_to_all | solution.py:821

commit v6 on v5

--- a/solution.py
+++ b/solution.py
@@ -16,13 +16,15 @@
 F32 = jnp.float32
 
 PAIR_UV = 0
-PAIR_VISC = 48
-PAIR_SURF = 72
-ROW_X = 73
-LAT_TILES = 79
+PAIR_STRIP = 48
+PAIR_SURF = 50
+ROW_X = 51
+LAT_TILES = 57
 ROW_TILES = 36
+PAIR_VISC = 36
+SECOND_TILES = 60
 PL_U, PL_V, PL_VISC, PL_WET, PL_STO, PL_SUR = 0, 48, 96, 143, 144, 145
-PLANES = 146
+BESIDE, BESIDE_WET = 99, 96
 HALO, CROSS = 152, 298
 GROUPS = 38
 LON_WIDE = 10
@@ -52,6 +54,10 @@
     return pltpu.roll(x, shift, 0)
 
 
+def strip_slot():
+    return ((lane_iota() + 4) >> 3) & 15
+
+
 def flip_lanes(x):
     return jnp.take_along_axis(x, 127 - lane_iota(), axis=1)
 
@@ -77,7 +83,7 @@
 
 def pack_lat(
     state_any, visc_any, wet_any, storage_any, surf_any,
-    out_b, out_a, out_state, out_visc, out_flat,
+    out_b, out_a, out_state, out_flat,
     pay_b, pay_a, state, visc, flat, wet, sems, out_sems,
 ):
     odd, top, _ = whereabouts()
@@ -98,27 +104,34 @@
     def pack(tiles):
         @pl.when(jnp.logical_not(top))
         def _():
-            for tile, first, second, _ in tiles():
+            for tile, first, second, _ in tiles(False):
                 rolled = sroll(second, 4)
                 pay_a[tile] = jnp.where(keep, first, rolled)
                 pay_b[tile] = jnp.where(keep, rolled, first)
 
         @pl.when(top)
         def _():
-            for tile, first, second, sign in tiles():
-                rolled = sroll(second, 4)
-                pay_a[tile] = jnp.where(keep, first, rolled)
-                turned = flip_rows(flip_lanes(jnp.where(keep, rolled, first)))
+            for tile, first, second, _ in tiles(False):
+                pay_a[tile] = jnp.where(keep, first, sroll(second, 4))
+            for tile, first, second, sign in tiles(True):
+                turned = flip_rows(flip_lanes(jnp.where(keep, sroll(second, 4), first)))
                 pay_b[tile] = -turned if sign < 0 else turned
 
-    def velocities():
+    def velocities(mirrored):
+        del mirrored
         for k in range(48):
             yield k, state[k * 8 : k * 8 + 8, :], state[(k + 48) * 8 : (k + 48) * 8 + 8, :], -1.0
 
-    def others():
-        for m in range(23):
-            yield PAIR_VISC + m, visc[2 * m], visc[2 * m + 1], 1.0
-        yield PAIR_VISC + 23, visc[46], flat[0], 1.0
+    def strip(t, mirrored):
+        tile = jnp.zeros((8, 128), F32)
+        for i in range(16 if t < 2 else 15):
+            slot = (16 - i) % 16 if mirrored else i
+            tile = jnp.where(strip_slot() == slot, lroll(visc[16 * t + i], 8 * slot) if slot else visc[16 * t + i], tile)
+        return tile
+
+    def others(mirrored):
+        yield PAIR_STRIP, strip(0, mirrored), strip(1, mirrored), 1.0
+        yield PAIR_STRIP + 1, strip(2, mirrored), flat[0], 1.0
         yield PAIR_SURF, flat[1], flat[2], 1.0
 
     def send(source, target, sem):
@@ -135,7 +148,7 @@
     for copy in copies[2:]:
         copy.wait()
     flat[0] = wet[...].astype(F32)
-    leaving += [send(visc, out_visc, 3), send(flat, out_flat, 4)]
+    leaving.append(send(flat, out_flat, 3))
     pack(others)
     least = jnp.broadcast_to(jnp.minimum(flat[0, 3:4, :], flat[0, 4:5, :]), (8, 128))
     for m in range(6):
@@ -146,12 +159,12 @@
         diff = jnp.where(level < least, row3 - row4, 0.0)
         pay_b[ROW_X + m] = -flip_lanes(diff)
     rest_b, rest_a = (pl.ds(PAIR_VISC, count - PAIR_VISC) for count in (LAT_TILES, ROW_X))
-    leaving += [send(pay_b.at[rest_b], out_b.at[rest_b], 5), send(pay_a.at[rest_a], out_a.at[rest_a], 6)]
+    leaving += [send(pay_b.at[rest_b], out_b.at[rest_b], 4), send(pay_a.at[rest_a], out_a.at[rest_a], 5)]
     for copy in leaving:
         copy.wait()
 
 
-def pack_tracers(state_any, pay_b, pay_a, far, near, tracer, sems):
+def pack_tracers(state_any, visc, pay_b, pay_a, far, near, tracer, sems):
     half = 144 * 8
     copies = [
         pltpu.make_async_copy(
@@ -165,6 +178,7 @@
         copy.wait()
     odd, top, odd_lon = whereabouts()
     lane = lane_iota()
+    keep = (sub_iota() < 4).astype(jnp.int32) == odd
 
     def rows_of(t):
         start = 8 * t * 8
@@ -174,14 +188,21 @@
         row0, row7 = rows_of(t)
         pay_a[t] = jnp.where(odd == 1, row0, row7)
         pay_b[t] = jnp.where(odd == 1, row7, row0)
+    for m in range(24):
+        first, rolled = visc[2 * m], sroll(visc[min(2 * m + 1, 46)], 4)
+        pay_a[PAIR_VISC + m] = jnp.where(keep, first, rolled)
+        pay_b[PAIR_VISC + m] = jnp.where(keep, rolled, first)
 
     @pl.when(top)
     def _():
         for t in range(ROW_TILES):
             pay_b[t] = flip_lanes(rows_of(t)[1])
+        for m in range(24):
+            first, rolled = visc[2 * m], sroll(visc[min(2 * m + 1, 46)], 4)
+            pay_b[PAIR_VISC + m] = flip_rows(flip_lanes(jnp.where(keep, rolled, first)))
 
     def scalar(n):
-        return tracer[n * 8 : n * 8 + 8, :]
+        return tracer[n * 8 : n * 8 + 8, :], 0
 
     for tile in range(3):
         planes = [functools.partial(scalar, n) for n in range(128 * tile, min(128 * tile + 128, 288))]
@@ -198,26 +219,32 @@
     for j, load in enumerate(planes):
         if load is None:
             continue
-        x = load()
-        x = lroll(x, j * width) if j else x
+        x, offset = load()
+        shift = (j * width - offset) & 127
+        x = lroll(x, shift) if shift else x
         west = jnp.where(slot_of == j, x, west)
         east = jnp.where(slot_of == (j - 1) % slots, x, east)
     return east, west
 
 
-def lon_planes(state, visc, flat, rows, row_x):
+def lon_planes(state, visc, flat, rows, strips, row_x):
     def plane(n):
         if n < 96:
-            return state[n * 8 : n * 8 + 8, :]
+            return state[n * 8 : n * 8 + 8, :], 0
         if n < 143:
-            return visc[n - 96]
+            return visc[n - 96], 0
         if n < 146:
-            return flat[n - 143]
+            return flat[n - 143], 0
         if n < HALO:
-            return flat[0]
+            return flat[0], 0
+        if n < HALO + 96:
+            return rows[n - HALO], 0
+        if n < HALO + PL_WET:
+            k = n - HALO - PL_VISC
+            return strips[k // 16], 8 * (k % 16)
         if n < CROSS:
-            return rows[n - HALO]
-        return row_x[n - CROSS]
+            return rows[n - HALO - PL_WET + BESIDE_WET], 0
+        return row_x[n - CROSS], 0
 
     lane = lane_iota()
     for tile in range(LON_WIDE):
@@ -227,7 +254,7 @@
 
 
 def pack_lon(
-    state, visc, flat, rec_b, rec_a, far_tracers, near_tracers, rows, row_x, far, near
+    state, visc, flat, rec_b, rec_a, far_tracers, near_tracers, rows, row_x, far, near, strips
 ):
     odd, _, odd_lon = whereabouts()
     sub = sub_iota()
@@ -241,16 +268,12 @@
         first, second = unpair(k)
         rows[PL_U + k] = first
         rows[PL_V + k] = second
-    for m in range(24):
-        first, second = unpair(PAIR_VISC + m)
-        rows[PL_VISC + 2 * m] = first
-        rows[PL_VISC + 2 * m + 1] = second
-    first, second = unpair(PAIR_SURF)
-    rows[PL_STO] = first
-    rows[PL_SUR] = second
+    strips[0], strips[1] = unpair(PAIR_STRIP)
+    strips[2], rows[BESIDE_WET] = unpair(PAIR_STRIP + 1)
+    rows[BESIDE_WET + 1], rows[BESIDE_WET + 2] = unpair(PAIR_SURF)
     for m in range(6):
         row_x[m] = rec_b[ROW_X + m]
-    for tile, (east, west) in lon_planes(state, visc, flat, rows, row_x):
+    for tile, (east, west) in lon_planes(state, visc, flat, rows, strips, row_x):
         far[tile] = jnp.where(odd_lon == 1, east, west)
         near[tile] = jnp.where(odd_lon == 1, west, east)
     for tile in range(3):
@@ -358,16 +381,19 @@
     return flux
 
 
-def momentum_inner(state, visc, flat, rows, row_x, mixed, flux_out, gain, done, counts):
-    _, top, _ = whereabouts()
+def momentum_inner(state, visc, flat, rows, row_x, rec_b, rec_a, mixed, flux_out, gain, done, counts):
+    odd, top, _ = whereabouts()
+    keep_rows = (sub_iota() < 4).astype(jnp.int32) != odd
 
     def load(field, chunk, i):
         n = 48 * field + CHUNK * chunk + i
         return [state[pl.ds(n * 8, 8), :], rows[n]]
 
     def coefficient_at(chunk, i):
-        k = CHUNK * chunk + i
-        return [visc[jnp.minimum(k, 46)], rows[PL_VISC + k]]
+        tile = PAIR_VISC + CHUNK // 2 * chunk + i // 2
+        a, b = rec_a[tile], rec_b[tile]
+        beside = sroll(jnp.where(keep_rows, b, a), 4) if i % 2 else jnp.where(keep_rows, a, b)
+        return [visc[jnp.minimum(CHUNK * chunk + i, 46)], beside]
 
     def cross_row(chunk, i):
         return jnp.broadcast_to(row_x[chunk, i : i + 1, :], (8, 128))
@@ -375,7 +401,7 @@
     def keep(field, k, tile):
         mixed[48 * field + k] = tile
 
-    flux = columns(load, cross_row, coefficient_at, [flat[0], rows[PL_WET]], top, counts, gain, done, keep)
+    flux = columns(load, cross_row, coefficient_at, [flat[0], rows[BESIDE_WET]], top, counts, gain, done, keep)
     for field in range(2):
         for j in range(2):
             flux_out[2 * field + j] = flux[field][j]
@@ -503,7 +529,7 @@
 
     def four(n, own):
         pair = [window(n), window(n + HALO)]
-        return [own, rows[n]] + [
+        return [own, rows[n - PL_WET + BESIDE_WET]] + [
             jnp.where(valid, jnp.where(lane < 64, to_last(e), to_first(e)), 0.0) for e in pair
         ]
 
@@ -764,56 +790,57 @@
 
     def local(ocean_state, viscosity, diffusivity, wet_levels, storage, surface_old):
         state = ocean_state.reshape(8 * K * 8, 128)
-        pay_b, pay_a, uv, visc, flat = kernel(
+        pay_b, pay_a, uv, flat = kernel(
             pack_lat,
             [ANY] * 5,
-            [(LAT_TILES, 8, 128), (ROW_X, 8, 128), (96 * 8, 128), (47, 8, 128), (3, 8, 128)],
+            [(LAT_TILES, 8, 128), (ROW_X, 8, 128), (96 * 8, 128), (3, 8, 128)],
             scratch=[
                 (LAT_TILES, 8, 128), (ROW_X, 8, 128),
                 (96 * 8, 128), (47, 8, 128), (3, 8, 128),
-                pltpu.VMEM((8, 128), jnp.int32), pltpu.SemaphoreType.DMA((6,)), pltpu.SemaphoreType.DMA((7,)),
+                pltpu.VMEM((8, 128), jnp.int32), pltpu.SemaphoreType.DMA((6,)), pltpu.SemaphoreType.DMA((6,)),
             ],
             out_spec=ANY,
             limit=FIRST_LIMIT,
         )(state, viscosity, wet_levels, storage, surface_old)
-        own = (uv, visc, flat)
+        own = (uv, viscosity, flat)
         rec_b = lax.ppermute(pay_b, both, pairs_b)
         rec_a = lax.ppermute(pay_a, both, pairs_a)
         row_b, row_a, far_tracers, near_tracers, tracer = kernel(
             pack_tracers,
-            [ANY],
-            [(ROW_TILES, 8, 128)] * 2 + [(3, 8, 128)] * 2 + [(288 * 8, 128)],
+            [ANY, VMEM],
+            [(SECOND_TILES, 8, 128)] * 2 + [(3, 8, 128)] * 2 + [(288 * 8, 128)],
             scratch=[pltpu.SemaphoreType.DMA((2,))],
             flops=1_000_000,
             nbytes=2_000_000,
-        )(state)
+        )(state, viscosity)
         rec_row_b = lax.ppermute(row_b, both, pairs_b)
         rec_row_a = lax.ppermute(row_a, both, pairs_a)
         rows, row_x, pay_far, pay_near = kernel(
             pack_lon,
             [VMEM] * 7,
-            [(PLANES, 8, 128), (6, 8, 128), (LON_TILES, 8, 128), (LON_TILES, 8, 128)],
+            [(BESIDE, 8, 128), (6, 8, 128), (LON_TILES, 8, 128), (LON_TILES, 8, 128)],
+            scratch=[(3, 8, 128)],
         )(*own, rec_b, rec_a, far_tracers, near_tracers)
         rec_far = lax.ppermute(pay_far, "lon", pairs_far)
         rec_near = lax.ppermute(pay_near, "lon", pairs_near)
         chunked = (K // CHUNK, CHUNK)
         inner, flux_inner = kernel(
             momentum_inner,
-            [VMEM] * 5,
+            [VMEM] * 7,
             [(2 * K, 8, 128), (4, 8, 128)],
             scratch=[(*chunked, 2, 8, 128), (2, *chunked, 2, 8, 128), (10, 8, 128)],
             flops=10_000_000,
             nbytes=6_000_000,
-        )(*own, rows, row_x)
+        )(*own, rows, row_x, rec_row_b, rec_row_a)
         mixed, moments = kernel(
             momentum_entry,
-            [VMEM] * 7 + [ANY] * 2,
+            [VMEM] * 7,
             [(2 * K + 8, 8, 128), (stages[0][1], 128)],
             scratch=[
                 (GROUPS, 8, 128), (K // CHUNK, 2, 8, 128), (2, K // CHUNK, 2, 8, 128),
                 (K, 2, 8, 128), (2, K, 2, 8, 128), (20, 8, 128),
             ],
-        )(flat, rows, flux_inner, pay_far, pay_near, rec_far, rec_near, rec_row_b, rec_row_a)
+        )(flat, rows, flux_inner, pay_far, pay_near, rec_far, rec_near)
         (first_groups, _), (second_groups, second_size) = stages
         parts = lax.all_to_all(moments, both, 0, 0, axis_index_groups=first_groups, tiled=True)
         (parts,) = kernel(combine, [VMEM], [(second_size, 128)])(parts)
@@ -836,7 +863,7 @@
 
 
 def momentum_entry(*refs):
-    inputs, outputs, scratch = refs[:7], refs[9:11], refs[11:]
+    inputs, outputs, scratch = refs[:7], refs[7:9], refs[9:]
     mixed, moments = outputs
     momentum(*inputs, mixed, moments, *scratch)
     planes2 = scratch[5]

time: 83.6 us -> 83.3 us (level)
  no operation moved by 1% of the time
where the time goes in v6:
time: 83.3 us; the launch traced here: 82.9 us
  starting transfers between devices  49.5 us (59%)
  blocking collectives  13.4 us (16%)
  Pallas kernels  11.2 us (13%)
  waiting for transfers between devices  7.91 us (9%)
  between operations  0.85 us (1%)
    all_to_all x1, starting transfers between devices, local(): lax.all_to_all(parts, both, 0, 0, axis_index_groups=second_groups, tiled=...  16.7 us
    ppermute x1, starting transfers between devices, local(): rec_far = lax.ppermute(pay_far, 'lon', pairs_far)  16.2 us
    all_to_all x1, blocking collectives, local(): lax.all_to_all(moments, both, 0, 0, axis_index_groups=first_groups, tiled...  13.4 us
    all_to_all x1, waiting for transfers between devices, local(): lax.all_to_all(parts, both, 0, 0, axis_index_groups=second_groups, tiled=...  7.89 us
    ppermute x1, starting transfers between devices, local(): rec_a = lax.ppermute(pay_a, both, pairs_a)  6.39 us
    ppermute x1, starting transfers between devices, local(): rec_row_a = lax.ppermute(row_a, both, pairs_a)  5.61 us
    ppermute x1, starting transfers between devices, local(): rec_near = lax.ppermute(pay_near, 'lon', pairs_near)  3.07 us
    pallas_call x1, Pallas kernels, local(): kernel(pack_lat, [ANY] * 5, [(LAT_TILES, 8, 128), (ROW_X, 8, 128), (96 *...  2.2 us
  transfers between devices with their start and end apart: 7, of which 1 were waited for; matrix products, arithmetic and copies ran while one was open for 0% of the time, Pallas kernels for 7%

profile of v6, /device:TPU:1, one launch (start us, length us, event | category | flops | bytes accessed | tf_op | source)
XLA Modules:
  0.0 82.9 jit_solution(16235443720708423964)
XLA Ops:
  0.7 2.2 %shard_map.78 = (f32[57,8,128]{2,1,0:T(8,128)}, f32[51,8,128]{2,1,0:T(8,128)}, f32[768,128]{1,0:T(8,128)}, f32[3,8,128]{2,1,0:T(8,128)}) custom-call(f32[3072,128]{1,0:T(8,128)} %bitcast.10, f32[47,8,128]{2,1,0:T(8,128)} %visc.5, s32[8,128]{1,0:T(8,128)} %wet_any.1, f32[8,128]{1,0:T(8,128)} %storage_any.1, f32[8,128]{1,0:T(8,128)} %surf_any.1), custom_call_target="tpu_custom_call" | custom-call | tf_op jit(solution)/shard_map/pallas_call | solution.py:793
  2.9 0.0 copy-start.2
  2.9 0.8 collective-permute-start
  3.7 6.4 %collective-permute-start.1 = (f32[51,8,128]{2,1,0:T(8,128)}, f32[51,8,128]{2,1,0:T(8,128)S(1)}, u32[]{:S(2)}, u32[]{:S(2)}) collective-permute-start(f32[51,8,128]{2,1,0:T(8,128)} %get-tuple-element.25), channel_id=1, source_target_pairs={{0,16},{1,17},{2,18},{3,19},{4,20},{5,21},{6,22},{7,23},{8,24},{9,... | collective-permute-start | bytes 626696 | tf_op jit(solution)/shard_map/ppermute | solution.py:807
  10.1 0.7 shard_map.77
  10.8 0.7 collective-permute-start.2
  11.5 5.6 %collective-permute-start.3 = (f32[60,8,128]{2,1,0:T(8,128)S(1)}, f32[60,8,128]{2,1,0:T(8,128)S(1)}, u32[]{:S(2)}, u32[]{:S(2)}) collective-permute-start(f32[60,8,128]{2,1,0:T(8,128)S(1)} %get-tuple-element.31), channel_id=1, source_target_pairs={{0,16},{1,17},{2,18},{3,19},{4,20},{5,21},{6,22},{7,23},{8,24},{9,... | collective-permute-start | bytes 737288 | tf_op jit(solution)/shard_map/ppermute | solution.py:817
  17.1 0.0 collective-permute-done.1.rec_a
  17.2 0.0 copy-start.4
  17.2 0.4 shard_map.79
  17.6 16.2 %collective-permute-start.4 = (f32[13,8,128]{2,1,0:T(8,128)S(1)}, f32[13,8,128]{2,1,0:T(8,128)S(1)}, u32[]{:S(2)}, u32[]{:S(2)}) collective-permute-start(f32[13,8,128]{2,1,0:T(8,128)S(1)} %get-tuple-element.33.refs_3_), channel_id=1, source_target_pairs={{0,15},{1,2},{2,1},{3,4},{4,3},{5,6},{6,5},{7,8},{8,7},{9,10},{10,... | collective-permute-start | bytes 159752 | tf_op jit(solution)/shard_map/ppermute | solution.py:824
  33.8 3.1 %collective-permute-start.5 = (f32[13,8,128]{2,1,0:T(8,128)S(1)}, f32[13,8,128]{2,1,0:T(8,128)S(1)}, u32[]{:S(2)}, u32[]{:S(2)}) collective-permute-start(f32[13,8,128]{2,1,0:T(8,128)S(1)} %get-tuple-element.34.refs_4_), channel_id=1, source_target_pairs={{0,1},{1,0},{2,3},{3,2},{4,5},{5,4},{6,7},{7,6},{8,9},{9,8},{10,11... | collective-permute-start | bytes 159752 | tf_op jit(solution)/shard_map/ppermute | solution.py:825
  36.9 0.0 collective-permute-done.2.rec_b
  36.9 0.0 collective-permute-done.3.rec_a
  36.9 1.4 %shard_map.80 = (f32[96,8,128]{2,1,0:T(8,128)S(1)}, f32[4,8,128]{2,1,0:T(8,128)S(1)}) custom-call(f32[768,128]{1,0:T(8,128)S(1)} %copy-done.2, f32[47,8,128]{2,1,0:T(8,128)S(1)} %copy-done.1, f32[3,8,128]{2,1,0:T(8,128)S(1)} %copy-done.3, f32[99,8,128]{2,1,0:T(8,128)S(1)} %get-tuple-element.28.rows.refs_1_, f32[6,8,128]{2,1,0:T(8,128)S(1)} %get-tuple-element.29.row_x, ...), custom_call_target="tpu_custom_call" | custom-call | flops 10000000 | bytes 6000000 | tf_op jit(solution)/shard_map/pallas_call | solution.py:827
  38.3 0.0 collective-permute-done.4.refs_5_.far
  38.3 1.8 %shard_map.81 = (f32[104,8,128]{2,1,0:T(8,128)S(1)}, f32[32,128]{1,0:T(8,128)S(1)}) custom-call(f32[3,8,128]{2,1,0:T(8,128)S(1)} %copy-done.3, f32[99,8,128]{2,1,0:T(8,128)S(1)} %get-tuple-element.28.rows.refs_1_, f32[4,8,128]{2,1,0:T(8,128)S(1)} %get-tuple-element.32.refs_2_, f32[13,8,128]{2,1,0:T(8,128)S(1)} %get-tuple-element.33.refs_3_, ...), custom_call_target="tpu_custom_call" | custom-call | tf_op jit(solution)/shard_map/pallas_call | solution.py:835
  40.1 13.4 %all_to_all.22 = f32[32,1,128]{2,1,0:T(1,128)S(1)} all-to-all(f32[32,1,128]{2,1,0:T(1,128)S(1)} %bitcast.14), channel_id=1, replica_groups={{0,1,4,5,8,9,12,13,16,17,20,21,24,25,28,29,32,33,36,37,40,41,44,45,48,4..., dimensions={0} | all-to-all | bytes 32768 | tf_op jit(solution)/shard_map/all_to_all | solution.py:845
  53.6 0.6 shard_map.82.after
  54.2 16.7 %all-to-all-start.1 = ((f32[16,1,128]{2,1,0:T(1,128)}), f32[16,1,128]{2,1,0:T(1,128)S(1)}, u32[]{:S(2)}, u32[]{:S(2)}) async-start(f32[16,1,128]{2,1,0:T(1,128)} %bitcast.6), calls=%async_computation.1 | async-start | bytes 16384 | tf_op jit(solution)/shard_map/all_to_all | solution.py:848
  70.9 1.9 %shard_map.83 = (f32[6,8,8,128]{3,2,1,0:T(8,128)S(1)}, f32[6,6,8,8,128]{4,3,2,1,0:T(8,128)S(1)}) custom-call(f32[2304,128]{1,0:T(8,128)S(1)} %get-tuple-element.21.state, f32[47,8,128]{2,1,0:T(8,128)S(1)} %copy-done.4, f32[3,8,128]{2,1,0:T(8,128)S(1)} %copy-done.3, f32[104,8,128]{2,1,0:T(8,128)S(1)} %get-tuple-element.35.mixed, ...), custom_call_target="tpu_custom_call" | custom-call | flops 10000000 | bytes 6000000 | tf_op jit(solution)/shard_map/pallas_call | solution.py:849
  72.8 1.5 %shard_map.84 = f32[384,8,128]{2,1,0:T(8,128)} custom-call(f32[6,8,8,128]{3,2,1,0:T(8,128)S(1)} %get-tuple-element.37.gain, f32[6,6,8,8,128]{4,3,2,1,0:T(8,128)S(1)} %get-tuple-element.38.done, f32[96,8,128]{2,1,0:T(8,128)S(1)} %get-tuple-element.39.inner, f32[104,8,128]{2,1,0:T(8,128)S(1)} %get-tuple-element.35.mixed), custom_call_target="tpu_custom_call" | custom-call | flops 10000000 | bytes 6000000 | tf_op jit(solution)/shard_map/pallas_call | solution.py:856
  74.3 7.9 %all-to-all-done.1 = f32[16,1,128]{2,1,0:T(1,128)S(1)} async-done(((f32[16,1,128]{2,1,0:T(1,128)}), f32[16,1,128]{2,1,0:T(1,128)S(1)}, u32[]{:S(2)}, u32[]{:S(2)}) %all-to-all-start.1) | async-done | bytes 8224 | tf_op jit(solution)/shard_map/all_to_all | solution.py:848
  82.2 0.7 shard_map.85
  (10 shorter events, 0.0 us)
Async XLA Ops:
  0.6 9.5 %copy-start.1 = (f32[47,8,128]{2,1,0:T(8,128)S(1)}, f32[47,8,128]{2,1,0:T(8,128)}, u32[]{:S(2)}) copy-start(f32[47,8,128]{2,1,0:T(8,128)} %visc.5) | copy-start | bytes 577540
  0.6 9.5 %copy-start = (f32[8,48,8,128]{3,2,1,0:T(8,128)S(1)}, f32[8,48,8,128]{3,2,1,0:T(8,128)}, u32[]{:S(2)}) copy-start(f32[8,48,8,128]{3,2,1,0:T(8,128)} %param.6) | copy-start | bytes 4718596
  2.9 14.3 %copy-start.2 = (f32[768,128]{1,0:T(8,128)S(1)}, f32[768,128]{1,0:T(8,128)}, u32[]{:S(2)}) copy-start(f32[768,128]{1,0:T(8,128)} %get-tuple-element.23.state) | copy-start | bytes 1179652
  2.9 14.3 %copy-start.3 = (f32[3,8,128]{2,1,0:T(8,128)S(1)}, f32[3,8,128]{2,1,0:T(8,128)}, u32[]{:S(2)}) copy-start(f32[3,8,128]{2,1,0:T(8,128)} %get-tuple-element.22.flat.refs_0_) | copy-start | bytes 36868
  2.9 14.3 %collective-permute-start = (f32[57,8,128]{2,1,0:T(8,128)}, f32[57,8,128]{2,1,0:T(8,128)S(1)}, u32[]{:S(2)}, u32[]{:S(2)}) collective-permute-start(f32[57,8,128]{2,1,0:T(8,128)} %get-tuple-element.24), channel_id=1, source_target_pairs={{16,32},{17,33},{18,34},{19,35},{20,36},{21,37},{22,38},{23,39},{2... | collective-permute-start | bytes 700424 | tf_op jit(solution)/shard_map/ppermute | solution.py:806
  3.7 13.4 %collective-permute-start.1 = (f32[51,8,128]{2,1,0:T(8,128)}, f32[51,8,128]{2,1,0:T(8,128)S(1)}, u32[]{:S(2)}, u32[]{:S(2)}) collective-permute-start(f32[51,8,128]{2,1,0:T(8,128)} %get-tuple-element.25), channel_id=1, source_target_pairs={{0,16},{1,17},{2,18},{3,19},{4,20},{5,21},{6,22},{7,23},{8,24},{9,... | collective-permute-start | bytes 626696 | tf_op jit(solution)/shard_map/ppermute | solution.py:807
  10.8 26.1 %collective-permute-start.2 = (f32[60,8,128]{2,1,0:T(8,128)S(1)}, f32[60,8,128]{2,1,0:T(8,128)S(1)}, u32[]{:S(2)}, u32[]{:S(2)}) collective-permute-start(f32[60,8,128]{2,1,0:T(8,128)S(1)} %get-tuple-element.30), channel_id=1, source_target_pairs={{16,32},{17,33},{18,34},{19,35},{20,36},{21,37},{22,38},{23,39},{2... | collective-permute-start | bytes 737288 | tf_op jit(solution)/shard_map/ppermute | solution.py:816
  11.5 25.4 %collective-permute-start.3 = (f32[60,8,128]{2,1,0:T(8,128)S(1)}, f32[60,8,128]{2,1,0:T(8,128)S(1)}, u32[]{:S(2)}, u32[]{:S(2)}) collective-permute-start(f32[60,8,128]{2,1,0:T(8,128)S(1)} %get-tuple-element.31), channel_id=1, source_target_pairs={{0,16},{1,17},{2,18},{3,19},{4,20},{5,21},{6,22},{7,23},{8,24},{9,... | collective-permute-start | bytes 737288 | tf_op jit(solution)/shard_map/ppermute | solution.py:817
  17.2 53.7 %copy-start.4 = (f32[47,8,128]{2,1,0:T(8,128)S(1)}, f32[47,8,128]{2,1,0:T(8,128)}, u32[]{:S(2)}) copy-start(f32[47,8,128]{2,1,0:T(8,128)} %diff.1) | copy-start | bytes 577540
  17.6 20.7 %collective-permute-start.4 = (f32[13,8,128]{2,1,0:T(8,128)S(1)}, f32[13,8,128]{2,1,0:T(8,128)S(1)}, u32[]{:S(2)}, u32[]{:S(2)}) collective-permute-start(f32[13,8,128]{2,1,0:T(8,128)S(1)} %get-tuple-element.33.refs_3_), channel_id=1, source_target_pairs={{0,15},{1,2},{2,1},{3,4},{4,3},{5,6},{6,5},{7,8},{8,7},{9,10},{10,... | collective-permute-start | bytes 159752 | tf_op jit(solution)/shard_map/ppermute | solution.py:824
  33.8 4.5 %collective-permute-start.5 = (f32[13,8,128]{2,1,0:T(8,128)S(1)}, f32[13,8,128]{2,1,0:T(8,128)S(1)}, u32[]{:S(2)}, u32[]{:S(2)}) collective-permute-start(f32[13,8,128]{2,1,0:T(8,128)S(1)} %get-tuple-element.34.refs_4_), channel_id=1, source_target_pairs={{0,1},{1,0},{2,3},{3,2},{4,5},{5,4},{6,7},{7,6},{8,9},{9,8},{10,11... | collective-permute-start | bytes 159752 | tf_op jit(solution)/shard_map/ppermute | solution.py:825
  54.2 28.0 %all-to-all-start.1 = ((f32[16,1,128]{2,1,0:T(1,128)}), f32[16,1,128]{2,1,0:T(1,128)S(1)}, u32[]{:S(2)}, u32[]{:S(2)}) async-start(f32[16,1,128]{2,1,0:T(1,128)} %bitcast.6), calls=%async_computation.1 | async-start | bytes 16384 | tf_op jit(solution)/shard_map/all_to_all | solution.py:848

commit v7 on v6

--- a/solution.py
+++ b/solution.py
@@ -164,25 +164,14 @@
         copy.wait()
 
 
-def pack_tracers(state_any, visc, pay_b, pay_a, far, near, tracer, sems):
-    half = 144 * 8
-    copies = [
-        pltpu.make_async_copy(
-            state_any.at[pl.ds((96 + 144 * i) * 8, half)], tracer.at[pl.ds(i * half, half)], sems.at[i]
-        )
-        for i in range(2)
-    ]
-    for copy in copies:
-        copy.start()
-    for copy in copies:
-        copy.wait()
+def pack_tracers(state, visc, pay_b, pay_a, far, near):
     odd, top, odd_lon = whereabouts()
     lane = lane_iota()
     keep = (sub_iota() < 4).astype(jnp.int32) == odd
 
     def rows_of(t):
-        start = 8 * t * 8
-        return tracer[pl.ds(start, 8, stride=8), :], tracer[pl.ds(start + 7, 8, stride=8), :]
+        start = (96 + 8 * t) * 8
+        return state[pl.ds(start, 8, stride=8), :], state[pl.ds(start + 7, 8, stride=8), :]
 
     for t in range(ROW_TILES):
         row0, row7 = rows_of(t)
@@ -202,7 +191,7 @@
             pay_b[PAIR_VISC + m] = flip_rows(flip_lanes(jnp.where(keep, rolled, first)))
 
     def scalar(n):
-        return tracer[n * 8 : n * 8 + 8, :], 0
+        return state[(96 + n) * 8 : (96 + n) * 8 + 8, :], 0
 
     for tile in range(3):
         planes = [functools.partial(scalar, n) for n in range(128 * tile, min(128 * tile + 128, 288))]
@@ -658,7 +647,7 @@
             new = []
             for f in range(6):
                 first = f * 48 + CHUNK * chunk
-                q = state[pl.ds((first + i) * 8, 8), :]
+                q = state[pl.ds((96 + first + i) * 8, 8), :]
                 row_a = rec_a[f * 6 + chunk, i : i + 1, :]
                 row_b = rec_b[f * 6 + chunk, i : i + 1, :]
                 row_n = jnp.broadcast_to(jnp.where(odd == 1, row_b, row_a), (8, 128))
@@ -805,11 +794,10 @@
         own = (uv, viscosity, flat)
         rec_b = lax.ppermute(pay_b, both, pairs_b)
         rec_a = lax.ppermute(pay_a, both, pairs_a)
-        row_b, row_a, far_tracers, near_tracers, tracer = kernel(
+        row_b, row_a, far_tracers, near_tracers = kernel(
             pack_tracers,
-            [ANY, VMEM],
-            [(SECOND_TILES, 8, 128)] * 2 + [(3, 8, 128)] * 2 + [(288 * 8, 128)],
-            scratch=[pltpu.SemaphoreType.DMA((2,))],
+            [VMEM, VMEM],
+            [(SECOND_TILES, 8, 128)] * 2 + [(3, 8, 128)] * 2,
             flops=1_000_000,
             nbytes=2_000_000,
         )(state, viscosity)
@@ -852,7 +840,7 @@
             [(*chunked, 8, 128), (6, *chunked, 8, 128)],
             flops=10_000_000,
             nbytes=6_000_000,
-        )(tracer, diffusivity, flat, mixed, rec_row_b, rec_row_a, rec_far, rec_near, sent)
+        )(state, diffusivity, flat, mixed, rec_row_b, rec_row_a, rec_far, rec_near, sent)
         (state_out,) = kernel(
             tracers_up, [VMEM] * 4, [(8 * K, 8, 128)], flops=10_000_000, nbytes=6_000_000
         )(gain, done, inner, mixed)

time: 83.3 us -> 83 us (level)
  no operation moved by 1% of the time
where the time goes in v7:
time: 83 us; the launch traced here: 82.7 us
  starting transfers between devices  49.5 us (60%)
  blocking collectives  13.4 us (16%)
  Pallas kernels  11 us (13%)
  waiting for transfers between devices  7.92 us (10%)
  between operations  0.85 us (1%)
    all_to_all x1, starting transfers between devices, local(): lax.all_to_all(parts, both, 0, 0, axis_index_groups=second_groups, tiled=...  16.7 us
    ppermute x1, starting transfers between devices, local(): rec_far = lax.ppermute(pay_far, 'lon', pairs_far)  16.2 us
    all_to_all x1, blocking collectives, local(): lax.all_to_all(moments, both, 0, 0, axis_index_groups=first_groups, tiled...  13.4 us
    all_to_all x1, waiting for transfers between devices, local(): lax.all_to_all(parts, both, 0, 0, axis_index_groups=second_groups, tiled=...  7.9 us
    ppermute x1, starting transfers between devices, local(): rec_a = lax.ppermute(pay_a, both, pairs_a)  6.39 us
    ppermute x1, starting transfers between devices, local(): rec_row_a = lax.ppermute(row_a, both, pairs_a)  5.61 us
    ppermute x1, starting transfers between devices, local(): rec_near = lax.ppermute(pay_near, 'lon', pairs_near)  3.07 us
    pallas_call x1, Pallas kernels, local(): kernel(pack_lat, [ANY] * 5, [(LAT_TILES, 8, 128), (ROW_X, 8, 128), (96 *...  2.2 us
  transfers between devices with their start and end apart: 7, of which 1 were waited for; matrix products, arithmetic and copies ran while one was open for 0% of the time, Pallas kernels for 7%

profile of v7, /device:TPU:1, one launch (start us, length us, event | category | flops | bytes accessed | tf_op | source)
XLA Modules:
  0.0 82.7 jit_solution(203382956985023903)
XLA Ops:
  0.7 2.2 %shard_map.77 = (f32[57,8,128]{2,1,0:T(8,128)}, f32[51,8,128]{2,1,0:T(8,128)}, f32[768,128]{1,0:T(8,128)}, f32[3,8,128]{2,1,0:T(8,128)}) custom-call(f32[3072,128]{1,0:T(8,128)} %bitcast.10, f32[47,8,128]{2,1,0:T(8,128)} %visc.5, s32[8,128]{1,0:T(8,128)} %wet_any.1, f32[8,128]{1,0:T(8,128)} %storage_any.1, f32[8,128]{1,0:T(8,128)} %surf_any.1), custom_call_target="tpu_custom_call" | custom-call | tf_op jit(solution)/shard_map/pallas_call | solution.py:782
  2.9 0.0 copy-start.2
  2.9 0.8 collective-permute-start
  3.7 6.4 %collective-permute-start.1 = (f32[51,8,128]{2,1,0:T(8,128)}, f32[51,8,128]{2,1,0:T(8,128)S(1)}, u32[]{:S(2)}, u32[]{:S(2)}) collective-permute-start(f32[51,8,128]{2,1,0:T(8,128)} %get-tuple-element.23), channel_id=1, source_target_pairs={{0,16},{1,17},{2,18},{3,19},{4,20},{5,21},{6,22},{7,23},{8,24},{9,... | collective-permute-start | bytes 626696 | tf_op jit(solution)/shard_map/ppermute | solution.py:796
  10.1 0.4 shard_map.78
  10.6 0.7 collective-permute-start.2
  11.2 5.6 %collective-permute-start.3 = (f32[60,8,128]{2,1,0:T(8,128)S(1)}, f32[60,8,128]{2,1,0:T(8,128)S(1)}, u32[]{:S(2)}, u32[]{:S(2)}) collective-permute-start(f32[60,8,128]{2,1,0:T(8,128)S(1)} %get-tuple-element.29), channel_id=1, source_target_pairs={{0,16},{1,17},{2,18},{3,19},{4,20},{5,21},{6,22},{7,23},{8,24},{9,... | collective-permute-start | bytes 737288 | tf_op jit(solution)/shard_map/ppermute | solution.py:805
  16.9 0.0 collective-permute-done.rec_b
  16.9 0.0 copy-start.4
  16.9 0.4 shard_map.79
  17.3 16.2 %collective-permute-start.4 = (f32[13,8,128]{2,1,0:T(8,128)S(1)}, f32[13,8,128]{2,1,0:T(8,128)S(1)}, u32[]{:S(2)}, u32[]{:S(2)}) collective-permute-start(f32[13,8,128]{2,1,0:T(8,128)S(1)} %get-tuple-element.31.refs_3_), channel_id=1, source_target_pairs={{0,15},{1,2},{2,1},{3,4},{4,3},{5,6},{6,5},{7,8},{8,7},{9,10},{10,... | collective-permute-start | bytes 159752 | tf_op jit(solution)/shard_map/ppermute | solution.py:812
  33.5 3.1 %collective-permute-start.5 = (f32[13,8,128]{2,1,0:T(8,128)S(1)}, f32[13,8,128]{2,1,0:T(8,128)S(1)}, u32[]{:S(2)}, u32[]{:S(2)}) collective-permute-start(f32[13,8,128]{2,1,0:T(8,128)S(1)} %get-tuple-element.32.refs_4_), channel_id=1, source_target_pairs={{0,1},{1,0},{2,3},{3,2},{4,5},{5,4},{6,7},{7,6},{8,9},{9,8},{10,11... | collective-permute-start | bytes 159752 | tf_op jit(solution)/shard_map/ppermute | solution.py:813
  36.6 0.0 collective-permute-done.2.rec_b
  36.6 0.0 collective-permute-done.3.rec_a
  36.6 1.4 %shard_map.80 = (f32[96,8,128]{2,1,0:T(8,128)S(1)}, f32[4,8,128]{2,1,0:T(8,128)S(1)}) custom-call(f32[768,128]{1,0:T(8,128)S(1)} %copy-done.2, f32[47,8,128]{2,1,0:T(8,128)S(1)} %copy-done.1, f32[3,8,128]{2,1,0:T(8,128)S(1)} %copy-done.3, f32[99,8,128]{2,1,0:T(8,128)S(1)} %get-tuple-element.26.rows.refs_1_, f32[6,8,128]{2,1,0:T(8,128)S(1)} %get-tuple-element.27.row_x, ...), custom_call_target="tpu_custom_call" | custom-call | flops 10000000 | bytes 6000000 | tf_op jit(solution)/shard_map/pallas_call | solution.py:815
  38.1 0.0 collective-permute-done.5.refs_6_.near
  38.1 1.8 %shard_map.81 = (f32[104,8,128]{2,1,0:T(8,128)S(1)}, f32[32,128]{1,0:T(8,128)S(1)}) custom-call(f32[3,8,128]{2,1,0:T(8,128)S(1)} %copy-done.3, f32[99,8,128]{2,1,0:T(8,128)S(1)} %get-tuple-element.26.rows.refs_1_, f32[4,8,128]{2,1,0:T(8,128)S(1)} %get-tuple-element.30.refs_2_, f32[13,8,128]{2,1,0:T(8,128)S(1)} %get-tuple-element.31.refs_3_, ...), custom_call_target="tpu_custom_call" | custom-call | tf_op jit(solution)/shard_map/pallas_call | solution.py:823
  39.9 13.4 %all_to_all.22 = f32[32,1,128]{2,1,0:T(1,128)S(1)} all-to-all(f32[32,1,128]{2,1,0:T(1,128)S(1)} %bitcast.15), channel_id=1, replica_groups={{0,1,4,5,8,9,12,13,16,17,20,21,24,25,28,29,32,33,36,37,40,41,44,45,48,4..., dimensions={0} | all-to-all | bytes 32768 | tf_op jit(solution)/shard_map/all_to_all | solution.py:833
  53.3 0.6 shard_map.82.after
  53.9 16.7 %all-to-all-start.1 = ((f32[16,1,128]{2,1,0:T(1,128)}), f32[16,1,128]{2,1,0:T(1,128)S(1)}, u32[]{:S(2)}, u32[]{:S(2)}) async-start(f32[16,1,128]{2,1,0:T(1,128)} %bitcast.6), calls=%async_computation.1 | async-start | bytes 16384 | tf_op jit(solution)/shard_map/all_to_all | solution.py:836
  70.6 1.8 %shard_map.83 = (f32[6,8,8,128]{3,2,1,0:T(8,128)S(1)}, f32[6,6,8,8,128]{4,3,2,1,0:T(8,128)S(1)}) custom-call(f32[3072,128]{1,0:T(8,128)S(1)} %bitcast.12, f32[47,8,128]{2,1,0:T(8,128)S(1)} %copy-done.4, f32[3,8,128]{2,1,0:T(8,128)S(1)} %copy-done.3, f32[104,8,128]{2,1,0:T(8,128)S(1)} %get-tuple-element.33.mixed, ...), custom_call_target="tpu_custom_call" | custom-call | flops 10000000 | bytes 6000000 | tf_op jit(solution)/shard_map/pallas_call | solution.py:837
  72.5 1.5 %shard_map.84 = f32[384,8,128]{2,1,0:T(8,128)} custom-call(f32[6,8,8,128]{3,2,1,0:T(8,128)S(1)} %get-tuple-element.35.gain, f32[6,6,8,8,128]{4,3,2,1,0:T(8,128)S(1)} %get-tuple-element.36.done, f32[96,8,128]{2,1,0:T(8,128)S(1)} %get-tuple-element.37.inner, f32[104,8,128]{2,1,0:T(8,128)S(1)} %get-tuple-element.33.mixed), custom_call_target="tpu_custom_call" | custom-call | flops 10000000 | bytes 6000000 | tf_op jit(solution)/shard_map/pallas_call | solution.py:844
  74.0 7.9 %all-to-all-done.1 = f32[16,1,128]{2,1,0:T(1,128)S(1)} async-done(((f32[16,1,128]{2,1,0:T(1,128)}), f32[16,1,128]{2,1,0:T(1,128)S(1)}, u32[]{:S(2)}, u32[]{:S(2)}) %all-to-all-start.1) | async-done | bytes 8224 | tf_op jit(solution)/shard_map/all_to_all | solution.py:836
  81.9 0.7 shard_map.85
  (10 shorter events, 0.0 us)
Async XLA Ops:
  0.6 9.5 %copy-start.1 = (f32[47,8,128]{2,1,0:T(8,128)S(1)}, f32[47,8,128]{2,1,0:T(8,128)}, u32[]{:S(2)}) copy-start(f32[47,8,128]{2,1,0:T(8,128)} %visc.5) | copy-start | bytes 577540
  0.6 9.5 %copy-start = (f32[8,48,8,128]{3,2,1,0:T(8,128)S(1)}, f32[8,48,8,128]{3,2,1,0:T(8,128)}, u32[]{:S(2)}) copy-start(f32[8,48,8,128]{3,2,1,0:T(8,128)} %param.6) | copy-start | bytes 4718596
  2.9 14.0 %copy-start.2 = (f32[768,128]{1,0:T(8,128)S(1)}, f32[768,128]{1,0:T(8,128)}, u32[]{:S(2)}) copy-start(f32[768,128]{1,0:T(8,128)} %get-tuple-element.21.state) | copy-start | bytes 1179652
  2.9 14.0 %copy-start.3 = (f32[3,8,128]{2,1,0:T(8,128)S(1)}, f32[3,8,128]{2,1,0:T(8,128)}, u32[]{:S(2)}) copy-start(f32[3,8,128]{2,1,0:T(8,128)} %get-tuple-element.20.flat.refs_0_) | copy-start | bytes 36868
  2.9 14.0 %collective-permute-start = (f32[57,8,128]{2,1,0:T(8,128)}, f32[57,8,128]{2,1,0:T(8,128)S(1)}, u32[]{:S(2)}, u32[]{:S(2)}) collective-permute-start(f32[57,8,128]{2,1,0:T(8,128)} %get-tuple-element.22), channel_id=1, source_target_pairs={{16,32},{17,33},{18,34},{19,35},{20,36},{21,37},{22,38},{23,39},{2... | collective-permute-start | bytes 700424 | tf_op jit(solution)/shard_map/ppermute | solution.py:795
  3.7 13.2 %collective-permute-start.1 = (f32[51,8,128]{2,1,0:T(8,128)}, f32[51,8,128]{2,1,0:T(8,128)S(1)}, u32[]{:S(2)}, u32[]{:S(2)}) collective-permute-start(f32[51,8,128]{2,1,0:T(8,128)} %get-tuple-element.23), channel_id=1, source_target_pairs={{0,16},{1,17},{2,18},{3,19},{4,20},{5,21},{6,22},{7,23},{8,24},{9,... | collective-permute-start | bytes 626696 | tf_op jit(solution)/shard_map/ppermute | solution.py:796
  10.6 26.1 %collective-permute-start.2 = (f32[60,8,128]{2,1,0:T(8,128)S(1)}, f32[60,8,128]{2,1,0:T(8,128)S(1)}, u32[]{:S(2)}, u32[]{:S(2)}) collective-permute-start(f32[60,8,128]{2,1,0:T(8,128)S(1)} %get-tuple-element.28), channel_id=1, source_target_pairs={{16,32},{17,33},{18,34},{19,35},{20,36},{21,37},{22,38},{23,39},{2... | collective-permute-start | bytes 737288 | tf_op jit(solution)/shard_map/ppermute | solution.py:804
  11.2 25.4 %collective-permute-start.3 = (f32[60,8,128]{2,1,0:T(8,128)S(1)}, f32[60,8,128]{2,1,0:T(8,128)S(1)}, u32[]{:S(2)}, u32[]{:S(2)}) collective-permute-start(f32[60,8,128]{2,1,0:T(8,128)S(1)} %get-tuple-element.29), channel_id=1, source_target_pairs={{0,16},{1,17},{2,18},{3,19},{4,20},{5,21},{6,22},{7,23},{8,24},{9,... | collective-permute-start | bytes 737288 | tf_op jit(solution)/shard_map/ppermute | solution.py:805
  16.9 53.7 %copy-start.4 = (f32[47,8,128]{2,1,0:T(8,128)S(1)}, f32[47,8,128]{2,1,0:T(8,128)}, u32[]{:S(2)}) copy-start(f32[47,8,128]{2,1,0:T(8,128)} %diff.1) | copy-start | bytes 577540
  17.3 20.8 %collective-permute-start.4 = (f32[13,8,128]{2,1,0:T(8,128)S(1)}, f32[13,8,128]{2,1,0:T(8,128)S(1)}, u32[]{:S(2)}, u32[]{:S(2)}) collective-permute-start(f32[13,8,128]{2,1,0:T(8,128)S(1)} %get-tuple-element.31.refs_3_), channel_id=1, source_target_pairs={{0,15},{1,2},{2,1},{3,4},{4,3},{5,6},{6,5},{7,8},{8,7},{9,10},{10,... | collective-permute-start | bytes 159752 | tf_op jit(solution)/shard_map/ppermute | solution.py:812
  33.5 4.5 %collective-permute-start.5 = (f32[13,8,128]{2,1,0:T(8,128)S(1)}, f32[13,8,128]{2,1,0:T(8,128)S(1)}, u32[]{:S(2)}, u32[]{:S(2)}) collective-permute-start(f32[13,8,128]{2,1,0:T(8,128)S(1)} %get-tuple-element.32.refs_4_), channel_id=1, source_target_pairs={{0,1},{1,0},{2,3},{3,2},{4,5},{5,4},{6,7},{7,6},{8,9},{9,8},{10,11... | collective-permute-start | bytes 159752 | tf_op jit(solution)/shard_map/ppermute | solution.py:813
  53.9 28.0 %all-to-all-start.1 = ((f32[16,1,128]{2,1,0:T(1,128)}), f32[16,1,128]{2,1,0:T(1,128)S(1)}, u32[]{:S(2)}, u32[]{:S(2)}) async-start(f32[16,1,128]{2,1,0:T(1,128)} %bitcast.6), calls=%async_computation.1 | async-start | bytes 16384 | tf_op jit(solution)/shard_map/all_to_all | solution.py:836
